TPU v7x, 32 devices: a whole 2x2x4 slice. The times are simulated.
32 devices in a mesh: pert: 2 (over y), space: 16 (over z, x, core).
Axes of the slice: x: 2, y: 2, z: 4, core: 2. Of those that a mesh axis runs over, the one named last changes fastest.
Arguments:
- spectra: float32 [320, 320, 256], P('space', None, 'pert'), may hold values from -6 to 6
- wave_order: int32 [320], replicated, may hold values from 0 to 319, as said below
- traj_wind: bfloat16 [2, 32, 480, 960], P(None, 'pert', 'space'), may hold values from -0.029907227 to 0.029907227
- traj_state: bfloat16 [2, 2, 32, 480, 960], P(None, None, 'pert', 'space'), may hold values from -6 to 6
- vertical_modes: float32 [32, 32], replicated, may hold values from -0.75 to 0.75
- mode_speeds: float32 [32], replicated, may hold values from 1e-06 to 0.001
Outputs:
- spectra_out: float32 [320, 320, 256], P('space', None, 'pert')
Inputs may be any that keep to these rules, and one draw needn't show every extreme that they name: wave_order is a permutation of 0 to 319 in which slots 2 i and 2 i + 1 hold two wavenumbers that add up to 319.
All inputs are finite; a program needn't handle non-finite values.
Results may differ from a plain program's by a relative error of at most 0.0085.
Values may be sent and summed in bfloat16 or wider, within the bound.
No kernel may reach another device: no remote copies, remote signals or barrier semaphores. Data moves between devices by JAX's collectives and lax.ppermute only.
A program may use at most 128 MiB of HBM per device.

v0:
```python
import math

import jax
import jax.numpy as jnp
import numpy as np
from jax import lax
from jax.experimental import pallas as pl
from jax.experimental.pallas import tpu as pltpu
from jax.sharding import PartitionSpec as P

NLAT = 480
NLON = 960
M = 320
VARS = 2
LEV = 32
STEPS = 2
ROWS = 336
ROWS_T = 384
DEPTH = 384
VMEM_BYTES = 48 * 1024 * 1024
BIG = 2.0**32
HIGHEST = lax.Precision.HIGHEST


def params():
    return pltpu.CompilerParams(vmem_limit_bytes=VMEM_BYTES)


def vmem(count):
    return [pl.BlockSpec(memory_space=pltpu.VMEM)] * count


def smem(count):
    return [pl.BlockSpec(memory_space=pltpu.SMEM)] * count


class Sizes:
    def __init__(self, space):
        self.space = space
        self.slots = M // space
        self.pairs = self.slots // 2
        self.lats = NLAT // space
        self.lat_pad = -(-self.lats // 8) * 8
        self.half = space // 2
        self.north = self.half * self.lat_pad
        self.pair_pad = -(-self.pairs // 8) * 8
        self.block = self.slots * self.lats
        self.block_pad = self.block + 8
        self.group = 6 if self.lats % 6 == 0 else -(-self.lats // 2) * 2
        self.groups = -(-self.lats // self.group)


def table_kernel(sz, wave_a, wave_b, start_a, start_b, cosines, table, table_t, rows_ref):
    shape = (sz.pair_pad, sz.north)
    wide = shape[1] // 128
    wa, wb = wave_a[...], wave_b[...]
    length = M - wa
    x = cosines[...]
    la, lb = start_a[...], start_b[...]

    def spread(v):
        return jnp.concatenate([v] * wide, axis=1)

    def body(block, carry):
        cur, prev, inv_prev, shift = carry
        big = jnp.maximum(jnp.abs(cur), jnp.abs(prev)) > BIG
        scale = jnp.where(big, 1.0 / BIG, 1.0)
        cur, prev = cur * scale, prev * scale
        shift = shift + jnp.where(big, 32.0, 0.0)
        second = spread(((block * 8).astype(jnp.float32) > length).astype(jnp.float32)) > 0.5
        base = jnp.exp2(0.5 * (jnp.where(second, lb, la) + shift))
        base_b = jnp.exp2(0.5 * lb)
        for j in range(8):
            r = (block * 8 + j).astype(jnp.float32)
            in_b = r >= length
            fresh = r == length
            m = jnp.where(in_b, wb, wa)
            k = jnp.where(in_b, r - length, r)
            n = m + k
            den = k * (2.0 * m + k)
            num = 4.0 * n * n - 1.0
            first = k < 0.5
            safe_den = jnp.where(first, 1.0, den)
            upper = jnp.where(first, 0.0, jnp.sqrt(num / safe_den))
            inv = jnp.where(first, 0.0, jnp.sqrt(safe_den / jnp.where(first, 1.0, num)))
            up_w = spread(upper)
            lo_w = spread(upper * inv_prev)
            new = up_w * x * cur - lo_w * prev
            fresh_w = spread(fresh.astype(jnp.float32)) > 0.5
            start = jnp.logical_or(fresh_w, r == 0.0)
            new = jnp.where(start, 1.0, new)
            prev = jnp.where(start, 0.0, cur)
            shift = jnp.where(fresh_w, 0.0, shift)
            base = jnp.where(fresh_w, base_b, base)
            cur = new
            inv_prev = inv
            value = (cur * base) * base
            for c in range(wide):
                rows_ref[c, pl.ds(block * 8 + j, sz.pair_pad, stride=ROWS), :] = value[
                    :, c * 128 : (c + 1) * 128
                ]
        return cur, prev, inv_prev, shift

    zero = jnp.zeros(shape, jnp.float32)
    lax.fori_loop(0, ROWS // 8, body, (zero, zero, jnp.zeros_like(wa), zero))
    ridx = lax.broadcasted_iota(jnp.int32, (ROWS, sz.north), 0)

    def emit(i, _):
        at = pl.multiple_of(i * ROWS, ROWS)
        full = jnp.concatenate([rows_ref[c, pl.ds(at, ROWS), :] for c in range(wide)], axis=1)
        full = jnp.where(ridx <= M, full, 0.0)
        table[i] = full.astype(jnp.bfloat16)
        padded = jnp.concatenate(
            [full, jnp.zeros((ROWS_T - ROWS, sz.north), jnp.float32)], axis=0
        )
        table_t[i] = jnp.transpose(padded).astype(jnp.bfloat16)
        return 0

    lax.fori_loop(0, sz.pairs, emit, 0)


def make_tables(sz, wave_a, wave_b, log_a, log_b, cosines):
    return pl.pallas_call(
        lambda *refs: table_kernel(sz, *refs),
        out_shape=(
            jax.ShapeDtypeStruct((sz.pairs, ROWS, sz.north), jnp.bfloat16),
            jax.ShapeDtypeStruct((sz.pairs, sz.north, ROWS_T), jnp.bfloat16),
        ),
        in_specs=vmem(5),
        out_specs=tuple(vmem(2)),
        scratch_shapes=[pltpu.VMEM((sz.north // 128, sz.pair_pad * ROWS, 128), jnp.float32)],
        compiler_params=params(),
        name="legendre_tables",
    )(wave_a, wave_b, log_a, log_b, cosines)


def row_facts(waves, i, columns):
    wave_a, wave_b = waves[2 * i], waves[2 * i + 1]
    length = M - wave_a
    r = lax.broadcasted_iota(jnp.int32, (ROWS, columns), 0)
    in_a = r < length
    k = jnp.where(in_a, r, r - length)
    even = jnp.bitwise_and(k, 1) == 0
    return wave_a, wave_b, length, r, in_a, k, even


def send_rows(sz, i, state, facts, table_t, stage):
    _, _, _, _, in_a, _, even = facts
    zero = jnp.zeros_like(state)
    in_b = jnp.logical_not(in_a)
    odd = jnp.logical_not(even)
    parts = [
        jnp.where(jnp.logical_and(side, sign), state, zero).astype(jnp.bfloat16)
        for side in (in_a, in_b)
        for sign in (even, odd)
    ]
    columns = state.shape[1]
    rhs = jnp.concatenate(parts, axis=1)
    rhs = jnp.concatenate([rhs, jnp.zeros((ROWS_T - ROWS, 4 * columns), jnp.bfloat16)], axis=0)
    out = jnp.dot(table_t[i], rhs, preferred_element_type=jnp.float32)
    for s in range(2):
        e = out[:, (2 * s) * columns : (2 * s + 1) * columns]
        o = out[:, (2 * s + 1) * columns : (2 * s + 2) * columns]
        north, south = e + o, e - o
        at = (2 * i + s) * sz.lats
        for b in range(sz.half):
            lo = b * sz.lat_pad
            stage[b, pl.ds(at, sz.lat_pad), :] = north[lo : lo + sz.lat_pad]
            stage[sz.space - 1 - b, pl.ds(at, sz.lat_pad), :] = south[lo : lo + sz.lat_pad]


def flush(sz, stage, send):
    def body(d, _):
        send[d] = stage[d, : sz.block, :].astype(jnp.bfloat16)
        return 0

    lax.fori_loop(0, sz.space, body, 0)


def load_rows(sz, recv, stage):
    def body(d, _):
        stage[d, : sz.block, :] = recv[d].astype(jnp.float32)
        stage[d, pl.ds(sz.block, 8), :] = jnp.zeros((8, stage.shape[2]), jnp.float32)
        return 0

    lax.fori_loop(0, sz.space, body, 0)


def change_rows(sz, i, facts, table, weights, stage):
    _, _, _, _, in_a, _, even = facts
    parts = []
    w = weights[...]
    for s in range(2):
        at = (2 * i + s) * sz.lats
        north = jnp.concatenate(
            [stage[b, pl.ds(at, sz.lat_pad), :] for b in range(sz.half)], axis=0
        )
        south = jnp.concatenate(
            [stage[sz.space - 1 - b, pl.ds(at, sz.lat_pad), :] for b in range(sz.half)], axis=0
        )
        parts.append(((north + south) * w).astype(jnp.bfloat16))
        parts.append(((north - south) * w).astype(jnp.bfloat16))
    rhs = jnp.concatenate(parts, axis=1)
    out = jnp.dot(table[i], rhs, preferred_element_type=jnp.float32)
    c = out.shape[1] // 4
    side_a = jnp.where(even, out[:, :c], out[:, c : 2 * c])
    side_b = jnp.where(even, out[:, 2 * c : 3 * c], out[:, 3 * c :])
    return jnp.where(in_a, side_a, side_b)


def kept(state, facts):
    wave_a, wave_b, _, r, in_a, _, _ = facts
    columns = state.shape[1]
    imaginary = lax.broadcasted_iota(jnp.int32, state.shape, 1) >= columns // 2
    wave = jnp.where(in_a, wave_a, wave_b)
    dropped = jnp.logical_or(jnp.logical_and(wave == 0, imaginary), r > M)
    return jnp.where(dropped, 0.0, state)


def updated(state, change, facts, mixing, mixing_t, speeds):
    wave_a, wave_b, _, _, in_a, k, _ = facts
    combined = state + change
    projected = jnp.dot(combined, mixing[...], precision=HIGHEST)
    n = (jnp.where(in_a, wave_a, wave_b) + k).astype(jnp.float32)
    stiffness = speeds[...] * (n * (n + 1.0))
    weighted = projected * (stiffness / (1.0 + stiffness))
    returned = jnp.dot(weighted, mixing_t[...], precision=HIGHEST)
    return kept(combined - returned, facts)


def first_kernel(sz, waves, spectra, turn, table_t, state_ref, send, stage):
    columns = spectra.shape[2]

    def body(i, _):
        facts = row_facts(waves, i, columns)
        length, r, in_a = facts[2], facts[3], facts[4]
        blank = jnp.zeros((ROWS - M, columns), jnp.float32)
        rows_a = jnp.concatenate([spectra[2 * i], blank], axis=0)
        rows_b = jnp.concatenate([spectra[2 * i + 1], blank], axis=0)
        packed = jnp.where(in_a, rows_a, pltpu.roll(rows_b, length, 0))
        state = jnp.dot(packed, turn[...], precision=HIGHEST)
        state = kept(state, facts)
        state_ref[i] = state
        send_rows(sz, i, state, facts, table_t, stage)
        return 0

    lax.fori_loop(0, sz.pairs, body, 0)
    flush(sz, stage, send)


def middle_kernel(
    sz, waves, state_in, recv, table, table_t, weights, mixing, mixing_t, speeds,
    state_out, send, stage_in, stage,
):
    columns = state_in.shape[2]
    load_rows(sz, recv, stage_in)

    def body(i, _):
        facts = row_facts(waves, i, columns)
        change = change_rows(sz, i, facts, table, weights, stage_in)
        state = updated(state_in[i], change, facts, mixing, mixing_t, speeds)
        state_out[i] = state
        send_rows(sz, i, state, facts, table_t, stage)
        return 0

    lax.fori_loop(0, sz.pairs, body, 0)
    flush(sz, stage, send)


def last_kernel(
    sz, waves, state_in, recv, table, weights, mixing, mixing_t, speeds, turn_t, out, stage_in
):
    columns = state_in.shape[2]
    load_rows(sz, recv, stage_in)

    def body(i, _):
        facts = row_facts(waves, i, columns)
        wave_a, wave_b, length, r = facts[:4]
        change = change_rows(sz, i, facts, table, weights, stage_in)
        state = updated(state_in[i], change, facts, mixing, mixing_t, speeds)
        state = jnp.dot(state, turn_t[...], precision=HIGHEST)
        out[2 * i] = jnp.where(r < length, state, 0.0)[:M]
        rolled = pltpu.roll(state, ROWS - length, 0)
        out[2 * i + 1] = jnp.where(r < M - wave_b, rolled, 0.0)[:M]
        return 0

    lax.fori_loop(0, sz.pairs, body, 0)


def grid_kernel(sz, flip, recv, traj, synth, slope, scale, send, stage_in, stage, lhs, values, slopes, force):
    lanes = recv.shape[2]
    rows = lanes // 2
    flat = M * sz.lats

    def load(d, _):
        at = pl.multiple_of(d * sz.block, 8)
        stage_in[pl.ds(at, sz.block), :] = recv[d].astype(jnp.float32)
        return 0

    lax.fori_loop(0, sz.space, load, 0)
    blank = jnp.zeros((DEPTH - M, lanes), jnp.float32)

    def body(g, _):
        for q in range(sz.group):
            t = g * sz.group + q
            if sz.groups == 1 and q >= sz.lats:
                lhs[q * rows : (q + 1) * rows, :] = jnp.zeros((rows, 2 * DEPTH), jnp.bfloat16)
                continue
            block = stage_in[pl.ds(t, M, stride=sz.lats), :]
            turned = jnp.transpose(jnp.concatenate([block, blank], axis=0)).astype(jnp.bfloat16)
            lhs[q * rows : (q + 1) * rows, :DEPTH] = turned[:rows]
            lhs[q * rows : (q + 1) * rows, DEPTH:] = turned[rows:]
        left = lhs[...]
        values[...] = jnp.dot(left, synth[...], preferred_element_type=jnp.float32)
        slopes[...] = jnp.dot(left, slope[...], preferred_element_type=jnp.float32)
        for q in range(sz.group):
            if sz.groups == 1 and q >= sz.lats:
                force[q * rows : (q + 1) * rows, :] = jnp.zeros((rows, NLON), jnp.bfloat16)
                continue
            t = g * sz.group + q
            here = jnp.where(flip[0] == 1, sz.lats - 1 - t, t)
            wind = traj[here, 0].astype(jnp.float32)
            for v in range(VARS):
                lo = q * rows + v * LEV
                other = traj[here, 1 + (v + 1) % VARS].astype(jnp.float32)
                force[lo : lo + LEV, :] = (
                    wind * slopes[lo : lo + LEV, :] + other * values[lo : lo + LEV, :]
                ).astype(jnp.bfloat16)
        forcing = force[...]
        spectrum = [
            lax.dot_general(
                synth[c * DEPTH : c * DEPTH + M, :],
                forcing,
                (((1,), (1,)), ((), ())),
                preferred_element_type=jnp.float32,
            )
            * scale[...][:, : 1]
            for c in range(2)
        ]
        lane = lax.broadcasted_iota(jnp.int32, (M, lanes), 1)
        left_side = lane < rows
        for q in range(0, sz.group, 2):
            re = spectrum[0][:, q * rows : (q + 2) * rows]
            im = spectrum[1][:, q * rows : (q + 2) * rows]
            t = g * sz.group + q
            stage[pl.ds(t, M, stride=sz.lats), :] = jnp.where(left_side, re, pltpu.roll(im, rows, 1))
            if sz.groups == 1 and q + 1 >= sz.lats:
                continue
            stage[pl.ds(t + 1, M, stride=sz.lats), :] = jnp.where(
                left_side, pltpu.roll(re, rows, 1), im
            )
        return 0

    lax.fori_loop(0, sz.groups, body, 0)

    def out(d, _):
        at = pl.multiple_of(d * sz.block, 8)
        send[d] = stage[pl.ds(at, sz.block), :].astype(jnp.bfloat16)
        return 0

    lax.fori_loop(0, sz.space, out, 0)


def grid_stage(sz, flip, recv, traj, synth, slope, scale):
    lanes = recv.shape[2]
    wide = sz.group * lanes // 2
    return pl.pallas_call(
        lambda *refs: grid_kernel(sz, *refs),
        out_shape=jax.ShapeDtypeStruct(recv.shape, jnp.bfloat16),
        in_specs=smem(1) + vmem(5),
        out_specs=vmem(1)[0],
        scratch_shapes=[
            pltpu.VMEM((M * sz.lats, lanes), jnp.float32),
            pltpu.VMEM((M * sz.lats, lanes), jnp.float32),
            pltpu.VMEM((wide, 2 * DEPTH), jnp.bfloat16),
            pltpu.VMEM((wide, NLON), jnp.float32),
            pltpu.VMEM((wide, NLON), jnp.float32),
            pltpu.VMEM((wide, NLON), jnp.bfloat16),
        ],
        compiler_params=params(),
        name="grid_stage",
    )(flip, recv, traj, synth, slope, scale)


def zonal_tables(wave_list):
    cell_index = jnp.arange(NLON, dtype=jnp.int32)
    wave_pad = jnp.concatenate([wave_list, jnp.zeros((DEPTH - M,), jnp.int32)])
    phase_index = wave_pad[:, None] * cell_index[None, :] % NLON
    angles = phase_index.astype(jnp.float32) * (2.0 * math.pi / NLON)
    factor = jnp.where(wave_pad == 0, 1.0, 2.0).astype(jnp.float32)
    inside = (jnp.arange(DEPTH) < M).astype(jnp.float32)
    gain = (factor * inside)[:, None]
    cosine, sine = gain * jnp.cos(angles), gain * jnp.sin(angles)
    wave = wave_pad.astype(jnp.float32)[:, None]
    synth = jnp.concatenate([-cosine, sine], axis=0).astype(jnp.bfloat16)
    slope = jnp.concatenate([wave * sine, wave * cosine], axis=0).astype(jnp.bfloat16)
    scale = jnp.broadcast_to((-1.0 / (NLON * factor[:M]))[:, None], (M, 128))
    return synth, slope, scale


def column_turn(columns):
    turn = np.zeros((columns, columns), np.float32)
    for c in range(columns):
        part, row = c % 2, c // 2
        turn[c, part * (columns // 2) + row] = 1.0
    return turn


def sectoral(wave, log_sine):
    gammas = jax.scipy.special.gammaln
    start = 0.5 * (
        gammas(wave + 1.5) - gammas(wave + 1.0) - gammas(jnp.float32(1.5))
    ) - 0.5 * math.log(2.0)
    return (start[:, None] + wave[:, None] * log_sine[None, :]) * (1.0 / math.log(2.0))


def shards(sz, spectra, wave_order, traj_wind, traj_state, vertical_modes, mode_speeds):
    columns = spectra.shape[2]
    rank = lax.axis_index("space")
    waves = lax.dynamic_slice_in_dim(wave_order, rank * sz.slots, sz.slots)

    place = np.arange(sz.north)
    block, inner = place // sz.lat_pad, place % sz.lat_pad
    real = inner < sz.lats
    colat = np.where(real, (block * sz.lats + inner + 0.5) * (math.pi / NLAT), math.pi / 2)
    cosines = jnp.asarray(np.cos(colat), jnp.float32)[None, :]
    log_sine = jnp.asarray(np.log(np.sin(colat)), jnp.float32)
    weights = jnp.asarray(
        np.broadcast_to((np.sin(colat) * (math.pi / NLAT) * real)[:, None], (sz.north, columns)),
        jnp.float32,
    )

    pair_waves = jnp.zeros((sz.pair_pad, 2), jnp.int32).at[: sz.pairs].set(waves.reshape(-1, 2))
    pair_waves = pair_waves.astype(jnp.float32)
    wide_a = jnp.broadcast_to(pair_waves[:, :1], (sz.pair_pad, 128))
    wide_b = jnp.broadcast_to(pair_waves[:, 1:], (sz.pair_pad, 128))
    table, table_t = make_tables(
        sz, wide_a, wide_b, sectoral(pair_waves[:, 0], log_sine), sectoral(pair_waves[:, 1], log_sine), cosines
    )

    turn = column_turn(columns)
    same = np.kron(np.eye(columns // LEV, dtype=np.float32), np.ones((LEV, LEV), np.float32))
    mixing = jnp.tile(vertical_modes.T, (columns // LEV, columns // LEV)) * same
    mixing_t = jnp.tile(vertical_modes, (columns // LEV, columns // LEV)) * same
    speeds = jnp.tile(mode_speeds, columns // LEV)[None, :]
    turn, turn_t = jnp.asarray(turn), jnp.asarray(turn.T)

    synth, slope, scale = zonal_tables(wave_order)
    flip = jnp.where(rank >= sz.half, 1, 0).astype(jnp.int32).reshape(1)

    stage_shape = pltpu.VMEM((sz.space, sz.block_pad, columns), jnp.float32)
    state_shape = jax.ShapeDtypeStruct((sz.pairs, ROWS, columns), jnp.float32)
    send_shape = jax.ShapeDtypeStruct((sz.space, sz.block, columns), jnp.bfloat16)

    state, send = pl.pallas_call(
        lambda *refs: first_kernel(sz, *refs),
        out_shape=(state_shape, send_shape),
        in_specs=smem(1) + vmem(3),
        out_specs=tuple(vmem(2)),
        scratch_shapes=[stage_shape],
        compiler_params=params(),
        name="first_inverse",
    )(waves, spectra, turn, table_t)

    for step in range(STEPS):
        local = jnp.concatenate([traj_wind[step][None], traj_state[step]], axis=0)
        traj = lax.all_gather(local, "pert", axis=1, tiled=True)
        traj = jnp.transpose(traj, (2, 0, 1, 3))
        recv = lax.all_to_all(send, "space", 0, 0, tiled=True)
        send = grid_stage(sz, flip, recv, traj, synth, slope, scale)
        recv = lax.all_to_all(send, "space", 0, 0, tiled=True)
        if step < STEPS - 1:
            state, send = pl.pallas_call(
                lambda *refs: middle_kernel(sz, *refs),
                out_shape=(state_shape, send_shape),
                in_specs=smem(1) + vmem(8),
                out_specs=tuple(vmem(2)),
                scratch_shapes=[stage_shape, stage_shape],
                compiler_params=params(),
                name="forward_inverse",
            )(waves, state, recv, table, table_t, weights, mixing, mixing_t, speeds)
        else:
            out = pl.pallas_call(
                lambda *refs: last_kernel(sz, *refs),
                out_shape=jax.ShapeDtypeStruct(spectra.shape, jnp.float32),
                in_specs=smem(1) + vmem(8),
                out_specs=vmem(1)[0],
                scratch_shapes=[stage_shape],
                compiler_params=params(),
                name="forward_last",
            )(waves, state, recv, table, weights, mixing, mixing_t, speeds, turn_t)
    return out


def solution(mesh):
    sz = Sizes(mesh.shape["space"])
    placed = (
        P("space", None, "pert"),
        P(),
        P(None, "pert", "space", None),
        P(None, None, "pert", "space", None),
        P(),
        P(),
    )
    return jax.shard_map(
        lambda *args: shards(sz, *args),
        mesh=mesh,
        in_specs=placed,
        out_specs=P("space", None, "pert"),
        check_vma=False,
    )
```

profile of v0, /device:TPU:15, one launch (start us, length us, event | category | flops | bytes accessed | tf_op | source)
XLA Modules:
  0.0 365.1 jit_solution(2324573803910958567)
XLA Ops:
  6.5 4.0 %fusion.19 = (bf16[1,2,16,30,960]{4,2,3,1,0:T(8,128)(2,1)}, bf16[1,2,16,30,960]{4,2,3,1,0:T(8,128)(2,1)S(1)}) fusion(bf16[2,2,16,30,960]{4,2,3,1,0:T(8,128)(2,1)} %param.17), kind=kLoop, calls=%fused_computation.103 | loop fusion | bytes 7372800 | tf_op jit(solution)/shard_map/slice | solution.py:466
  10.8 1.3 copy-done.15
  13.2 1.9 pad_maximum_fusion
  16.4 8.8 %legendre_tables.1 = (bf16[10,336,256]{2,1,0:T(8,128)(2,1)S(1)}, bf16[10,256,384]{2,1,0:T(8,128)(2,1)S(1)}) custom-call(f32[16,128]{1,0:T(8,128)S(1)} %broadcast_in_dim.21.refs_0_, f32[16,128]{1,0:T(8,128)S(1)} %broadcast_in_dim.23.refs_1_, f32[16,256]{1,0:T(8,128)S(1)} %get-tuple-element.44.refs_2_, f32[16,256]{1,0:T(8,128)S(1)} %get-tuple-element.43.refs_3_, ...), custom_call_target="tpu_custom_call" | custom-call | tf_op jit(solution)/shard_map/legendre_tables/pallas_call | solution.py:123
  26.4 13.5 %first_inverse.1 = (f32[10,336,128]{2,1,0:T(8,128)S(1)}, bf16[16,600,128]{2,1,0:T(8,128)(2,1)}) custom-call(s32[20]{0:T(128)S(1)} %dynamic_slice.3.refs_0_, f32[20,320,128]{2,1,0:T(8,128)} %refs_1_.1, f32[128,128]{1,0:T(8,128)S(1)} %copy-done.12, bf16[10,256,384]{2,1,0:T(8,128)(2,1)S(1)} %get-tuple-element.23.refs_3_.refs_4_), custom_call_target="tpu_custom_call" | custom-call | tf_op jit(solution)/shard_map/first_inverse/pallas_call | solution.py:455
  41.2 6.5 %all-to-all-start = ((bf16[16,600,128]{2,1,0:T(8,128)(2,1)}), bf16[16,600,128]{2,1,0:T(8,128)(2,1)}, u32[]{:S(2)}, u32[]{:S(2)}) async-start(bf16[16,600,128]{2,1,0:T(8,128)(2,1)} %get-tuple-element.25), calls=%async_computation | async-start | bytes 4915200 | tf_op jit(solution)/shard_map/all_to_all | solution.py:469
  47.7 7.5 %multiply_convert_fusion.1 = (bf16[384,960]{1,0:T(8,128)(2,1)S(1)}, bf16[384,960]{1,0:T(8,128)(2,1)S(1)}, bf16[384,960]{1,0:T(8,128)(2,1)S(1)}, bf16[384,960]{1,0:T(8,128)(2,1)S(1)}) fusion(f32[384]{0:T(512)S(1)} %get-tuple-element.41, s32[384]{0:T(512)S(1)} %get-tuple-element.42, f32[384]{0:T(512)S(1)} %get-tuple-element.40), kind=kLoop, calls=%fused_computation.10 | loop fusion | flops 6635520 | bytes 2953728 | tf_op jit(solution)/shard_map/convert
  55.7 47.2 %all-to-all-done.refs_1_ = bf16[16,600,128]{2,1,0:T(8,128)(2,1)} async-done(((bf16[16,600,128]{2,1,0:T(8,128)(2,1)}), bf16[16,600,128]{2,1,0:T(8,128)(2,1)}, u32[]{:S(2)}, u32[]{:S(2)}) %all-to-all-start) | async-done | bytes 2457632 | tf_op jit(solution)/shard_map/all_to_all | solution.py:469
  103.1 16.6 %grid_stage.2 = bf16[16,600,128]{2,1,0:T(8,128)(2,1)S(1)} custom-call(s32[1]{0:T(128)} %bitcast.4.refs_0_, bf16[16,600,128]{2,1,0:T(8,128)(2,1)} %all-to-all-done.refs_1_, bf16[30,3,32,960]{3,2,1,0:T(8,128)(2,1)} %bitcast.24, bf16[768,960]{1,0:T(8,128)(2,1)S(1)} %get-tuple-element.49.refs_3_, bf16[768,960]{1,0:T(8,128)(2,1)S(1)} %get-tuple-element.50.refs_4_, ...), custom_call_target="tpu_custom_call" | custom-call | tf_op jit(solution)/shard_map/grid_stage/pallas_call | solution.py:367
  119.6 1.5 copy-done
  121.1 4.9 %all-to-all-start.1 = ((bf16[16,600,128]{2,1,0:T(8,128)(2,1)}), bf16[16,600,128]{2,1,0:T(8,128)(2,1)}, u32[]{:S(2)}, u32[]{:S(2)}) async-start(bf16[16,600,128]{2,1,0:T(8,128)(2,1)} %copy-done), calls=%async_computation.1 | async-start | bytes 4915200 | tf_op jit(solution)/shard_map/all_to_all | solution.py:471
  126.1 1.9 copy.35
  127.9 1.9 pad_maximum_fusion.1
  130.6 1.8 broadcast_multiply_fusion
  134.8 46.8 %all-to-all-done.1.refs_2_ = bf16[16,600,128]{2,1,0:T(8,128)(2,1)} async-done(((bf16[16,600,128]{2,1,0:T(8,128)(2,1)}), bf16[16,600,128]{2,1,0:T(8,128)(2,1)}, u32[]{:S(2)}, u32[]{:S(2)}) %all-to-all-start.1) | async-done | bytes 2457632 | tf_op jit(solution)/shard_map/all_to_all | solution.py:471
  181.6 1.5 copy-done.3
  183.0 1.5 copy-done.8
  185.4 17.1 %forward_inverse.1 = (f32[10,336,128]{2,1,0:T(8,128)S(1)}, bf16[16,600,128]{2,1,0:T(8,128)(2,1)}) custom-call(s32[20]{0:T(128)S(1)} %dynamic_slice.3.refs_0_, f32[10,336,128]{2,1,0:T(8,128)S(1)} %copy-done.8, bf16[16,600,128]{2,1,0:T(8,128)(2,1)} %all-to-all-done.1.refs_2_, bf16[10,336,256]{2,1,0:T(8,128)(2,1)S(1)} %copy-done.3, ...), custom_call_target="tpu_custom_call" | custom-call | tf_op jit(solution)/shard_map/forward_inverse/pallas_call | solution.py:473
  202.5 1.3 copy-done.5
  203.7 4.6 %all-to-all-start.2 = ((bf16[16,600,128]{2,1,0:T(8,128)(2,1)}), bf16[16,600,128]{2,1,0:T(8,128)(2,1)}, u32[]{:S(2)}, u32[]{:S(2)}) async-start(bf16[16,600,128]{2,1,0:T(8,128)(2,1)} %get-tuple-element.28), calls=%async_computation.2 | async-start | bytes 4915200 | tf_op jit(solution)/shard_map/all_to_all | solution.py:469
  208.4 55.2 %all-to-all-done.2.refs_1_ = bf16[16,600,128]{2,1,0:T(8,128)(2,1)} async-done(((bf16[16,600,128]{2,1,0:T(8,128)(2,1)}), bf16[16,600,128]{2,1,0:T(8,128)(2,1)}, u32[]{:S(2)}, u32[]{:S(2)}) %all-to-all-start.2) | async-done | bytes 2457632 | tf_op jit(solution)/shard_map/all_to_all | solution.py:469
  263.6 16.5 %grid_stage.3 = bf16[16,600,128]{2,1,0:T(8,128)(2,1)S(1)} custom-call(s32[1]{0:T(128)} %bitcast.4.refs_0_, bf16[16,600,128]{2,1,0:T(8,128)(2,1)} %all-to-all-done.2.refs_1_, bf16[30,3,32,960]{3,2,1,0:T(8,128)(2,1)} %bitcast.25, bf16[768,960]{1,0:T(8,128)(2,1)S(1)} %get-tuple-element.49.refs_3_, bf16[768,960]{1,0:T(8,128)(2,1)S(1)} %get-tuple-element.50.refs_4_, ...), custom_call_target="tpu_custom_call" | custom-call | tf_op jit(solution)/shard_map/grid_stage/pallas_call | solution.py:367
  280.2 60.1 %all_to_all.20.refs_2_ = bf16[16,600,128]{2,1,0:T(8,128)(2,1)} all-to-all(bf16[16,600,128]{2,1,0:T(8,128)(2,1)S(1)} %grid_stage.3), channel_id=1, replica_groups=mesh['pert'=2,'space'=16] {'space'}, dimensions={0} | all-to-all | bytes 4915200 | tf_op jit(solution)/shard_map/all_to_all | solution.py:471
  340.3 17.9 %forward_last.1 = f32[20,320,128]{2,1,0:T(8,128)} custom-call(s32[20]{0:T(128)S(1)} %dynamic_slice.3.refs_0_, f32[10,336,128]{2,1,0:T(8,128)S(1)} %copy-done.6, bf16[16,600,128]{2,1,0:T(8,128)(2,1)} %all_to_all.20.refs_2_, bf16[10,336,256]{2,1,0:T(8,128)(2,1)S(1)} %copy-done.4, f32[256,128]{1,0:T(8,128)S(1)} %copy-done.10, ...), custom_call_target="tpu_custom_call" | custom-call | tf_op jit(solution)/shard_map/forward_last/pallas_call | solution.py:483
  (61 shorter events, 9.8 us)
Async XLA Ops:
  6.5 96.4 %all-gather.3.cloned.1.call-start = ((), (), s32[]{:S(2)}) async-start(), calls=%async_computation.4 | async-start | bytes 8847360 | tf_op jit(solution)/shard_map/all_gather | solution.py:467
  10.6 1.5 copy-start.15
  15.1 1.1 copy-start.18
  15.1 1.3 copy-start.13
  15.1 11.3 %copy-start.12 = (f32[128,128]{1,0:T(8,128)S(1)}, f32[128,128]{1,0:T(8,128)}, u32[]{:S(2)}) copy-start(f32[128,128]{1,0:T(8,128)} %constant.163.clone.refs_2_) | copy-start | bytes 196612
  25.2 1.2 copy-start.2
  26.4 13.6 %copy-start.1 = (bf16[10,256,384]{2,1,0:T(8,128)(2,1)}, bf16[10,256,384]{2,1,0:T(8,128)(2,1)S(1)}, u32[]{:S(2)}) copy-start(bf16[10,256,384]{2,1,0:T(8,128)(2,1)S(1)} %get-tuple-element.23.refs_3_.refs_4_) | copy-start | bytes 5898244
  40.0 1.2 copy-start.7
  41.2 61.7 %all-to-all-start = ((bf16[16,600,128]{2,1,0:T(8,128)(2,1)}), bf16[16,600,128]{2,1,0:T(8,128)(2,1)}, u32[]{:S(2)}, u32[]{:S(2)}) async-start(bf16[16,600,128]{2,1,0:T(8,128)(2,1)} %get-tuple-element.25), calls=%async_computation | async-start | bytes 4915200 | tf_op jit(solution)/shard_map/all_to_all | solution.py:469
  119.6 1.5 copy-start
  121.1 60.4 %all-to-all-start.1 = ((bf16[16,600,128]{2,1,0:T(8,128)(2,1)}), bf16[16,600,128]{2,1,0:T(8,128)(2,1)}, u32[]{:S(2)}, u32[]{:S(2)}) async-start(bf16[16,600,128]{2,1,0:T(8,128)(2,1)} %copy-done), calls=%async_computation.1 | async-start | bytes 4915200 | tf_op jit(solution)/shard_map/all_to_all | solution.py:471
  126.0 82.4 %all-gather.5.cloned.1.call-start = ((), (), s32[]{:S(2)}) async-start(), calls=%async_computation.5 | async-start | bytes 8847360 | tf_op jit(solution)/shard_map/all_gather | solution.py:467
  126.1 1.9 copy-start.14
  129.8 0.7 copy-start.16
  129.8 4.8 %copy-start.19 = (f32[32]{0:T(128)S(1)}, f32[32]{0:T(128)}, u32[]{:S(2)}) copy-start(f32[32]{0:T(128)} %param.19) | copy-start | bytes 388
  181.6 1.5 copy-start.3
  183.0 1.5 copy-start.8
  184.5 0.9 copy-start.9
  202.5 1.3 copy-start.5
  203.7 59.9 %all-to-all-start.2 = ((bf16[16,600,128]{2,1,0:T(8,128)(2,1)}), bf16[16,600,128]{2,1,0:T(8,128)(2,1)}, u32[]{:S(2)}, u32[]{:S(2)}) async-start(bf16[16,600,128]{2,1,0:T(8,128)(2,1)} %get-tuple-element.28), calls=%async_computation.2 | async-start | bytes 4915200 | tf_op jit(solution)/shard_map/all_to_all | solution.py:469
  280.2 60.1 %copy-start.4 = (bf16[10,336,256]{2,1,0:T(8,128)(2,1)S(1)}, bf16[10,336,256]{2,1,0:T(8,128)(2,1)}, u32[]{:S(2)}) copy-start(bf16[10,336,256]{2,1,0:T(8,128)(2,1)} %copy-done.2) | copy-start | bytes 5160964
  280.2 60.1 %copy-start.6 = (f32[10,336,128]{2,1,0:T(8,128)S(1)}, f32[10,336,128]{2,1,0:T(8,128)}, u32[]{:S(2)}) copy-start(f32[10,336,128]{2,1,0:T(8,128)} %copy-done.5) | copy-start | bytes 5160964
  280.2 60.1 %copy-start.10 = (f32[256,128]{1,0:T(8,128)S(1)}, f32[256,128]{1,0:T(8,128)}, u32[]{:S(2)}) copy-start(f32[256,128]{1,0:T(8,128)} %constant.161.clone.refs_5_.refs_4_) | copy-start | bytes 393220
  280.2 60.1 %copy-start.11 = (f32[128,128]{1,0:T(8,128)S(1)}, f32[128,128]{1,0:T(8,128)}, u32[]{:S(2)}) copy-start(f32[128,128]{1,0:T(8,128)} %constant.164.clone.refs_8_) | copy-start | bytes 196612
  (1 other events, 0.7 us)
Sparse Core Ops, SparseCore 0:
  15.3 76.1 all-gather.2
  130.0 75.5 all-gather.4
where the time goes:
time: 368 us; the launch traced here: 365 us
  waiting for transfers between devices  149 us (40%)
  Pallas kernels  90.5 us (25%)
  blocking collectives  60.1 us (16%)
  local copies, waits for them, and re-layouts  21.8 us (6%)
  starting transfers between devices  16 us (4%)
  other arithmetic  13.8 us (4%)
  between operations  13.6 us (4%)
    all_to_all x3, waiting for transfers between devices, shards(): recv = lax.all_to_all(send, 'space', 0, 0, tiled=True)  149 us
    all_to_all x1, blocking collectives, shards(): recv = lax.all_to_all(send, 'space', 0, 0, tiled=True)  60.1 us
    pallas_call x2, Pallas kernels, grid_stage(): pl.pallas_call(lambda *refs: grid_kernel(sz, *refs), out_shape=jax.ShapeD...  33.1 us
    pallas_call x1, Pallas kernels, shards(): pl.pallas_call(lambda *refs: last_kernel(sz, *refs), out_shape=jax.ShapeD...  17.9 us
    pallas_call x1, Pallas kernels, shards(): pl.pallas_call(lambda *refs: middle_kernel(sz, *refs), out_shape=(state_s...  17.1 us
    all_to_all x3, starting transfers between devices, shards(): recv = lax.all_to_all(send, 'space', 0, 0, tiled=True)  16 us
    unnamed x43, local copies, waits for them, and re-layouts  14.9 us
    pallas_call x1, Pallas kernels, shards(): pl.pallas_call(lambda *refs: first_kernel(sz, *refs), out_shape=(state_sh...  13.5 us
  transfers between devices with their start and end apart: 5, of which 3 were waited for; matrix products, arithmetic and copies ran while one was open for 5% of the time, Pallas kernels for 11%

commit v1 on v0

v1 whole, which is shorter than its diff:
```python
import math

import jax
import jax.numpy as jnp
import numpy as np
from jax import lax
from jax.experimental import pallas as pl
from jax.experimental.pallas import tpu as pltpu
from jax.sharding import PartitionSpec as P

NLAT = 480
NLON = 960
M = 320
VARS = 2
LEV = 32
STEPS = 2
ROWS = 336
ROWS_T = 384
DEPTH = 384
VMEM_BYTES = 48 * 1024 * 1024
BIG = 2.0**32


def params():
    return pltpu.CompilerParams(vmem_limit_bytes=VMEM_BYTES)


def cost(microseconds):
    return pl.CostEstimate(flops=int(microseconds * 1.0e9), bytes_accessed=1 << 20, transcendentals=0)


def vmem(count):
    return [pl.BlockSpec(memory_space=pltpu.VMEM)] * count


def smem(count):
    return [pl.BlockSpec(memory_space=pltpu.SMEM)] * count


class Sizes:
    def __init__(self, space):
        self.space = space
        self.slots = M // space
        self.pairs = self.slots // 2
        self.lats = NLAT // space
        self.half = space // 2
        self.parts = 2
        self.part_pad = -(-self.lats // (8 * self.parts)) * 8
        first = -(-self.lats // self.parts)
        self.part_lats = [first, self.lats - first]
        self.part_start = [0, first]
        self.part_rows = self.half * self.part_pad
        self.north = self.parts * self.part_rows
        self.pair_pad = -(-self.pairs // 8) * 8
        self.group = 8

    def block(self, part):
        return self.slots * self.part_lats[part]

    def block_pad(self, part):
        last = (self.slots - 1) * self.part_lats[part] + self.part_pad
        return -(-last // 8) * 8


def table_kernel(sz, wave_a, wave_b, start_a, start_b, cosines, table, table_t, rows_ref):
    shape = (sz.pair_pad, sz.north)
    wide = shape[1] // 128
    wa, wb = wave_a[...], wave_b[...]
    length = M - wa
    x = cosines[...]
    la, lb = start_a[...], start_b[...]

    def spread(v):
        return jnp.concatenate([v] * wide, axis=1)

    def body(block, carry):
        cur, prev, inv_prev, shift = carry
        big = jnp.maximum(jnp.abs(cur), jnp.abs(prev)) > BIG
        scale = jnp.where(big, 1.0 / BIG, 1.0)
        cur, prev = cur * scale, prev * scale
        shift = shift + jnp.where(big, 32.0, 0.0)
        second = spread(((block * 8).astype(jnp.float32) > length).astype(jnp.float32)) > 0.5
        base = jnp.exp2(0.5 * (jnp.where(second, lb, la) + shift))
        base_b = jnp.exp2(0.5 * lb)
        for j in range(8):
            r = (block * 8 + j).astype(jnp.float32)
            in_b = r >= length
            fresh = r == length
            m = jnp.where(in_b, wb, wa)
            k = jnp.where(in_b, r - length, r)
            n = m + k
            den = k * (2.0 * m + k)
            num = 4.0 * n * n - 1.0
            first = k < 0.5
            safe_den = jnp.where(first, 1.0, den)
            upper = jnp.where(first, 0.0, jnp.sqrt(num / safe_den))
            inv = jnp.where(first, 0.0, jnp.sqrt(safe_den / jnp.where(first, 1.0, num)))
            up_w = spread(upper)
            lo_w = spread(upper * inv_prev)
            new = up_w * x * cur - lo_w * prev
            fresh_w = spread(fresh.astype(jnp.float32)) > 0.5
            start = jnp.logical_or(fresh_w, r == 0.0)
            new = jnp.where(start, 1.0, new)
            prev = jnp.where(start, 0.0, cur)
            shift = jnp.where(fresh_w, 0.0, shift)
            base = jnp.where(fresh_w, base_b, base)
            cur = new
            inv_prev = inv
            value = (cur * base) * base
            for c in range(wide):
                rows_ref[c, pl.ds(block * 8 + j, sz.pair_pad, stride=ROWS), :] = value[
                    :, c * 128 : (c + 1) * 128
                ]
        return cur, prev, inv_prev, shift

    zero = jnp.zeros(shape, jnp.float32)
    lax.fori_loop(0, ROWS // 8, body, (zero, zero, jnp.zeros_like(wa), zero))
    ridx = lax.broadcasted_iota(jnp.int32, (ROWS, sz.north), 0)

    def emit(i, _):
        at = pl.multiple_of(i * ROWS, ROWS)
        full = jnp.concatenate([rows_ref[c, pl.ds(at, ROWS), :] for c in range(wide)], axis=1)
        full = jnp.where(ridx <= M, full, 0.0)
        table[i] = full.astype(jnp.bfloat16)
        padded = jnp.concatenate(
            [full, jnp.zeros((ROWS_T - ROWS, sz.north), jnp.float32)], axis=0
        )
        table_t[i] = jnp.transpose(padded).astype(jnp.bfloat16)
        return 0

    lax.fori_loop(0, sz.pairs, emit, 0)


def make_tables(sz, wave_a, wave_b, log_a, log_b, cosines):
    return pl.pallas_call(
        lambda *refs: table_kernel(sz, *refs),
        out_shape=(
            jax.ShapeDtypeStruct((sz.pairs, ROWS, sz.north), jnp.bfloat16),
            jax.ShapeDtypeStruct((sz.pairs, sz.north, ROWS_T), jnp.bfloat16),
        ),
        in_specs=vmem(5),
        out_specs=tuple(vmem(2)),
        scratch_shapes=[pltpu.VMEM((sz.north // 128, sz.pair_pad * ROWS, 128), jnp.float32)],
        compiler_params=params(),
        name="legendre_tables",
    )(wave_a, wave_b, log_a, log_b, cosines)


def row_facts(waves, i, columns):
    wave_a, wave_b = waves[2 * i], waves[2 * i + 1]
    length = M - wave_a
    r = lax.broadcasted_iota(jnp.int32, (ROWS, columns), 0)
    in_a = r < length
    k = jnp.where(in_a, r, r - length)
    even = jnp.bitwise_and(k, 1) == 0
    return wave_a, wave_b, length, r, in_a, k, even


def send_rows(sz, part, i, state, facts, table_t, stage):
    _, _, _, _, in_a, _, even = facts
    zero = jnp.zeros_like(state)
    in_b = jnp.logical_not(in_a)
    odd = jnp.logical_not(even)
    pieces = [
        jnp.where(jnp.logical_and(side, sign), state, zero).astype(jnp.bfloat16)
        for side in (in_a, in_b)
        for sign in (even, odd)
    ]
    columns = state.shape[1]
    rhs = jnp.concatenate(pieces, axis=1)
    rhs = jnp.concatenate([rhs, jnp.zeros((ROWS_T - ROWS, 4 * columns), jnp.bfloat16)], axis=0)
    rows = table_t[i, part * sz.part_rows : (part + 1) * sz.part_rows, :]
    out = jnp.dot(rows, rhs, preferred_element_type=jnp.float32)
    size = sz.part_pad
    for s in range(2):
        e = out[:, (2 * s) * columns : (2 * s + 1) * columns]
        o = out[:, (2 * s + 1) * columns : (2 * s + 2) * columns]
        north, south = e + o, e - o
        at = (2 * i + s) * sz.part_lats[part]
        for b in range(sz.half):
            lo = b * size
            stage[b, pl.ds(at, size), :] = north[lo : lo + size]
            stage[sz.space - 1 - b, pl.ds(at, size), :] = south[lo : lo + size]


def flush(sz, part, stage, send):
    def body(d, _):
        send[d] = stage[d, : sz.block(part), :].astype(jnp.bfloat16)
        return 0

    lax.fori_loop(0, sz.space, body, 0)


def load_rows(sz, part, recv, stage):
    rows = sz.block_pad(part)

    def body(d, _):
        stage[d, rows - 16 : rows, :] = jnp.zeros((16, stage.shape[2]), jnp.float32)
        stage[d, : sz.block(part), :] = recv[d].astype(jnp.float32)
        return 0

    lax.fori_loop(0, sz.space, body, 0)


def change_rows(sz, part, i, facts, table, weights, stage):
    _, _, _, _, in_a, _, even = facts
    pieces = []
    lo = part * sz.part_rows
    w = weights[lo : lo + sz.part_rows, :]
    size = sz.part_pad
    for s in range(2):
        at = (2 * i + s) * sz.part_lats[part]
        north = jnp.concatenate([stage[b, pl.ds(at, size), :] for b in range(sz.half)], axis=0)
        south = jnp.concatenate(
            [stage[sz.space - 1 - b, pl.ds(at, size), :] for b in range(sz.half)], axis=0
        )
        pieces.append(((north + south) * w).astype(jnp.bfloat16))
        pieces.append(((north - south) * w).astype(jnp.bfloat16))
    rhs = jnp.concatenate(pieces, axis=1)
    out = jnp.dot(table[i, :, lo : lo + sz.part_rows], rhs, preferred_element_type=jnp.float32)
    c = out.shape[1] // 4
    side_a = jnp.where(even, out[:, :c], out[:, c : 2 * c])
    side_b = jnp.where(even, out[:, 2 * c : 3 * c], out[:, 3 * c :])
    return jnp.where(in_a, side_a, side_b)


def kept(state, facts):
    wave_a, wave_b, _, r, in_a, _, _ = facts
    columns = state.shape[1]
    imaginary = lax.broadcasted_iota(jnp.int32, state.shape, 1) >= columns // 2
    wave = jnp.where(in_a, wave_a, wave_b)
    dropped = jnp.logical_or(jnp.logical_and(wave == 0, imaginary), r > M)
    return jnp.where(dropped, 0.0, state)


def halves(x):
    high = x.astype(jnp.bfloat16)
    low = (x - high.astype(jnp.float32)).astype(jnp.bfloat16)
    return jnp.concatenate([high, low], axis=1)


def dot_split(x, both):
    out = jnp.dot(halves(x), both, preferred_element_type=jnp.float32)
    c = out.shape[1] // 2
    return out[:, :c] + out[:, c:]


def updated(state, change, facts, mixing, mixing_t, speeds):
    wave_a, wave_b, _, _, in_a, k, _ = facts
    combined = state + change
    projected = dot_split(combined, mixing[...])
    n = (jnp.where(in_a, wave_a, wave_b) + k).astype(jnp.float32)
    stiffness = speeds[...] * (n * (n + 1.0))
    weighted = projected * (stiffness / (1.0 + stiffness))
    returned = dot_split(weighted, mixing_t[...])
    return kept(combined - returned, facts)


def first_kernel(sz, waves, spectra, turn, table_t, state_ref, send, stage):
    columns = spectra.shape[2]

    def body(i, _):
        facts = row_facts(waves, i, columns)
        length, in_a = facts[2], facts[4]
        blank = jnp.zeros((ROWS - M, columns), jnp.float32)
        rows_a = jnp.concatenate([spectra[2 * i], blank], axis=0)
        rows_b = jnp.concatenate([spectra[2 * i + 1], blank], axis=0)
        packed = jnp.where(in_a, rows_a, pltpu.roll(rows_b, length, 0))
        state = kept(dot_split(packed, turn[...]), facts)
        state_ref[i] = state
        send_rows(sz, 0, i, state, facts, table_t, stage)
        return 0

    lax.fori_loop(0, sz.pairs, body, 0)
    flush(sz, 0, stage, send)


def inverse_kernel(sz, part, waves, state, table_t, send, stage):
    def body(i, _):
        facts = row_facts(waves, i, state.shape[2])
        send_rows(sz, part, i, state[i], facts, table_t, stage)
        return 0

    lax.fori_loop(0, sz.pairs, body, 0)
    flush(sz, part, stage, send)


def forward_kernel(sz, part, waves, state, recv, table, weights, out, stage):
    load_rows(sz, part, recv, stage)

    def body(i, _):
        facts = row_facts(waves, i, state.shape[2])
        out[i] = state[i] + change_rows(sz, part, i, facts, table, weights, stage)
        return 0

    lax.fori_loop(0, sz.pairs, body, 0)


def middle_kernel(
    sz, waves, partial, recv, table, table_t, weights, mixing, mixing_t, speeds,
    state_out, send, stage_in, stage,
):
    columns = partial.shape[2]
    part = sz.parts - 1
    load_rows(sz, part, recv, stage_in)

    def body(i, _):
        facts = row_facts(waves, i, columns)
        change = change_rows(sz, part, i, facts, table, weights, stage_in)
        state = updated(partial[i], change, facts, mixing, mixing_t, speeds)
        state_out[i] = state
        send_rows(sz, 0, i, state, facts, table_t, stage)
        return 0

    lax.fori_loop(0, sz.pairs, body, 0)
    flush(sz, 0, stage, send)


def last_kernel(
    sz, waves, partial, recv, table, weights, mixing, mixing_t, speeds, turn_t, out, stage_in
):
    columns = partial.shape[2]
    part = sz.parts - 1
    load_rows(sz, part, recv, stage_in)

    def body(i, _):
        facts = row_facts(waves, i, columns)
        wave_a, wave_b, length, r = facts[:4]
        change = change_rows(sz, part, i, facts, table, weights, stage_in)
        state = updated(partial[i], change, facts, mixing, mixing_t, speeds)
        state = dot_split(state, turn_t[...])
        out[2 * i] = jnp.where(r < length, state, 0.0)[:M]
        rolled = pltpu.roll(state, ROWS - length, 0)
        out[2 * i + 1] = jnp.where(r < M - wave_b, rolled, 0.0)[:M]
        return 0

    lax.fori_loop(0, sz.pairs, body, 0)


def grid_kernel(
    sz, part, flip, recv, traj, synth, slope, scale, send, stage_in, stage, lhs, values, slopes, force
):
    lanes = recv.shape[2]
    rows = lanes // 2
    lats = sz.part_lats[part]
    block = sz.block(part)
    groups = -(-lats // sz.group)

    def load(d, _):
        stage_in[pl.ds(d * block, block), :] = recv[d].astype(jnp.float32)
        return 0

    lax.fori_loop(0, sz.space, load, 0)
    blank = jnp.zeros((DEPTH - M, lanes), jnp.float32)

    def body(g, _):
        for q in range(sz.group):
            t = jnp.minimum(g * sz.group + q, lats - 1)
            rows_t = stage_in[pl.ds(t, M, stride=lats), :]
            turned = jnp.transpose(jnp.concatenate([rows_t, blank], axis=0)).astype(jnp.bfloat16)
            lhs[q * rows : (q + 1) * rows, :DEPTH] = turned[:rows]
            lhs[q * rows : (q + 1) * rows, DEPTH:] = turned[rows:]
        left = lhs[...]
        values[...] = jnp.dot(left, synth[...], preferred_element_type=jnp.float32)
        slopes[...] = jnp.dot(left, slope[...], preferred_element_type=jnp.float32)
        for q in range(sz.group):
            t = jnp.minimum(g * sz.group + q, lats - 1)
            here = jnp.where(flip[0] == 1, lats - 1 - t, t)
            wind = traj[here, 0].astype(jnp.float32)
            for v in range(VARS):
                lo = q * rows + v * LEV
                other = traj[here, 1 + (v + 1) % VARS].astype(jnp.float32)
                force[lo : lo + LEV, :] = (
                    wind * slopes[lo : lo + LEV, :] + other * values[lo : lo + LEV, :]
                ).astype(jnp.bfloat16)
        forcing = force[...]
        spectrum = [
            lax.dot_general(
                synth[c * DEPTH : c * DEPTH + M, :],
                forcing,
                (((1,), (1,)), ((), ())),
                preferred_element_type=jnp.float32,
            )
            * scale[...][:, :1]
            for c in range(2)
        ]
        left_side = lax.broadcasted_iota(jnp.int32, (M, lanes), 1) < rows
        for q in range(0, sz.group, 2):
            re = spectrum[0][:, q * rows : (q + 2) * rows]
            im = spectrum[1][:, q * rows : (q + 2) * rows]
            pair = (
                jnp.where(left_side, re, pltpu.roll(im, rows, 1)),
                jnp.where(left_side, pltpu.roll(re, rows, 1), im),
            )
            for o in range(2):
                t = g * sz.group + q + o

                def store(t=t, value=pair[o]):
                    stage[pl.ds(t, M, stride=lats), :] = value

                if (groups - 1) * sz.group + q + o < lats:
                    store()
                else:
                    pl.when(t < lats)(store)
        return 0

    lax.fori_loop(0, groups, body, 0)

    def out(d, _):
        send[d] = stage[pl.ds(d * block, block), :].astype(jnp.bfloat16)
        return 0

    lax.fori_loop(0, sz.space, out, 0)


def grid_stage(sz, part, flip, recv, traj, synth, slope, scale):
    lanes = recv.shape[2]
    wide = sz.group * lanes // 2
    count = M * sz.part_lats[part]
    return pl.pallas_call(
        lambda *refs: grid_kernel(sz, part, *refs),
        out_shape=jax.ShapeDtypeStruct(recv.shape, jnp.bfloat16),
        in_specs=smem(1) + vmem(5),
        out_specs=vmem(1)[0],
        scratch_shapes=[
            pltpu.VMEM((count, lanes), jnp.float32),
            pltpu.VMEM((count, lanes), jnp.float32),
            pltpu.VMEM((wide, 2 * DEPTH), jnp.bfloat16),
            pltpu.VMEM((wide, NLON), jnp.float32),
            pltpu.VMEM((wide, NLON), jnp.float32),
            pltpu.VMEM((wide, NLON), jnp.bfloat16),
        ],
        compiler_params=params(),
        cost_estimate=cost(9.0),
        name="grid_stage",
    )(flip, recv, traj, synth, slope, scale)


def zonal_tables(wave_list):
    cell_index = jnp.arange(NLON, dtype=jnp.int32)
    wave_pad = jnp.concatenate([wave_list, jnp.zeros((DEPTH - M,), jnp.int32)])
    phase_index = wave_pad[:, None] * cell_index[None, :] % NLON
    angles = phase_index.astype(jnp.float32) * (2.0 * math.pi / NLON)
    factor = jnp.where(wave_pad == 0, 1.0, 2.0).astype(jnp.float32)
    inside = (jnp.arange(DEPTH) < M).astype(jnp.float32)
    gain = (factor * inside)[:, None]
    cosine, sine = gain * jnp.cos(angles), gain * jnp.sin(angles)
    wave = wave_pad.astype(jnp.float32)[:, None]
    synth = jnp.concatenate([-cosine, sine], axis=0).astype(jnp.bfloat16)
    slope = jnp.concatenate([wave * sine, wave * cosine], axis=0).astype(jnp.bfloat16)
    scale = jnp.broadcast_to((-1.0 / (NLON * factor[:M]))[:, None], (M, 128))
    return synth, slope, scale


def column_turn(columns):
    turn = np.zeros((columns, columns), np.float32)
    for c in range(columns):
        part, row = c % 2, c // 2
        turn[c, part * (columns // 2) + row] = 1.0
    return turn


def split_matrix(matrix):
    high = matrix.astype(jnp.bfloat16)
    low = (matrix - high.astype(jnp.float32)).astype(jnp.bfloat16)
    top = jnp.concatenate([high, low], axis=1)
    bottom = jnp.concatenate([high, jnp.zeros_like(low)], axis=1)
    return jnp.concatenate([top, bottom], axis=0)


def sectoral(wave, log_sine):
    gammas = jax.scipy.special.gammaln
    start = 0.5 * (
        gammas(wave + 1.5) - gammas(wave + 1.0) - gammas(jnp.float32(1.5))
    ) - 0.5 * math.log(2.0)
    return (start[:, None] + wave[:, None] * log_sine[None, :]) * (1.0 / math.log(2.0))


def shards(sz, spectra, wave_order, traj_wind, traj_state, vertical_modes, mode_speeds):
    columns = spectra.shape[2]
    rank = lax.axis_index("space")
    waves = lax.dynamic_slice_in_dim(wave_order, rank * sz.slots, sz.slots)

    place = np.arange(sz.north)
    part, within = place // sz.part_rows, place % sz.part_rows
    block, inner = within // sz.part_pad, within % sz.part_pad
    real = inner < np.asarray(sz.part_lats)[part]
    index = block * sz.lats + np.asarray(sz.part_start)[part] + inner
    colat = np.where(real, (index + 0.5) * (math.pi / NLAT), math.pi / 2)
    cosines = jnp.asarray(np.cos(colat), jnp.float32)[None, :]
    log_sine = jnp.asarray(np.log(np.sin(colat)), jnp.float32)
    weights = jnp.asarray(
        np.broadcast_to((np.sin(colat) * (math.pi / NLAT) * real)[:, None], (sz.north, columns)),
        jnp.float32,
    )

    pair_waves = jnp.zeros((sz.pair_pad, 2), jnp.int32).at[: sz.pairs].set(waves.reshape(-1, 2))
    pair_waves = pair_waves.astype(jnp.float32)
    wide_a = jnp.broadcast_to(pair_waves[:, :1], (sz.pair_pad, 128))
    wide_b = jnp.broadcast_to(pair_waves[:, 1:], (sz.pair_pad, 128))
    table, table_t = make_tables(
        sz, wide_a, wide_b, sectoral(pair_waves[:, 0], log_sine), sectoral(pair_waves[:, 1], log_sine), cosines
    )

    turn = column_turn(columns)
    same = np.kron(np.eye(columns // LEV, dtype=np.float32), np.ones((LEV, LEV), np.float32))
    mixing = split_matrix(jnp.tile(vertical_modes.T, (columns // LEV, columns // LEV)) * same)
    mixing_t = split_matrix(jnp.tile(vertical_modes, (columns // LEV, columns // LEV)) * same)
    speeds = jnp.tile(mode_speeds, columns // LEV)[None, :]
    turn, turn_t = split_matrix(jnp.asarray(turn)), split_matrix(jnp.asarray(turn.T))

    synth, slope, scale = zonal_tables(wave_order)
    south = rank >= sz.half
    flip = jnp.where(south, 1, 0).astype(jnp.int32).reshape(1)

    def stages(part):
        return pltpu.VMEM((sz.space, sz.block_pad(part), columns), jnp.float32)

    def sends(part):
        return jax.ShapeDtypeStruct((sz.space, sz.block(part), columns), jnp.bfloat16)

    state_shape = jax.ShapeDtypeStruct((sz.pairs, ROWS, columns), jnp.float32)

    def call(body, out_shape, args, scratch, microseconds, name):
        single = not isinstance(out_shape, tuple)
        outs = vmem(1)[0] if single else tuple(vmem(len(out_shape)))
        return pl.pallas_call(
            body,
            out_shape=out_shape,
            in_specs=smem(1) + vmem(len(args) - 1),
            out_specs=outs,
            scratch_shapes=scratch,
            compiler_params=params(),
            cost_estimate=cost(microseconds),
            name=name,
        )(*args)

    def gather(step, part):
        local = jnp.concatenate([traj_wind[step][None], traj_state[step]], axis=0)
        start, size = sz.part_start[part], sz.part_lats[part]
        at = jnp.where(south, sz.lats - start - size, start)
        local = lax.dynamic_slice_in_dim(local, at, size, axis=2)
        traj = lax.all_gather(local, "pert", axis=1, tiled=True)
        return jnp.transpose(traj, (2, 0, 1, 3))

    def transpose(value):
        return lax.all_to_all(value, "space", 0, 0, tiled=True)

    def inverse_rest(state):
        return call(
            lambda *refs: inverse_kernel(sz, 1, *refs),
            sends(1), (waves, state, table_t), [stages(1)], 6.0, "inverse_rest",
        )

    state, send_0 = call(
        lambda *refs: first_kernel(sz, *refs),
        (state_shape, sends(0)), (waves, spectra, turn, table_t), [stages(0)], 8.0, "first_inverse",
    )
    for step in range(STEPS):
        recv_0 = transpose(send_0)
        recv_1 = transpose(inverse_rest(state))
        back_0 = transpose(
            grid_stage(sz, 0, flip, recv_0, gather(step, 0), synth, slope, scale)
        )
        back_1 = transpose(
            grid_stage(sz, 1, flip, recv_1, gather(step, 1), synth, slope, scale)
        )
        partial = call(
            lambda *refs: forward_kernel(sz, 0, *refs),
            state_shape, (waves, state, back_0, table, weights), [stages(0)], 6.0, "forward_part",
        )
        if step < STEPS - 1:
            state, send_0 = call(
                lambda *refs: middle_kernel(sz, *refs),
                (state_shape, sends(0)),
                (waves, partial, back_1, table, table_t, weights, mixing, mixing_t, speeds),
                [stages(1), stages(0)], 12.0, "forward_inverse",
            )
        else:
            out = call(
                lambda *refs: last_kernel(sz, *refs),
                jax.ShapeDtypeStruct(spectra.shape, jnp.float32),
                (waves, partial, back_1, table, weights, mixing, mixing_t, speeds, turn_t),
                [stages(1)], 10.0, "forward_last",
            )
    return out


def solution(mesh):
    sz = Sizes(mesh.shape["space"])
    placed = (
        P("space", None, "pert"),
        P(),
        P(None, "pert", "space", None),
        P(None, None, "pert", "space", None),
        P(),
        P(),
    )
    return jax.shard_map(
        lambda *args: shards(sz, *args),
        mesh=mesh,
        in_specs=placed,
        out_specs=P("space", None, "pert"),
        check_vma=False,
    )
```

time: 368 us -> 351 us (0.954)
  blocking collectives: 60.1 us -> 0 us
  starting transfers between devices: 16 us -> 43.1 us
  local copies, waits for them, and re-layouts: 21.8 us -> 36 us
  other arithmetic: 13.8 us -> 20.1 us
    all_to_all x3 -> x8, waiting for transfers between devices: 149 us -> 82.3 us  [transpose(): return lax.all_to_all(value, 'space', 0, 0, tiled=True)]
    all_gather x2 -> x4, waiting for transfers between devices: 0.01 us -> 64.9 us  [gather(): traj = lax.all_gather(local, 'pert', axis=1, tiled=True)]
    all_to_all x1 -> x0, blocking collectives: 60.1 us -> none  [shards(): recv = lax.all_to_all(send, 'space', 0, 0, tiled=True)]
    all_to_all x3 -> x8, starting transfers between devices: 16 us -> 42.9 us  [transpose(): return lax.all_to_all(value, 'space', 0, 0, tiled=True)]
    unnamed x43 -> x67, local copies, waits for them, and re-layouts: 14.9 us -> 27.8 us
    pallas_call x5 -> x11, Pallas kernels: 81.7 us -> 78.7 us  [the longest x7 44.8 us: call(): pl.pallas_call(body, out_shape=out_shape, in_specs=smem(1) + vmem(len(arg...]
  transfers between devices with their start and end apart: 5 -> 12, of which waited for: 3 -> 10; matrix products, arithmetic and copies ran while one was open for 5% -> 8% of each run, Pallas kernels for 11% -> 15%
where the time goes in v1:
time: 351 us; the launch traced here: 349 us
  waiting for transfers between devices  148 us (42%)
  Pallas kernels  87.5 us (25%)
  starting transfers between devices  43.1 us (12%)
  local copies, waits for them, and re-layouts  36 us (10%)
  other arithmetic  20.1 us (6%)
  between operations  13.5 us (4%)
    all_to_all x8, waiting for transfers between devices, transpose(): return lax.all_to_all(value, 'space', 0, 0, tiled=True)  82.3 us
    all_gather x4, waiting for transfers between devices, gather(): traj = lax.all_gather(local, 'pert', axis=1, tiled=True)  64.9 us
    pallas_call x7, Pallas kernels, call(): pl.pallas_call(body, out_shape=out_shape, in_specs=smem(1) + vmem(len(arg...  44.8 us
    all_to_all x8, starting transfers between devices, transpose(): return lax.all_to_all(value, 'space', 0, 0, tiled=True)  42.9 us
    pallas_call x4, Pallas kernels, grid_stage(): pl.pallas_call(lambda *refs: grid_kernel(sz, part, *refs), out_shape=jax....  33.9 us
    unnamed x67, local copies, waits for them, and re-layouts  27.8 us
    another operation x1, other arithmetic  8.79 us
    pallas_call x1, Pallas kernels, make_tables(): pl.pallas_call(lambda *refs: table_kernel(sz, *refs), out_shape=(jax.Shap...  8.78 us
  transfers between devices with their start and end apart: 12, of which 10 were waited for; matrix products, arithmetic and copies ran while one was open for 8% of the time, Pallas kernels for 15%

profile of v1, /device:TPU:15, one launch (start us, length us, event | category | flops | bytes accessed | tf_op | source)
XLA Modules:
  0.0 348.6 jit_solution(4607403820044110631)
XLA Ops:
  9.2 8.8 %legendre_tables.1 = (bf16[10,336,256]{2,1,0:T(8,128)(2,1)S(1)}, bf16[10,256,384]{2,1,0:T(8,128)(2,1)S(1)}) custom-call(f32[16,128]{1,0:T(8,128)S(1)} %broadcast_in_dim.21.refs_0_, f32[16,128]{1,0:T(8,128)S(1)} %broadcast_in_dim.23.refs_1_, f32[16,256]{1,0:T(8,128)S(1)} %get-tuple-element.52.refs_2_, f32[16,256]{1,0:T(8,128)S(1)} %get-tuple-element.51.refs_3_, ...), custom_call_target="tpu_custom_call" | custom-call | tf_op jit(solution)/shard_map/legendre_tables/pallas_call | solution.py:135
  19.1 8.3 %first_inverse.1 = (f32[10,336,128]{2,1,0:T(8,128)S(1)}, bf16[16,300,128]{2,1,0:T(8,128)(2,1)}) custom-call(s32[20]{0:T(128)S(1)} %dynamic_slice.15.refs_0_, f32[20,320,128]{2,1,0:T(8,128)} %refs_1_.1, bf16[256,256]{1,0:T(8,128)(2,1)S(1)} %copy-done.19, bf16[10,256,384]{2,1,0:T(8,128)(2,1)S(1)} %get-tuple-element.23.refs_3_.refs_2_.refs_4_), custom_call_target="tpu_custom_call" | custom-call | flops 8000000000 | bytes 1048576 | tf_op jit(solution)/shard_map/first_inverse/pallas_call | solution.py:527
  28.6 6.6 %all-to-all-start = ((bf16[16,300,128]{2,1,0:T(8,128)(2,1)}), bf16[16,300,128]{2,1,0:T(8,128)(2,1)S(1)}, u32[]{:S(2)}, u32[]{:S(2)}) async-start(bf16[16,300,128]{2,1,0:T(8,128)(2,1)} %get-tuple-element.25), calls=%async_computation | async-start | bytes 2490368 | tf_op jit(solution)/shard_map/all_to_all | solution.py:547
  48.8 15.9 %all-to-all-done.refs_1_ = bf16[16,300,128]{2,1,0:T(8,128)(2,1)S(1)} async-done(((bf16[16,300,128]{2,1,0:T(8,128)(2,1)}), bf16[16,300,128]{2,1,0:T(8,128)(2,1)S(1)}, u32[]{:S(2)}, u32[]{:S(2)}) %all-to-all-start) | async-done | bytes 1228832 | tf_op jit(solution)/shard_map/all_to_all | solution.py:547
  70.0 8.8 %multiply_convert_fusion.1 = (bf16[384,960]{1,0:T(8,128)(2,1)}, bf16[384,960]{1,0:T(8,128)(2,1)}, bf16[384,960]{1,0:T(8,128)(2,1)}, bf16[384,960]{1,0:T(8,128)(2,1)}) fusion(f32[384]{0:T(512)S(1)} %get-tuple-element.49, s32[384]{0:T(512)S(1)} %get-tuple-element.50, f32[384]{0:T(512)S(1)} %get-tuple-element.48), kind=kLoop, calls=%fused_computation.16 | loop fusion | flops 6635520 | bytes 2953728 | tf_op jit(solution)/shard_map/convert
  86.9 8.2 %grid_stage.4 = bf16[16,300,128]{2,1,0:T(8,128)(2,1)S(1)} custom-call(s32[1]{0:T(128)} %bitcast.4.refs_0_, bf16[16,300,128]{2,1,0:T(8,128)(2,1)S(1)} %copy-done.1, bf16[15,3,32,960]{3,2,1,0:T(8,128)(2,1)} %bitcast.23, bf16[768,960]{1,0:T(8,128)(2,1)S(1)} %get-tuple-element.59.refs_3_, bf16[768,960]{1,0:T(8,128)(2,1)S(1)} %get-tuple-element.60.refs_4_, ...), custom_call_target="tpu_custom_call" | custom-call | flops 8999999488 | bytes 1048576 | tf_op jit(solution)/shard_map/grid_stage/pallas_call | solution.py:420
  98.4 4.9 %all-to-all-start.1 = ((bf16[16,300,128]{2,1,0:T(8,128)(2,1)}), bf16[16,300,128]{2,1,0:T(8,128)(2,1)}, u32[]{:S(2)}, u32[]{:S(2)}) async-start(bf16[16,300,128]{2,1,0:T(8,128)(2,1)} %copy-done.6), calls=%async_computation.1 | async-start | bytes 2490368 | tf_op jit(solution)/shard_map/all_to_all | solution.py:547
  103.3 26.5 %all-gather.7.cloned.1.call-done = bf16[3,32,15,960]{3,1,0,2:T(8,128)(2,1)} async-done(((bf16[3,16,15,960]{3,1,0,2:T(8,128)(2,1)}), bf16[3,32,15,960]{3,1,0,2:T(8,128)(2,1)}) %all-gather.7.cloned.1.call-update) | async-done | bytes 2764816 | tf_op jit(solution)/shard_map/all_gather | solution.py:543
  129.8 8.6 %grid_stage.5 = bf16[16,300,128]{2,1,0:T(8,128)(2,1)S(1)} custom-call(s32[1]{0:T(128)} %bitcast.4.refs_0_, bf16[16,300,128]{2,1,0:T(8,128)(2,1)} %all-to-all-done.2.refs_1_, bf16[15,3,32,960]{3,2,1,0:T(8,128)(2,1)} %bitcast.24, bf16[768,960]{1,0:T(8,128)(2,1)S(1)} %get-tuple-element.59.refs_3_, bf16[768,960]{1,0:T(8,128)(2,1)S(1)} %get-tuple-element.60.refs_4_, ...), custom_call_target="tpu_custom_call" | custom-call | flops 8999999488 | bytes 1048576 | tf_op jit(solution)/shard_map/grid_stage/pallas_call | solution.py:420
  139.5 6.5 %all-to-all-start.3 = ((bf16[16,300,128]{2,1,0:T(8,128)(2,1)}), bf16[16,300,128]{2,1,0:T(8,128)(2,1)}, u32[]{:S(2)}, u32[]{:S(2)}) async-start(bf16[16,300,128]{2,1,0:T(8,128)(2,1)} %copy-done.2), calls=%async_computation.3 | async-start | bytes 2490368 | tf_op jit(solution)/shard_map/all_to_all | solution.py:547
  159.1 16.2 %all-to-all-done.3.refs_2_ = bf16[16,300,128]{2,1,0:T(8,128)(2,1)} async-done(((bf16[16,300,128]{2,1,0:T(8,128)(2,1)}), bf16[16,300,128]{2,1,0:T(8,128)(2,1)}, u32[]{:S(2)}, u32[]{:S(2)}) %all-to-all-start.3) | async-done | bytes 1228832 | tf_op jit(solution)/shard_map/all_to_all | solution.py:547
  177.1 10.2 %forward_inverse.1 = (f32[10,336,128]{2,1,0:T(8,128)S(1)}, bf16[16,300,128]{2,1,0:T(8,128)(2,1)S(1)}) custom-call(s32[20]{0:T(128)S(1)} %dynamic_slice.15.refs_0_, f32[10,336,128]{2,1,0:T(8,128)} %copy-done.28, bf16[16,300,128]{2,1,0:T(8,128)(2,1)} %all-to-all-done.3.refs_2_, bf16[10,336,256]{2,1,0:T(8,128)(2,1)} %copy-done.13, ...), custom_call_target="tpu_custom_call" | custom-call | flops 12000000000 | bytes 1048576 | tf_op jit(solution)/shard_map/forward_inverse/pallas_call | solution.py:527
  189.5 4.9 %all-to-all-start.4 = ((bf16[16,300,128]{2,1,0:T(8,128)(2,1)}), bf16[16,300,128]{2,1,0:T(8,128)(2,1)}, u32[]{:S(2)}, u32[]{:S(2)}) async-start(bf16[16,300,128]{2,1,0:T(8,128)(2,1)} %copy-done.3), calls=%async_computation.4 | async-start | bytes 2490368 | tf_op jit(solution)/shard_map/all_to_all | solution.py:547
  205.4 18.5 %all-to-all-done.4.refs_1_ = bf16[16,300,128]{2,1,0:T(8,128)(2,1)} async-done(((bf16[16,300,128]{2,1,0:T(8,128)(2,1)}), bf16[16,300,128]{2,1,0:T(8,128)(2,1)}, u32[]{:S(2)}, u32[]{:S(2)}) %all-to-all-start.4) | async-done | bytes 1228832 | tf_op jit(solution)/shard_map/all_to_all | solution.py:547
  223.9 4.6 %all-to-all-start.6 = ((bf16[16,300,128]{2,1,0:T(8,128)(2,1)}), bf16[16,300,128]{2,1,0:T(8,128)(2,1)}, u32[]{:S(2)}, u32[]{:S(2)}) async-start(bf16[16,300,128]{2,1,0:T(8,128)(2,1)} %copy-done.4), calls=%async_computation.6 | async-start | bytes 2490368 | tf_op jit(solution)/shard_map/all_to_all | solution.py:547
  229.1 11.6 %all-gather.9.cloned.1.call-done = bf16[3,32,15,960]{3,1,0,2:T(8,128)(2,1)} async-done(((bf16[3,16,15,960]{3,1,0,2:T(8,128)(2,1)}), bf16[3,32,15,960]{3,1,0,2:T(8,128)(2,1)}) %all-gather.9.cloned.1.call-update) | async-done | bytes 2764816 | tf_op jit(solution)/shard_map/all_gather | solution.py:543
  240.7 8.6 %grid_stage.6 = bf16[16,300,128]{2,1,0:T(8,128)(2,1)S(1)} custom-call(s32[1]{0:T(128)} %bitcast.4.refs_0_, bf16[16,300,128]{2,1,0:T(8,128)(2,1)} %all-to-all-done.4.refs_1_, bf16[15,3,32,960]{3,2,1,0:T(8,128)(2,1)} %bitcast.25, bf16[768,960]{1,0:T(8,128)(2,1)S(1)} %get-tuple-element.59.refs_3_, bf16[768,960]{1,0:T(8,128)(2,1)S(1)} %get-tuple-element.60.refs_4_, ...), custom_call_target="tpu_custom_call" | custom-call | flops 8999999488 | bytes 1048576 | tf_op jit(solution)/shard_map/grid_stage/pallas_call | solution.py:420
  250.3 7.7 %all-to-all-done.6.refs_1_ = bf16[16,300,128]{2,1,0:T(8,128)(2,1)} async-done(((bf16[16,300,128]{2,1,0:T(8,128)(2,1)}), bf16[16,300,128]{2,1,0:T(8,128)(2,1)}, u32[]{:S(2)}, u32[]{:S(2)}) %all-to-all-start.6) | async-done | bytes 1228832 | tf_op jit(solution)/shard_map/all_to_all | solution.py:547
  262.6 22.3 %all-gather.11.cloned.1.call-done = bf16[3,32,15,960]{3,1,0,2:T(8,128)(2,1)} async-done(((bf16[3,16,15,960]{3,1,0,2:T(8,128)(2,1)}), bf16[3,32,15,960]{3,1,0,2:T(8,128)(2,1)}) %all-gather.11.cloned.1.call-update) | async-done | bytes 2764816 | tf_op jit(solution)/shard_map/all_gather | solution.py:543
  285.0 8.6 %grid_stage.7 = bf16[16,300,128]{2,1,0:T(8,128)(2,1)S(1)} custom-call(s32[1]{0:T(128)} %bitcast.4.refs_0_, bf16[16,300,128]{2,1,0:T(8,128)(2,1)} %all-to-all-done.6.refs_1_, bf16[15,3,32,960]{3,2,1,0:T(8,128)(2,1)} %bitcast.26, bf16[768,960]{1,0:T(8,128)(2,1)S(1)} %get-tuple-element.59.refs_3_, bf16[768,960]{1,0:T(8,128)(2,1)S(1)} %get-tuple-element.60.refs_4_, ...), custom_call_target="tpu_custom_call" | custom-call | flops 8999999488 | bytes 1048576 | tf_op jit(solution)/shard_map/grid_stage/pallas_call | solution.py:420
  294.6 6.5 %all-to-all-start.7 = ((bf16[16,300,128]{2,1,0:T(8,128)(2,1)}), bf16[16,300,128]{2,1,0:T(8,128)(2,1)S(1)}, u32[]{:S(2)}, u32[]{:S(2)}) async-start(bf16[16,300,128]{2,1,0:T(8,128)(2,1)} %copy-done.7), calls=%async_computation.7 | async-start | bytes 2490368 | tf_op jit(solution)/shard_map/all_to_all | solution.py:547
  302.6 4.7 %forward_part.3.refs_1_ = f32[10,336,128]{2,1,0:T(8,128)S(1)} custom-call(s32[20]{0:T(128)S(1)} %dynamic_slice.15.refs_0_, f32[10,336,128]{2,1,0:T(8,128)S(1)} %copy-done.25, bf16[16,300,128]{2,1,0:T(8,128)(2,1)} %all-to-all-done.5.refs_2_, bf16[10,336,256]{2,1,0:T(8,128)(2,1)} %copy-done.13, f32[256,128]{1,0:T(8,128)S(1)} %copy-done.17), custom_call_target="tpu_custom_call" | custom-call | flops 6000000000 | bytes 1048576 | tf_op jit(solution)/shard_map/forward_part/pallas_call | solution.py:527
  308.5 21.8 %all-to-all-done.7.refs_2_ = bf16[16,300,128]{2,1,0:T(8,128)(2,1)S(1)} async-done(((bf16[16,300,128]{2,1,0:T(8,128)(2,1)}), bf16[16,300,128]{2,1,0:T(8,128)(2,1)S(1)}, u32[]{:S(2)}, u32[]{:S(2)}) %all-to-all-start.7) | async-done | bytes 1228832 | tf_op jit(solution)/shard_map/all_to_all | solution.py:547
  332.6 9.5 %forward_last.1 = f32[20,320,128]{2,1,0:T(8,128)} custom-call(s32[20]{0:T(128)S(1)} %dynamic_slice.15.refs_0_, f32[10,336,128]{2,1,0:T(8,128)S(1)} %copy-done.27, bf16[16,300,128]{2,1,0:T(8,128)(2,1)S(1)} %all-to-all-done.7.refs_2_, bf16[10,336,256]{2,1,0:T(8,128)(2,1)S(1)} %copy-done.14, f32[256,128]{1,0:T(8,128)S(1)} %copy-done.17, ...), custom_call_target="tpu_custom_call" | custom-call | flops 10000000000 | bytes 1048576 | tf_op jit(solution)/shard_map/forward_last/pallas_call | solution.py:527
  (110 shorter events, 76.7 us)
Async XLA Ops:
  18.0 9.4 %copy-start.13 = (bf16[10,336,256]{2,1,0:T(8,128)(2,1)}, bf16[10,336,256]{2,1,0:T(8,128)(2,1)S(1)}, u32[]{:S(2)}) copy-start(bf16[10,336,256]{2,1,0:T(8,128)(2,1)S(1)} %get-tuple-element.26.refs_3_) | copy-start | bytes 5160964
  18.0 25.0 %copy-start.11 = (bf16[10,256,384]{2,1,0:T(8,128)(2,1)}, bf16[10,256,384]{2,1,0:T(8,128)(2,1)S(1)}, u32[]{:S(2)}) copy-start(bf16[10,256,384]{2,1,0:T(8,128)(2,1)S(1)} %get-tuple-element.23.refs_3_.refs_2_.refs_4_) | copy-start | bytes 5898244
  28.6 36.1 %all-to-all-start = ((bf16[16,300,128]{2,1,0:T(8,128)(2,1)}), bf16[16,300,128]{2,1,0:T(8,128)(2,1)S(1)}, u32[]{:S(2)}, u32[]{:S(2)}) async-start(bf16[16,300,128]{2,1,0:T(8,128)(2,1)} %get-tuple-element.25), calls=%async_computation | async-start | bytes 2490368 | tf_op jit(solution)/shard_map/all_to_all | solution.py:547
  35.1 50.4 %all-gather.5.cloned.1.call-start = ((), (), s32[]{:S(2)}) async-start(), calls=%async_computation.8 | async-start | bytes 4423680 | tf_op jit(solution)/shard_map/all_gather | solution.py:543
  35.2 2.8 copy-start.29
  43.0 1.5 copy-start.21
  48.8 21.1 %copy-start.31 = (s32[320]{0:T(512)S(1)}, s32[320]{0:T(512)}, u32[]{:S(2)}) copy-start(s32[320]{0:T(512)} %param.15) | copy-start | bytes 3844
  64.7 5.2 %copy-start = (bf16[16,300,128]{2,1,0:T(8,128)(2,1)}, bf16[16,300,128]{2,1,0:T(8,128)(2,1)S(1)}, u32[]{:S(2)}) copy-start(bf16[16,300,128]{2,1,0:T(8,128)(2,1)S(1)} %all-to-all-done.refs_1_) | copy-start | bytes 3686404
  64.7 33.7 %all-to-all-start.2 = ((bf16[16,300,128]{2,1,0:T(8,128)(2,1)}), bf16[16,300,128]{2,1,0:T(8,128)(2,1)}, u32[]{:S(2)}, u32[]{:S(2)}) async-start(bf16[16,300,128]{2,1,0:T(8,128)(2,1)} %inverse_rest.2), calls=%async_computation.2 | async-start | bytes 2490368 | tf_op jit(solution)/shard_map/all_to_all | solution.py:547
  69.2 60.6 %all-gather.7.cloned.1.call-start = ((), (), s32[]{:S(2)}) async-start(), calls=%async_computation.9 | async-start | bytes 4423680 | tf_op jit(solution)/shard_map/all_gather | solution.py:543
  98.4 41.1 %all-to-all-start.1 = ((bf16[16,300,128]{2,1,0:T(8,128)(2,1)}), bf16[16,300,128]{2,1,0:T(8,128)(2,1)}, u32[]{:S(2)}, u32[]{:S(2)}) async-start(bf16[16,300,128]{2,1,0:T(8,128)(2,1)} %copy-done.6), calls=%async_computation.1 | async-start | bytes 2490368 | tf_op jit(solution)/shard_map/all_to_all | solution.py:547
  139.5 6.5 %copy-start.30 = (f32[32,32]{1,0:T(8,128)S(1)}, f32[32,32]{1,0:T(8,128)}, u32[]{:S(2)}) copy-start(f32[32,32]{1,0:T(8,128)} %param.18) | copy-start | bytes 12292
  139.5 10.7 %copy-start.32 = (f32[32]{0:T(128)S(1)}, f32[32]{0:T(128)}, u32[]{:S(2)}) copy-start(f32[32]{0:T(128)} %param.19) | copy-start | bytes 388
  139.5 35.8 %all-to-all-start.3 = ((bf16[16,300,128]{2,1,0:T(8,128)(2,1)}), bf16[16,300,128]{2,1,0:T(8,128)(2,1)}, u32[]{:S(2)}, u32[]{:S(2)}) async-start(bf16[16,300,128]{2,1,0:T(8,128)(2,1)} %copy-done.2), calls=%async_computation.3 | async-start | bytes 2490368 | tf_op jit(solution)/shard_map/all_to_all | solution.py:547
  189.5 34.4 %all-to-all-start.4 = ((bf16[16,300,128]{2,1,0:T(8,128)(2,1)}), bf16[16,300,128]{2,1,0:T(8,128)(2,1)}, u32[]{:S(2)}, u32[]{:S(2)}) async-start(bf16[16,300,128]{2,1,0:T(8,128)(2,1)} %copy-done.3), calls=%async_computation.4 | async-start | bytes 2490368 | tf_op jit(solution)/shard_map/all_to_all | solution.py:547
  194.4 46.4 %all-gather.9.cloned.1.call-start = ((), (), s32[]{:S(2)}) async-start(), calls=%async_computation.10 | async-start | bytes 4423680 | tf_op jit(solution)/shard_map/all_gather | solution.py:543
  198.1 1.5 copy-start.12
  223.9 34.1 %all-to-all-start.6 = ((bf16[16,300,128]{2,1,0:T(8,128)(2,1)}), bf16[16,300,128]{2,1,0:T(8,128)(2,1)}, u32[]{:S(2)}, u32[]{:S(2)}) async-start(bf16[16,300,128]{2,1,0:T(8,128)(2,1)} %copy-done.4), calls=%async_computation.6 | async-start | bytes 2490368 | tf_op jit(solution)/shard_map/all_to_all | solution.py:547
  228.5 56.5 %all-gather.11.cloned.1.call-start = ((), (), s32[]{:S(2)}) async-start(), calls=%async_computation.11 | async-start | bytes 4423680 | tf_op jit(solution)/shard_map/all_gather | solution.py:543
  258.1 36.5 %all-to-all-start.5 = ((bf16[16,300,128]{2,1,0:T(8,128)(2,1)}), bf16[16,300,128]{2,1,0:T(8,128)(2,1)}, u32[]{:S(2)}, u32[]{:S(2)}) async-start(bf16[16,300,128]{2,1,0:T(8,128)(2,1)} %copy-done.5), calls=%async_computation.5 | async-start | bytes 2490368 | tf_op jit(solution)/shard_map/all_to_all | solution.py:547
  294.6 6.5 %copy-start.17 = (f32[256,128]{1,0:T(8,128)S(1)}, f32[256,128]{1,0:T(8,128)}, u32[]{:S(2)}) copy-start(f32[256,128]{1,0:T(8,128)} %constant.168.clone.refs_4_.refs_5_) | copy-start | bytes 393220
  294.6 35.7 %all-to-all-start.7 = ((bf16[16,300,128]{2,1,0:T(8,128)(2,1)}), bf16[16,300,128]{2,1,0:T(8,128)(2,1)S(1)}, u32[]{:S(2)}, u32[]{:S(2)}) async-start(bf16[16,300,128]{2,1,0:T(8,128)(2,1)} %copy-done.7), calls=%async_computation.7 | async-start | bytes 2490368 | tf_op jit(solution)/shard_map/all_to_all | solution.py:547
  302.6 27.7 %copy-start.9 = (bf16[256,256]{1,0:T(8,128)(2,1)S(1)}, bf16[256,256]{1,0:T(8,128)(2,1)}, u32[]{:S(2)}) copy-start(bf16[256,256]{1,0:T(8,128)(2,1)} %get-tuple-element.62.refs_7_.refs_6_) | copy-start | bytes 393220
  302.6 27.7 %copy-start.14 = (bf16[10,336,256]{2,1,0:T(8,128)(2,1)S(1)}, bf16[10,336,256]{2,1,0:T(8,128)(2,1)}, u32[]{:S(2)}) copy-start(bf16[10,336,256]{2,1,0:T(8,128)(2,1)} %copy-done.13) | copy-start | bytes 5160964
  (21 other events, 23.6 us)
Sparse Core Ops, SparseCore 0:
  43.1 42.3 all-gather.4
  87.0 42.7 all-gather.6
  198.2 42.4 all-gather.8
  242.1 42.7 all-gather.10

commit v2 on v1

--- a/solution.py
+++ b/solution.py
@@ -15,7 +15,7 @@
 LEV = 32
 STEPS = 2
 ROWS = 336
-ROWS_T = 384
+EACH = ROWS // 2
 DEPTH = 384
 VMEM_BYTES = 48 * 1024 * 1024
 BIG = 2.0**32
@@ -63,69 +63,63 @@
 
 
 def table_kernel(sz, wave_a, wave_b, start_a, start_b, cosines, table, table_t, rows_ref):
-    shape = (sz.pair_pad, sz.north)
-    wide = shape[1] // 128
+    wide = range(sz.north // 128)
     wa, wb = wave_a[...], wave_b[...]
     length = M - wa
-    x = cosines[...]
-    la, lb = start_a[...], start_b[...]
-
-    def spread(v):
-        return jnp.concatenate([v] * wide, axis=1)
+
+    def tile(ref, c):
+        return ref[:, c * 128 : (c + 1) * 128]
 
     def body(block, carry):
-        cur, prev, inv_prev, shift = carry
-        big = jnp.maximum(jnp.abs(cur), jnp.abs(prev)) > BIG
-        scale = jnp.where(big, 1.0 / BIG, 1.0)
-        cur, prev = cur * scale, prev * scale
-        shift = shift + jnp.where(big, 32.0, 0.0)
-        second = spread(((block * 8).astype(jnp.float32) > length).astype(jnp.float32)) > 0.5
-        base = jnp.exp2(0.5 * (jnp.where(second, lb, la) + shift))
-        base_b = jnp.exp2(0.5 * lb)
+        cur, prev, shift, inv_prev = carry
+        second = (block * 8).astype(jnp.float32) > length
+        cur, prev, shift, base, base_b = list(cur), list(prev), list(shift), [], []
+        for c in wide:
+            big = jnp.maximum(jnp.abs(cur[c]), jnp.abs(prev[c])) > BIG
+            scale = jnp.where(big, 1.0 / BIG, 1.0)
+            cur[c], prev[c] = cur[c] * scale, prev[c] * scale
+            shift[c] = shift[c] + jnp.where(big, 32.0, 0.0)
+            start = jnp.where(second, tile(start_b, c), tile(start_a, c))
+            base.append(jnp.exp2(0.5 * (start + shift[c])))
+            base_b.append(jnp.exp2(0.5 * tile(start_b, c)))
         for j in range(8):
             r = (block * 8 + j).astype(jnp.float32)
+            fresh = r == length
+            begin = jnp.logical_or(fresh, r == 0.0)
             in_b = r >= length
-            fresh = r == length
             m = jnp.where(in_b, wb, wa)
             k = jnp.where(in_b, r - length, r)
             n = m + k
-            den = k * (2.0 * m + k)
+            den = k * (m + n)
             num = 4.0 * n * n - 1.0
-            first = k < 0.5
-            safe_den = jnp.where(first, 1.0, den)
-            upper = jnp.where(first, 0.0, jnp.sqrt(num / safe_den))
-            inv = jnp.where(first, 0.0, jnp.sqrt(safe_den / jnp.where(first, 1.0, num)))
-            up_w = spread(upper)
-            lo_w = spread(upper * inv_prev)
-            new = up_w * x * cur - lo_w * prev
-            fresh_w = spread(fresh.astype(jnp.float32)) > 0.5
-            start = jnp.logical_or(fresh_w, r == 0.0)
-            new = jnp.where(start, 1.0, new)
-            prev = jnp.where(start, 0.0, cur)
-            shift = jnp.where(fresh_w, 0.0, shift)
-            base = jnp.where(fresh_w, base_b, base)
-            cur = new
-            inv_prev = inv
-            value = (cur * base) * base
-            for c in range(wide):
-                rows_ref[c, pl.ds(block * 8 + j, sz.pair_pad, stride=ROWS), :] = value[
-                    :, c * 128 : (c + 1) * 128
-                ]
-        return cur, prev, inv_prev, shift
-
-    zero = jnp.zeros(shape, jnp.float32)
-    lax.fori_loop(0, ROWS // 8, body, (zero, zero, jnp.zeros_like(wa), zero))
-    ridx = lax.broadcasted_iota(jnp.int32, (ROWS, sz.north), 0)
+            root = lax.rsqrt(jnp.maximum(num * den, 1.0))
+            upper = num * root
+            lower = upper * inv_prev
+            inv_prev = den * root
+            for c in wide:
+                new = upper * tile(cosines, c) * cur[c] - lower * prev[c]
+                prev[c] = cur[c]
+                cur[c] = jnp.where(begin, 1.0, new)
+                shift[c] = jnp.where(fresh, 0.0, shift[c])
+                base[c] = jnp.where(fresh, base_b[c], base[c])
+                at = (j % 2) * EACH + block * 4 + j // 2
+                rows_ref[c, pl.ds(at, sz.pair_pad, stride=ROWS), :] = (cur[c] * base[c]) * base[c]
+        return tuple(cur), tuple(prev), tuple(shift), inv_prev
+
+    zero = jnp.zeros((sz.pair_pad, 128), jnp.float32)
+    zeros = tuple(zero for _ in wide)
+    lax.fori_loop(0, ROWS // 8, body, (zeros, zeros, zeros, zero))
+    index = lax.broadcasted_iota(jnp.int32, (EACH, sz.north), 0)
+    blank = jnp.zeros((256 - EACH, sz.north), jnp.float32)
 
     def emit(i, _):
-        at = pl.multiple_of(i * ROWS, ROWS)
-        full = jnp.concatenate([rows_ref[c, pl.ds(at, ROWS), :] for c in range(wide)], axis=1)
-        full = jnp.where(ridx <= M, full, 0.0)
-        table[i] = full.astype(jnp.bfloat16)
-        padded = jnp.concatenate(
-            [full, jnp.zeros((ROWS_T - ROWS, sz.north), jnp.float32)], axis=0
-        )
-        table_t[i] = jnp.transpose(padded).astype(jnp.bfloat16)
+        for p in range(2):
+            at = i * ROWS + p * EACH
+            full = jnp.concatenate([rows_ref[c, pl.ds(at, EACH), :] for c in wide], axis=1)
+            full = jnp.where(2 * index + p <= M, full, 0.0)
+            table[i, p] = full.astype(jnp.bfloat16)
+            turned = jnp.transpose(jnp.concatenate([full, blank], axis=0))
+            table_t[i, p] = turned.astype(jnp.bfloat16)
         return 0
 
     lax.fori_loop(0, sz.pairs, emit, 0)
@@ -135,8 +129,8 @@
     return pl.pallas_call(
         lambda *refs: table_kernel(sz, *refs),
         out_shape=(
-            jax.ShapeDtypeStruct((sz.pairs, ROWS, sz.north), jnp.bfloat16),
-            jax.ShapeDtypeStruct((sz.pairs, sz.north, ROWS_T), jnp.bfloat16),
+            jax.ShapeDtypeStruct((sz.pairs, 2, EACH, sz.north), jnp.bfloat16),
+            jax.ShapeDtypeStruct((sz.pairs, 2, sz.north, 256), jnp.bfloat16),
         ),
         in_specs=vmem(5),
         out_specs=tuple(vmem(2)),
@@ -149,33 +143,37 @@
 def row_facts(waves, i, columns):
     wave_a, wave_b = waves[2 * i], waves[2 * i + 1]
     length = M - wave_a
-    r = lax.broadcasted_iota(jnp.int32, (ROWS, columns), 0)
+    q = lax.broadcasted_iota(jnp.int32, (ROWS, columns), 0)
+    r = jnp.where(q < EACH, 2 * q, 2 * (q - EACH) + 1)
     in_a = r < length
     k = jnp.where(in_a, r, r - length)
-    even = jnp.bitwise_and(k, 1) == 0
-    return wave_a, wave_b, length, r, in_a, k, even
+    odd = jnp.bitwise_and(length, 1).astype(jnp.float32)
+    sign_b = 1.0 - 2.0 * odd
+    return wave_a, wave_b, length, r, in_a, k, sign_b
 
 
 def send_rows(sz, part, i, state, facts, table_t, stage):
-    _, _, _, _, in_a, _, even = facts
-    zero = jnp.zeros_like(state)
-    in_b = jnp.logical_not(in_a)
-    odd = jnp.logical_not(even)
-    pieces = [
-        jnp.where(jnp.logical_and(side, sign), state, zero).astype(jnp.bfloat16)
-        for side in (in_a, in_b)
-        for sign in (even, odd)
-    ]
+    in_a, sign_b = facts[4], facts[6]
     columns = state.shape[1]
-    rhs = jnp.concatenate(pieces, axis=1)
-    rhs = jnp.concatenate([rhs, jnp.zeros((ROWS_T - ROWS, 4 * columns), jnp.bfloat16)], axis=0)
-    rows = table_t[i, part * sz.part_rows : (part + 1) * sz.part_rows, :]
-    out = jnp.dot(rows, rhs, preferred_element_type=jnp.float32)
+    rhs = jnp.concatenate(
+        [
+            jnp.where(in_a, state, 0.0).astype(jnp.bfloat16),
+            jnp.where(in_a, 0.0, state).astype(jnp.bfloat16),
+        ],
+        axis=1,
+    )
+    blank = jnp.zeros((256 - EACH, 2 * columns), jnp.bfloat16)
+    sums = []
+    for p in range(2):
+        rows = table_t[i, p, part * sz.part_rows : (part + 1) * sz.part_rows, :]
+        side = jnp.concatenate([rhs[p * EACH : (p + 1) * EACH], blank], axis=0)
+        sums.append(jnp.dot(rows, side, preferred_element_type=jnp.float32))
     size = sz.part_pad
+    plus, minus = sums[0] + sums[1], sums[0] - sums[1]
     for s in range(2):
-        e = out[:, (2 * s) * columns : (2 * s + 1) * columns]
-        o = out[:, (2 * s + 1) * columns : (2 * s + 2) * columns]
-        north, south = e + o, e - o
+        north = plus[:, s * columns : (s + 1) * columns]
+        south = minus[:, s * columns : (s + 1) * columns]
+        south = south * sign_b if s == 1 else south
         at = (2 * i + s) * sz.part_lats[part]
         for b in range(sz.half):
             lo = b * size
@@ -203,29 +201,35 @@
 
 
 def change_rows(sz, part, i, facts, table, weights, stage):
-    _, _, _, _, in_a, _, even = facts
-    pieces = []
+    in_a, sign_b = facts[4], facts[6]
     lo = part * sz.part_rows
     w = weights[lo : lo + sz.part_rows, :]
     size = sz.part_pad
+    plus, minus = [], []
     for s in range(2):
         at = (2 * i + s) * sz.part_lats[part]
         north = jnp.concatenate([stage[b, pl.ds(at, size), :] for b in range(sz.half)], axis=0)
         south = jnp.concatenate(
             [stage[sz.space - 1 - b, pl.ds(at, size), :] for b in range(sz.half)], axis=0
         )
-        pieces.append(((north + south) * w).astype(jnp.bfloat16))
-        pieces.append(((north - south) * w).astype(jnp.bfloat16))
-    rhs = jnp.concatenate(pieces, axis=1)
-    out = jnp.dot(table[i, :, lo : lo + sz.part_rows], rhs, preferred_element_type=jnp.float32)
-    c = out.shape[1] // 4
-    side_a = jnp.where(even, out[:, :c], out[:, c : 2 * c])
-    side_b = jnp.where(even, out[:, 2 * c : 3 * c], out[:, 3 * c :])
-    return jnp.where(in_a, side_a, side_b)
+        north, south = north * w, south * (w * sign_b if s == 1 else w)
+        plus.append((north + south).astype(jnp.bfloat16))
+        minus.append((north - south).astype(jnp.bfloat16))
+    pieces = []
+    for p, rows in enumerate((plus, minus)):
+        out = jnp.dot(
+            table[i, p, :, lo : lo + sz.part_rows],
+            jnp.concatenate(rows, axis=1),
+            preferred_element_type=jnp.float32,
+        )
+        c = out.shape[1] // 2
+        mine = in_a[p * EACH : (p + 1) * EACH]
+        pieces.append(jnp.where(mine, out[:, :c], out[:, c:]))
+    return jnp.concatenate(pieces, axis=0)
 
 
 def kept(state, facts):
-    wave_a, wave_b, _, r, in_a, _, _ = facts
+    wave_a, wave_b, _, r, in_a = facts[:5]
     columns = state.shape[1]
     imaginary = lax.broadcasted_iota(jnp.int32, state.shape, 1) >= columns // 2
     wave = jnp.where(in_a, wave_a, wave_b)
@@ -246,7 +250,7 @@
 
 
 def updated(state, change, facts, mixing, mixing_t, speeds):
-    wave_a, wave_b, _, _, in_a, k, _ = facts
+    wave_a, wave_b, _, _, in_a, k = facts[:6]
     combined = state + change
     projected = dot_split(combined, mixing[...])
     n = (jnp.where(in_a, wave_a, wave_b) + k).astype(jnp.float32)
@@ -256,17 +260,20 @@
     return kept(combined - returned, facts)
 
 
-def first_kernel(sz, waves, spectra, turn, table_t, state_ref, send, stage):
+def first_kernel(sz, waves, spectra, turn, table_t, state_ref, send, stage, mixed):
     columns = spectra.shape[2]
 
     def body(i, _):
         facts = row_facts(waves, i, columns)
-        length, in_a = facts[2], facts[4]
+        length = facts[2]
+        natural = lax.broadcasted_iota(jnp.int32, (ROWS, columns), 0)
         blank = jnp.zeros((ROWS - M, columns), jnp.float32)
         rows_a = jnp.concatenate([spectra[2 * i], blank], axis=0)
         rows_b = jnp.concatenate([spectra[2 * i + 1], blank], axis=0)
-        packed = jnp.where(in_a, rows_a, pltpu.roll(rows_b, length, 0))
-        state = kept(dot_split(packed, turn[...]), facts)
+        packed = jnp.where(natural < length, rows_a, pltpu.roll(rows_b, length, 0))
+        mixed[...] = dot_split(packed, turn[...])
+        state = jnp.concatenate([mixed[pl.ds(p, EACH, stride=2), :] for p in range(2)], axis=0)
+        state = kept(state, facts)
         state_ref[i] = state
         send_rows(sz, 0, i, state, facts, table_t, stage)
         return 0
@@ -317,7 +324,7 @@
 
 
 def last_kernel(
-    sz, waves, partial, recv, table, weights, mixing, mixing_t, speeds, turn_t, out, stage_in
+    sz, waves, partial, recv, table, weights, mixing, mixing_t, speeds, turn_t, out, stage_in, mixed
 ):
     columns = partial.shape[2]
     part = sz.parts - 1
@@ -325,10 +332,14 @@
 
     def body(i, _):
         facts = row_facts(waves, i, columns)
-        wave_a, wave_b, length, r = facts[:4]
+        wave_b, length = facts[1:3]
+        r = lax.broadcasted_iota(jnp.int32, (ROWS, columns), 0)
         change = change_rows(sz, part, i, facts, table, weights, stage_in)
         state = updated(partial[i], change, facts, mixing, mixing_t, speeds)
         state = dot_split(state, turn_t[...])
+        for p in range(2):
+            mixed[pl.ds(p, EACH, stride=2), :] = state[p * EACH : (p + 1) * EACH]
+        state = mixed[...]
         out[2 * i] = jnp.where(r < length, state, 0.0)[:M]
         rolled = pltpu.roll(state, ROWS - length, 0)
         out[2 * i + 1] = jnp.where(r < M - wave_b, rolled, 0.0)[:M]
@@ -535,13 +546,30 @@
             name=name,
         )(*args)
 
+    count = traj_wind.shape[1]
+    members = LEV // count
+    member = lax.axis_index("pert")
+
     def gather(step, part):
         local = jnp.concatenate([traj_wind[step][None], traj_state[step]], axis=0)
         start, size = sz.part_start[part], sz.part_lats[part]
         at = jnp.where(south, sz.lats - start - size, start)
         local = lax.dynamic_slice_in_dim(local, at, size, axis=2)
-        traj = lax.all_gather(local, "pert", axis=1, tiled=True)
-        return jnp.transpose(traj, (2, 0, 1, 3))
+        local = jnp.transpose(local, (2, 0, 1, 3))
+        pieces = [local]
+        for shift in range(1, members):
+            pieces.append(
+                lax.ppermute(
+                    local, "pert", [(i, (i - shift) % members) for i in range(members)]
+                )
+            )
+        placed = []
+        for place in range(members):
+            chosen = pieces[0]
+            for shift in range(1, members):
+                chosen = jnp.where((member + shift) % members == place, pieces[shift], chosen)
+            placed.append(chosen)
+        return jnp.concatenate(placed, axis=2)
 
     def transpose(value):
         return lax.all_to_all(value, "space", 0, 0, tiled=True)
@@ -554,17 +582,29 @@
 
     state, send_0 = call(
         lambda *refs: first_kernel(sz, *refs),
-        (state_shape, sends(0)), (waves, spectra, turn, table_t), [stages(0)], 8.0, "first_inverse",
+        (state_shape, sends(0)), (waves, spectra, turn, table_t),
+        [stages(0), pltpu.VMEM((ROWS, columns), jnp.float32)], 8.0, "first_inverse",
     )
+    traj = {(0, 0): gather(0, 0)}
     for step in range(STEPS):
         recv_0 = transpose(send_0)
-        recv_1 = transpose(inverse_rest(state))
-        back_0 = transpose(
-            grid_stage(sz, 0, flip, recv_0, gather(step, 0), synth, slope, scale)
-        )
-        back_1 = transpose(
-            grid_stage(sz, 1, flip, recv_1, gather(step, 1), synth, slope, scale)
-        )
+        send_1 = inverse_rest(state)
+        if step == 0:
+            traj[0, 1] = gather(0, 1)
+            send_1, traj[0, 0] = lax.optimization_barrier((send_1, traj[0, 0]))
+        recv_1 = transpose(send_1)
+        grid_0 = grid_stage(sz, 0, flip, recv_0, traj[step, 0], synth, slope, scale)
+        if step == 0:
+            traj[1, 0] = gather(1, 0)
+            grid_0, traj[0, 1] = lax.optimization_barrier((grid_0, traj[0, 1]))
+        back_0 = transpose(grid_0)
+        grid_1 = grid_stage(sz, 1, flip, recv_1, traj[step, 1], synth, slope, scale)
+        if step == 0:
+            traj[1, 1] = gather(1, 1)
+            grid_1, traj[1, 0] = lax.optimization_barrier((grid_1, traj[1, 0]))
+        back_1 = transpose(grid_1)
+        if step == 0:
+            back_0, traj[1, 1] = lax.optimization_barrier((back_0, traj[1, 1]))
         partial = call(
             lambda *refs: forward_kernel(sz, 0, *refs),
             state_shape, (waves, state, back_0, table, weights), [stages(0)], 6.0, "forward_part",
@@ -581,7 +621,7 @@
                 lambda *refs: last_kernel(sz, *refs),
                 jax.ShapeDtypeStruct(spectra.shape, jnp.float32),
                 (waves, partial, back_1, table, weights, mixing, mixing_t, speeds, turn_t),
-                [stages(1)], 10.0, "forward_last",
+                [stages(1), pltpu.VMEM((ROWS, columns), jnp.float32)], 10.0, "forward_last",
             )
     return out
 

time: 351 us -> 346 us (0.986)
  between operations: 13.5 us -> 0.36 us
  other arithmetic: 20.1 us -> 31.6 us
  starting transfers between devices: 43.1 us -> 48.1 us
  local copies, waits for them, and re-layouts: 36 us -> 31.3 us
  Pallas kernels: 87.5 us -> 82.9 us
    all_gather x4 -> x0, waiting for transfers between devices: 64.9 us -> none  [gather(): traj = lax.all_gather(local, 'pert', axis=1, tiled=True)]
    ppermute x0 -> x4, waiting for transfers between devices: none -> 49.2 us  [gather(): lax.ppermute(local, 'pert', [(i, (i - shift) % members) for i in range(me...]
    all_to_all x8, waiting for transfers between devices: 82.3 us -> 101 us  [transpose(): return lax.all_to_all(value, 'space', 0, 0, tiled=True)]
    select_n x0 -> x4, other arithmetic: none -> 8.04 us  [gather(): jnp.where((member + shift) % members == place, pieces[shift], chosen)]
    transpose x0 -> x2, other arithmetic: none -> 3.72 us  [gather(): local = jnp.transpose(local, (2, 0, 1, 3))]
    concatenate x2 -> x4, other arithmetic: 5.52 us -> 8.35 us  [gather(): return jnp.concatenate(placed, axis=2)]
  transfers between devices with their start and end apart: 12 -> 12, of which waited for: 10 -> 10; matrix products, arithmetic and copies ran while one was open for 8% -> 11% of each run, Pallas kernels for 15% -> 14%
where the time goes in v2:
time: 346 us; the launch traced here: 345 us
  waiting for transfers between devices  151 us (44%)
  Pallas kernels  82.9 us (24%)
  starting transfers between devices  48.1 us (14%)
  other arithmetic  31.6 us (9%)
  local copies, waits for them, and re-layouts  31.3 us (9%)
    all_to_all x8, waiting for transfers between devices, transpose(): return lax.all_to_all(value, 'space', 0, 0, tiled=True)  101 us
    ppermute x4, waiting for transfers between devices, gather(): lax.ppermute(local, 'pert', [(i, (i - shift) % members) for i in range(me...  49.2 us
    all_to_all x8, starting transfers between devices, transpose(): return lax.all_to_all(value, 'space', 0, 0, tiled=True)  46.2 us
    pallas_call x7, Pallas kernels, call(): pl.pallas_call(body, out_shape=out_shape, in_specs=smem(1) + vmem(len(arg...  42.3 us
    pallas_call x4, Pallas kernels, grid_stage(): pl.pallas_call(lambda *refs: grid_kernel(sz, part, *refs), out_shape=jax....  33.9 us
    unnamed x67, local copies, waits for them, and re-layouts  24.4 us
    concatenate x4, other arithmetic, gather(): return jnp.concatenate(placed, axis=2)  8.35 us
    select_n x4, other arithmetic, gather(): jnp.where((member + shift) % members == place, pieces[shift], chosen)  8.04 us
  transfers between devices with their start and end apart: 12, of which 10 were waited for; matrix products, arithmetic and copies ran while one was open for 11% of the time, Pallas kernels for 14%

profile of v2, /device:TPU:15, one launch (start us, length us, event | category | flops | bytes accessed | tf_op | source)
XLA Modules:
  0.0 344.8 jit_solution(1299567192635480461)
XLA Ops:
  2.6 6.6 %legendre_tables.1 = (bf16[10,2,168,256]{3,2,1,0:T(8,128)(2,1)S(1)}, bf16[10,2,256,256]{3,2,1,0:T(8,128)(2,1)S(1)}) custom-call(f32[16,128]{1,0:T(8,128)S(1)} %broadcast_in_dim.21.refs_0_, f32[16,128]{1,0:T(8,128)S(1)} %broadcast_in_dim.23.refs_1_, f32[16,256]{1,0:T(8,128)S(1)} %get-tuple-element.76.refs_2_, f32[16,256]{1,0:T(8,128)S(1)} %get-tuple-element.75.refs_3_, ...), custom_call_target="tpu_custom_call" | custom-call | tf_op jit(solution)/shard_map/legendre_tables/pallas_call | solution.py:129
  11.5 7.9 %first_inverse.1 = (f32[10,336,128]{2,1,0:T(8,128)S(1)}, bf16[16,300,128]{2,1,0:T(8,128)(2,1)}) custom-call(s32[20]{0:T(128)S(1)} %dynamic_slice.15.refs_0_, f32[20,320,128]{2,1,0:T(8,128)} %refs_1_.1, bf16[256,256]{1,0:T(8,128)(2,1)S(1)} %copy-done.20, bf16[10,2,256,256]{3,2,1,0:T(8,128)(2,1)S(1)} %get-tuple-element.31.refs_3_.refs_2_.refs_4_), custom_call_target="tpu_custom_call" | custom-call | flops 8000000000 | bytes 1048576 | tf_op jit(solution)/shard_map/first_inverse/pallas_call | solution.py:538
  19.4 6.6 %all-to-all-start = ((bf16[16,300,128]{2,1,0:T(8,128)(2,1)}), bf16[16,300,128]{2,1,0:T(8,128)(2,1)S(1)}, u32[]{:S(2)}, u32[]{:S(2)}) async-start(bf16[16,300,128]{2,1,0:T(8,128)(2,1)} %get-tuple-element.33), calls=%async_computation | async-start | bytes 2490368 | tf_op jit(solution)/shard_map/all_to_all | solution.py:575
  41.3 24.7 %collective-permute-done = bf16[15,3,16,960]{3,2,1,0:T(8,128)(2,1)} collective-permute-done((bf16[15,3,16,960]{3,2,1,0:T(8,128)(2,1)}, bf16[15,3,16,960]{3,2,1,0:T(8,128)(2,1)}, u32[]{:S(2)}, u32[]{:S(2)}) %collective-permute-start) | collective-permute-done | bytes 1382432 | tf_op jit(solution)/shard_map/ppermute | solution.py:562
  70.1 7.8 %all-to-all-start.2 = ((bf16[16,300,128]{2,1,0:T(8,128)(2,1)}), bf16[16,300,128]{2,1,0:T(8,128)(2,1)}, u32[]{:S(2)}, u32[]{:S(2)}) async-start(bf16[16,300,128]{2,1,0:T(8,128)(2,1)} %inverse_rest.2), calls=%async_computation.2 | async-start | bytes 2490368 | tf_op jit(solution)/shard_map/all_to_all | solution.py:575
  77.9 7.5 %multiply_convert_fusion.1 = (bf16[384,960]{1,0:T(8,128)(2,1)S(1)}, bf16[384,960]{1,0:T(8,128)(2,1)S(1)}, bf16[384,960]{1,0:T(8,128)(2,1)S(1)}, bf16[384,960]{1,0:T(8,128)(2,1)S(1)}) fusion(f32[384]{0:T(512)S(1)} %get-tuple-element.73, s32[384]{0:T(512)S(1)} %get-tuple-element.74, f32[384]{0:T(512)S(1)} %get-tuple-element.72), kind=kLoop, calls=%fused_computation.20 | loop fusion | flops 6635520 | bytes 2953728 | tf_op jit(solution)/shard_map/convert
  85.9 11.7 %collective-permute-done.1 = bf16[15,3,16,960]{3,2,1,0:T(8,128)(2,1)} collective-permute-done((bf16[15,3,16,960]{3,2,1,0:T(8,128)(2,1)}, bf16[15,3,16,960]{3,2,1,0:T(8,128)(2,1)}, u32[]{:S(2)}, u32[]{:S(2)}) %collective-permute-start.1) | collective-permute-done | bytes 1382432 | tf_op jit(solution)/shard_map/ppermute | solution.py:562
  102.0 8.2 %grid_stage.4 = bf16[16,300,128]{2,1,0:T(8,128)(2,1)S(1)} custom-call(s32[1]{0:T(128)} %bitcast.4.refs_0_, bf16[16,300,128]{2,1,0:T(8,128)(2,1)S(1)} %copy-done.1, bf16[15,3,32,960]{3,2,1,0:T(8,128)(2,1)} %pad_maximum_fusion.refs_2_, bf16[768,960]{1,0:T(8,128)(2,1)S(1)} %get-tuple-element.83.refs_3_, bf16[768,960]{1,0:T(8,128)(2,1)S(1)} %get-tuple-element.84.refs_4_, ...), custom_call_target="tpu_custom_call" | custom-call | flops 8999999488 | bytes 1048576 | tf_op jit(solution)/shard_map/grid_stage/pallas_call | solution.py:431
  111.2 7.7 %all-to-all-start.1 = ((bf16[16,300,128]{2,1,0:T(8,128)(2,1)}), bf16[16,300,128]{2,1,0:T(8,128)(2,1)}, u32[]{:S(2)}, u32[]{:S(2)}) async-start(bf16[16,300,128]{2,1,0:T(8,128)(2,1)} %copy-done.3), calls=%async_computation.1 | async-start | bytes 2490368 | tf_op jit(solution)/shard_map/all_to_all | solution.py:575
  119.1 10.1 %collective-permute-done.3 = bf16[15,3,16,960]{3,2,1,0:T(8,128)(2,1)} collective-permute-done((bf16[15,3,16,960]{3,2,1,0:T(8,128)(2,1)}, bf16[15,3,16,960]{3,2,1,0:T(8,128)(2,1)}, u32[]{:S(2)}, u32[]{:S(2)}) %collective-permute-start.3) | collective-permute-done | bytes 1382432 | tf_op jit(solution)/shard_map/ppermute | solution.py:562
  133.4 8.6 %grid_stage.5 = bf16[16,300,128]{2,1,0:T(8,128)(2,1)S(1)} custom-call(s32[1]{0:T(128)} %bitcast.4.refs_0_, bf16[16,300,128]{2,1,0:T(8,128)(2,1)} %all-to-all-done.2.refs_1_, bf16[15,3,32,960]{3,2,1,0:T(8,128)(2,1)} %pad_maximum_fusion.1.refs_2_, bf16[768,960]{1,0:T(8,128)(2,1)S(1)} %get-tuple-element.83.refs_3_, ...), custom_call_target="tpu_custom_call" | custom-call | flops 8999999488 | bytes 1048576 | tf_op jit(solution)/shard_map/grid_stage/pallas_call | solution.py:431
  143.0 5.5 %all-to-all-done.1.refs_2_ = bf16[16,300,128]{2,1,0:T(8,128)(2,1)} async-done(((bf16[16,300,128]{2,1,0:T(8,128)(2,1)}), bf16[16,300,128]{2,1,0:T(8,128)(2,1)}, u32[]{:S(2)}, u32[]{:S(2)}) %all-to-all-start.1) | async-done | bytes 1228832 | tf_op jit(solution)/shard_map/all_to_all | solution.py:575
  170.3 12.2 %all-to-all-done.3.refs_2_ = bf16[16,300,128]{2,1,0:T(8,128)(2,1)} async-done(((bf16[16,300,128]{2,1,0:T(8,128)(2,1)}), bf16[16,300,128]{2,1,0:T(8,128)(2,1)}, u32[]{:S(2)}, u32[]{:S(2)}) %all-to-all-start.3) | async-done | bytes 1228832 | tf_op jit(solution)/shard_map/all_to_all | solution.py:575
  184.3 10.1 %forward_inverse.1 = (f32[10,336,128]{2,1,0:T(8,128)S(1)}, bf16[16,300,128]{2,1,0:T(8,128)(2,1)S(1)}) custom-call(s32[20]{0:T(128)S(1)} %dynamic_slice.15.refs_0_, f32[10,336,128]{2,1,0:T(8,128)} %copy-done.28, bf16[16,300,128]{2,1,0:T(8,128)(2,1)} %all-to-all-done.3.refs_2_, bf16[10,2,168,256]{3,2,1,0:T(8,128)(2,1)} %copy-done.14, ...), custom_call_target="tpu_custom_call" | custom-call | flops 12000000000 | bytes 1048576 | tf_op jit(solution)/shard_map/forward_inverse/pallas_call | solution.py:538
  208.6 22.3 %all-to-all-done.4.refs_1_ = bf16[16,300,128]{2,1,0:T(8,128)(2,1)} async-done(((bf16[16,300,128]{2,1,0:T(8,128)(2,1)}), bf16[16,300,128]{2,1,0:T(8,128)(2,1)}, u32[]{:S(2)}, u32[]{:S(2)}) %all-to-all-start.4) | async-done | bytes 1228832 | tf_op jit(solution)/shard_map/all_to_all | solution.py:575
  230.8 4.9 %all-to-all-start.6 = ((bf16[16,300,128]{2,1,0:T(8,128)(2,1)}), bf16[16,300,128]{2,1,0:T(8,128)(2,1)}, u32[]{:S(2)}, u32[]{:S(2)}) async-start(bf16[16,300,128]{2,1,0:T(8,128)(2,1)} %copy-done.6), calls=%async_computation.6 | async-start | bytes 2490368 | tf_op jit(solution)/shard_map/all_to_all | solution.py:575
  235.7 8.6 %grid_stage.6 = bf16[16,300,128]{2,1,0:T(8,128)(2,1)S(1)} custom-call(s32[1]{0:T(128)} %bitcast.4.refs_0_, bf16[16,300,128]{2,1,0:T(8,128)(2,1)} %all-to-all-done.4.refs_1_, bf16[15,3,32,960]{3,2,1,0:T(8,128)(2,1)} %pad_maximum_fusion.3.refs_2_, bf16[768,960]{1,0:T(8,128)(2,1)S(1)} %get-tuple-element.83.refs_3_, ...), custom_call_target="tpu_custom_call" | custom-call | flops 8999999488 | bytes 1048576 | tf_op jit(solution)/shard_map/grid_stage/pallas_call | solution.py:431
  245.3 19.6 %all-to-all-done.6.refs_1_ = bf16[16,300,128]{2,1,0:T(8,128)(2,1)} async-done(((bf16[16,300,128]{2,1,0:T(8,128)(2,1)}), bf16[16,300,128]{2,1,0:T(8,128)(2,1)}, u32[]{:S(2)}, u32[]{:S(2)}) %all-to-all-start.6) | async-done | bytes 1228832 | tf_op jit(solution)/shard_map/all_to_all | solution.py:575
  265.0 4.9 %all-to-all-start.5 = ((bf16[16,300,128]{2,1,0:T(8,128)(2,1)}), bf16[16,300,128]{2,1,0:T(8,128)(2,1)}, u32[]{:S(2)}, u32[]{:S(2)}) async-start(bf16[16,300,128]{2,1,0:T(8,128)(2,1)} %copy-done.4), calls=%async_computation.5 | async-start | bytes 2490368 | tf_op jit(solution)/shard_map/all_to_all | solution.py:575
  269.8 8.6 %grid_stage.7 = bf16[16,300,128]{2,1,0:T(8,128)(2,1)S(1)} custom-call(s32[1]{0:T(128)} %bitcast.4.refs_0_, bf16[16,300,128]{2,1,0:T(8,128)(2,1)} %all-to-all-done.6.refs_1_, bf16[15,3,32,960]{3,2,1,0:T(8,128)(2,1)} %pad_maximum_fusion.2.refs_2_, bf16[768,960]{1,0:T(8,128)(2,1)S(1)} %get-tuple-element.83.refs_3_, ...), custom_call_target="tpu_custom_call" | custom-call | flops 8999999488 | bytes 1048576 | tf_op jit(solution)/shard_map/grid_stage/pallas_call | solution.py:431
  279.5 19.6 %all-to-all-done.5.refs_2_ = bf16[16,300,128]{2,1,0:T(8,128)(2,1)} async-done(((bf16[16,300,128]{2,1,0:T(8,128)(2,1)}), bf16[16,300,128]{2,1,0:T(8,128)(2,1)}, u32[]{:S(2)}, u32[]{:S(2)}) %all-to-all-start.5) | async-done | bytes 1228832 | tf_op jit(solution)/shard_map/all_to_all | solution.py:575
  299.1 4.9 %all-to-all-start.7 = ((bf16[16,300,128]{2,1,0:T(8,128)(2,1)}), bf16[16,300,128]{2,1,0:T(8,128)(2,1)S(1)}, u32[]{:S(2)}, u32[]{:S(2)}) async-start(bf16[16,300,128]{2,1,0:T(8,128)(2,1)} %copy-done.5), calls=%async_computation.7 | async-start | bytes 2490368 | tf_op jit(solution)/shard_map/all_to_all | solution.py:575
  310.9 22.2 %all-to-all-done.7.refs_2_ = bf16[16,300,128]{2,1,0:T(8,128)(2,1)S(1)} async-done(((bf16[16,300,128]{2,1,0:T(8,128)(2,1)}), bf16[16,300,128]{2,1,0:T(8,128)(2,1)S(1)}, u32[]{:S(2)}, u32[]{:S(2)}) %all-to-all-start.7) | async-done | bytes 1228832 | tf_op jit(solution)/shard_map/all_to_all | solution.py:575
  335.5 9.3 %forward_last.1 = f32[20,320,128]{2,1,0:T(8,128)} custom-call(s32[20]{0:T(128)S(1)} %dynamic_slice.15.refs_0_, f32[10,336,128]{2,1,0:T(8,128)S(1)} %copy-done.27, bf16[16,300,128]{2,1,0:T(8,128)(2,1)S(1)} %all-to-all-done.7.refs_2_, bf16[10,2,168,256]{3,2,1,0:T(8,128)(2,1)S(1)} %copy-done.15, f32[256,128]{1,0:T(8,128)S(1)} %copy-done.18, ...), custom_call_target="tpu_custom_call" | custom-call | flops 10000000000 | bytes 1048576 | tf_op jit(solution)/shard_map/forward_last/pallas_call | solution.py:538
  (114 shorter events, 84.5 us)
Async XLA Ops:
  10.5 9.0 %copy-start.11 = (bf16[10,2,256,256]{3,2,1,0:T(8,128)(2,1)}, bf16[10,2,256,256]{3,2,1,0:T(8,128)(2,1)S(1)}, u32[]{:S(2)}) copy-start(bf16[10,2,256,256]{3,2,1,0:T(8,128)(2,1)S(1)} %get-tuple-element.31.refs_3_.refs_2_.refs_4_) | copy-start | bytes 7864324
  19.4 16.3 %copy-start.21 = (f32[10,336,128]{2,1,0:T(8,128)}, f32[10,336,128]{2,1,0:T(8,128)S(1)}, u32[]{:S(2)}) copy-start(f32[10,336,128]{2,1,0:T(8,128)S(1)} %get-tuple-element.32.refs_1_) | copy-start | bytes 5160964
  19.4 50.7 %all-to-all-start = ((bf16[16,300,128]{2,1,0:T(8,128)(2,1)}), bf16[16,300,128]{2,1,0:T(8,128)(2,1)S(1)}, u32[]{:S(2)}, u32[]{:S(2)}) async-start(bf16[16,300,128]{2,1,0:T(8,128)(2,1)} %get-tuple-element.33), calls=%async_computation | async-start | bytes 2490368 | tf_op jit(solution)/shard_map/all_to_all | solution.py:575
  32.2 33.8 %collective-permute-start = (bf16[15,3,16,960]{3,2,1,0:T(8,128)(2,1)}, bf16[15,3,16,960]{3,2,1,0:T(8,128)(2,1)}, u32[]{:S(2)}, u32[]{:S(2)}) collective-permute-start(bf16[15,3,16,960]{3,2,1,0:T(8,128)(2,1)} %get-tuple-element.60), channel_id=1, source_target_pairs={{0,16},{16,0},{1,17},{17,1},{2,18},{18,2},{3,19},{19,3},{4,20},{20... | collective-permute-start | bytes 4147208 | tf_op jit(solution)/shard_map/ppermute | solution.py:562
  32.5 65.2 %collective-permute-start.1 = (bf16[15,3,16,960]{3,2,1,0:T(8,128)(2,1)}, bf16[15,3,16,960]{3,2,1,0:T(8,128)(2,1)}, u32[]{:S(2)}, u32[]{:S(2)}) collective-permute-start(bf16[15,3,16,960]{3,2,1,0:T(8,128)(2,1)} %get-tuple-element.59), channel_id=1, source_target_pairs={{0,16},{16,0},{1,17},{17,1},{2,18},{18,2},{3,19},{19,3},{4,20},{20... | collective-permute-start | bytes 4147208 | tf_op jit(solution)/shard_map/ppermute | solution.py:562
  35.6 93.7 %collective-permute-start.3 = (bf16[15,3,16,960]{3,2,1,0:T(8,128)(2,1)}, bf16[15,3,16,960]{3,2,1,0:T(8,128)(2,1)}, u32[]{:S(2)}, u32[]{:S(2)}) collective-permute-start(bf16[15,3,16,960]{3,2,1,0:T(8,128)(2,1)} %get-tuple-element.53), channel_id=1, source_target_pairs={{0,16},{16,0},{1,17},{17,1},{2,18},{18,2},{3,19},{19,3},{4,20},{20... | collective-permute-start | bytes 4147208 | tf_op jit(solution)/shard_map/ppermute | solution.py:562
  70.1 7.8 %copy-start.31 = (s32[320]{0:T(512)S(1)}, s32[320]{0:T(512)}, u32[]{:S(2)}) copy-start(s32[320]{0:T(512)} %param.15) | copy-start | bytes 3844
  70.1 15.4 %copy-start = (bf16[16,300,128]{2,1,0:T(8,128)(2,1)}, bf16[16,300,128]{2,1,0:T(8,128)(2,1)S(1)}, u32[]{:S(2)}) copy-start(bf16[16,300,128]{2,1,0:T(8,128)(2,1)S(1)} %all-to-all-done.refs_1_) | copy-start | bytes 3686404
  70.1 41.1 %all-to-all-start.2 = ((bf16[16,300,128]{2,1,0:T(8,128)(2,1)}), bf16[16,300,128]{2,1,0:T(8,128)(2,1)}, u32[]{:S(2)}, u32[]{:S(2)}) async-start(bf16[16,300,128]{2,1,0:T(8,128)(2,1)} %inverse_rest.2), calls=%async_computation.2 | async-start | bytes 2490368 | tf_op jit(solution)/shard_map/all_to_all | solution.py:575
  99.7 2.3 copy-start.1
  111.2 37.2 %all-to-all-start.1 = ((bf16[16,300,128]{2,1,0:T(8,128)(2,1)}), bf16[16,300,128]{2,1,0:T(8,128)(2,1)}, u32[]{:S(2)}, u32[]{:S(2)}) async-start(bf16[16,300,128]{2,1,0:T(8,128)(2,1)} %copy-done.3), calls=%async_computation.1 | async-start | bytes 2490368 | tf_op jit(solution)/shard_map/all_to_all | solution.py:575
  118.9 41.9 %collective-permute-start.2 = (bf16[15,3,16,960]{3,2,1,0:T(8,128)(2,1)}, bf16[15,3,16,960]{3,2,1,0:T(8,128)(2,1)}, u32[]{:S(2)}, u32[]{:S(2)}) collective-permute-start(bf16[15,3,16,960]{3,2,1,0:T(8,128)(2,1)} %get-tuple-element.54), channel_id=1, source_target_pairs={{0,16},{16,0},{1,17},{17,1},{2,18},{18,2},{3,19},{19,3},{4,20},{20... | collective-permute-start | bytes 4147208 | tf_op jit(solution)/shard_map/ppermute | solution.py:562
  143.0 10.2 %copy-start.30 = (f32[32,32]{1,0:T(8,128)S(1)}, f32[32,32]{1,0:T(8,128)}, u32[]{:S(2)}) copy-start(f32[32,32]{1,0:T(8,128)} %param.18) | copy-start | bytes 12292
  143.0 14.4 %copy-start.32 = (f32[32]{0:T(128)S(1)}, f32[32]{0:T(128)}, u32[]{:S(2)}) copy-start(f32[32]{0:T(128)} %param.19) | copy-start | bytes 388
  148.5 34.0 %all-to-all-start.3 = ((bf16[16,300,128]{2,1,0:T(8,128)(2,1)}), bf16[16,300,128]{2,1,0:T(8,128)(2,1)}, u32[]{:S(2)}, u32[]{:S(2)}) async-start(bf16[16,300,128]{2,1,0:T(8,128)(2,1)} %copy-done.2), calls=%async_computation.3 | async-start | bytes 2490368 | tf_op jit(solution)/shard_map/all_to_all | solution.py:575
  162.9 2.1 copy-start.16
  162.9 2.0 copy-start.22
  196.7 34.1 %all-to-all-start.4 = ((bf16[16,300,128]{2,1,0:T(8,128)(2,1)}), bf16[16,300,128]{2,1,0:T(8,128)(2,1)}, u32[]{:S(2)}, u32[]{:S(2)}) async-start(bf16[16,300,128]{2,1,0:T(8,128)(2,1)} %copy-done.7), calls=%async_computation.4 | async-start | bytes 2490368 | tf_op jit(solution)/shard_map/all_to_all | solution.py:575
  230.8 34.1 %all-to-all-start.6 = ((bf16[16,300,128]{2,1,0:T(8,128)(2,1)}), bf16[16,300,128]{2,1,0:T(8,128)(2,1)}, u32[]{:S(2)}, u32[]{:S(2)}) async-start(bf16[16,300,128]{2,1,0:T(8,128)(2,1)} %copy-done.6), calls=%async_computation.6 | async-start | bytes 2490368 | tf_op jit(solution)/shard_map/all_to_all | solution.py:575
  265.0 34.1 %all-to-all-start.5 = ((bf16[16,300,128]{2,1,0:T(8,128)(2,1)}), bf16[16,300,128]{2,1,0:T(8,128)(2,1)}, u32[]{:S(2)}, u32[]{:S(2)}) async-start(bf16[16,300,128]{2,1,0:T(8,128)(2,1)} %copy-done.4), calls=%async_computation.5 | async-start | bytes 2490368 | tf_op jit(solution)/shard_map/all_to_all | solution.py:575
  279.5 24.5 %copy-start.18 = (f32[256,128]{1,0:T(8,128)S(1)}, f32[256,128]{1,0:T(8,128)}, u32[]{:S(2)}) copy-start(f32[256,128]{1,0:T(8,128)} %constant.198.clone.refs_4_.refs_5_) | copy-start | bytes 393220
  299.1 34.0 %all-to-all-start.7 = ((bf16[16,300,128]{2,1,0:T(8,128)(2,1)}), bf16[16,300,128]{2,1,0:T(8,128)(2,1)S(1)}, u32[]{:S(2)}, u32[]{:S(2)}) async-start(bf16[16,300,128]{2,1,0:T(8,128)(2,1)} %copy-done.5), calls=%async_computation.7 | async-start | bytes 2490368 | tf_op jit(solution)/shard_map/all_to_all | solution.py:575
  305.4 27.7 %copy-start.9 = (bf16[256,256]{1,0:T(8,128)(2,1)S(1)}, bf16[256,256]{1,0:T(8,128)(2,1)}, u32[]{:S(2)}) copy-start(bf16[256,256]{1,0:T(8,128)(2,1)} %get-tuple-element.86.refs_7_.refs_6_) | copy-start | bytes 393220
  305.4 27.7 %copy-start.15 = (bf16[10,2,168,256]{3,2,1,0:T(8,128)(2,1)S(1)}, bf16[10,2,168,256]{3,2,1,0:T(8,128)(2,1)}, u32[]{:S(2)}) copy-start(bf16[10,2,168,256]{3,2,1,0:T(8,128)(2,1)} %copy-done.14) | copy-start | bytes 5160964
  (21 other events, 25.0 us)

commit v3 on v2

--- a/solution.py
+++ b/solution.py
@@ -16,6 +16,8 @@
 STEPS = 2
 ROWS = 336
 EACH = ROWS // 2
+SHIFTED = 2 * ROWS
+UNROLL = 5
 DEPTH = 384
 VMEM_BYTES = 48 * 1024 * 1024
 BIG = 2.0**32
@@ -26,7 +28,7 @@
 
 
 def cost(microseconds):
-    return pl.CostEstimate(flops=int(microseconds * 1.0e9), bytes_accessed=1 << 20, transcendentals=0)
+    return pl.CostEstimate(flops=int(microseconds * 30.0e9), bytes_accessed=1 << 20, transcendentals=0)
 
 
 def vmem(count):
@@ -45,10 +47,12 @@
         self.lats = NLAT // space
         self.half = space // 2
         self.parts = 2
-        self.part_pad = -(-self.lats // (8 * self.parts)) * 8
-        first = -(-self.lats // self.parts)
-        self.part_lats = [first, self.lats - first]
-        self.part_start = [0, first]
+        middle = self.lats // 2
+        middle += (self.lats - middle) % 2
+        edge = (self.lats - middle) // 2
+        self.ranges = [[(edge, middle)], [(0, edge), (self.lats - edge, edge)]]
+        self.part_lats = [middle, 2 * edge]
+        self.part_pad = -(-max(self.part_lats) // 8) * 8
         self.part_rows = self.half * self.part_pad
         self.north = self.parts * self.part_rows
         self.pair_pad = -(-self.pairs // 8) * 8
@@ -140,6 +144,17 @@
     )(wave_a, wave_b, log_a, log_b, cosines)
 
 
+def each_pair(sz, body):
+    step = max(d for d in range(1, UNROLL + 1) if sz.pairs % d == 0)
+
+    def several(g, carry):
+        for u in range(step):
+            body(g * step + u, u)
+        return carry
+
+    lax.fori_loop(0, sz.pairs // step, several, 0)
+
+
 def row_facts(waves, i, columns):
     wave_a, wave_b = waves[2 * i], waves[2 * i + 1]
     length = M - wave_a
@@ -260,47 +275,48 @@
     return kept(combined - returned, facts)
 
 
-def first_kernel(sz, waves, spectra, turn, table_t, state_ref, send, stage, mixed):
+def first_kernel(sz, waves, spectra, turn, table_t, state_ref, send, stage, shifted):
     columns = spectra.shape[2]
-
-    def body(i, _):
+    blank = jnp.zeros((EACH - M // 2, columns), jnp.float32)
+    shifted[...] = jnp.zeros_like(shifted)
+
+    def body(i, u):
         facts = row_facts(waves, i, columns)
-        length = facts[2]
-        natural = lax.broadcasted_iota(jnp.int32, (ROWS, columns), 0)
-        blank = jnp.zeros((ROWS - M, columns), jnp.float32)
-        rows_a = jnp.concatenate([spectra[2 * i], blank], axis=0)
-        rows_b = jnp.concatenate([spectra[2 * i + 1], blank], axis=0)
-        packed = jnp.where(natural < length, rows_a, pltpu.roll(rows_b, length, 0))
-        mixed[...] = dot_split(packed, turn[...])
-        state = jnp.concatenate([mixed[pl.ds(p, EACH, stride=2), :] for p in range(2)], axis=0)
+        length, in_a = facts[2], facts[4]
+        shifted[u, pl.ds(ROWS, M), :] = spectra[2 * i + 1]
+        rows = []
+        for p in range(2):
+            rows_a = jnp.concatenate(
+                [spectra[2 * i, pl.ds(p, M // 2, stride=2), :], blank], axis=0
+            )
+            rows_b = shifted[u, pl.ds(ROWS - length + p, EACH, stride=2), :]
+            rows.append(jnp.where(in_a[p * EACH : (p + 1) * EACH], rows_a, rows_b))
+        state = dot_split(jnp.concatenate(rows, axis=0), turn[...])
         state = kept(state, facts)
         state_ref[i] = state
         send_rows(sz, 0, i, state, facts, table_t, stage)
-        return 0
-
-    lax.fori_loop(0, sz.pairs, body, 0)
+
+    each_pair(sz, body)
     flush(sz, 0, stage, send)
 
 
 def inverse_kernel(sz, part, waves, state, table_t, send, stage):
-    def body(i, _):
+    def body(i, u):
         facts = row_facts(waves, i, state.shape[2])
         send_rows(sz, part, i, state[i], facts, table_t, stage)
-        return 0
-
-    lax.fori_loop(0, sz.pairs, body, 0)
+
+    each_pair(sz, body)
     flush(sz, part, stage, send)
 
 
 def forward_kernel(sz, part, waves, state, recv, table, weights, out, stage):
     load_rows(sz, part, recv, stage)
 
-    def body(i, _):
+    def body(i, u):
         facts = row_facts(waves, i, state.shape[2])
         out[i] = state[i] + change_rows(sz, part, i, facts, table, weights, stage)
-        return 0
-
-    lax.fori_loop(0, sz.pairs, body, 0)
+
+    each_pair(sz, body)
 
 
 def middle_kernel(
@@ -311,15 +327,14 @@
     part = sz.parts - 1
     load_rows(sz, part, recv, stage_in)
 
-    def body(i, _):
+    def body(i, u):
         facts = row_facts(waves, i, columns)
         change = change_rows(sz, part, i, facts, table, weights, stage_in)
         state = updated(partial[i], change, facts, mixing, mixing_t, speeds)
         state_out[i] = state
         send_rows(sz, 0, i, state, facts, table_t, stage)
-        return 0
-
-    lax.fori_loop(0, sz.pairs, body, 0)
+
+    each_pair(sz, body)
     flush(sz, 0, stage, send)
 
 
@@ -329,28 +344,32 @@
     columns = partial.shape[2]
     part = sz.parts - 1
     load_rows(sz, part, recv, stage_in)
-
-    def body(i, _):
+    mixed[...] = jnp.zeros_like(mixed)
+
+    def body(i, u):
         facts = row_facts(waves, i, columns)
         wave_b, length = facts[1:3]
-        r = lax.broadcasted_iota(jnp.int32, (ROWS, columns), 0)
+        r = lax.broadcasted_iota(jnp.int32, (M, columns), 0)
         change = change_rows(sz, part, i, facts, table, weights, stage_in)
         state = updated(partial[i], change, facts, mixing, mixing_t, speeds)
         state = dot_split(state, turn_t[...])
         for p in range(2):
-            mixed[pl.ds(p, EACH, stride=2), :] = state[p * EACH : (p + 1) * EACH]
-        state = mixed[...]
-        out[2 * i] = jnp.where(r < length, state, 0.0)[:M]
-        rolled = pltpu.roll(state, ROWS - length, 0)
-        out[2 * i + 1] = jnp.where(r < M - wave_b, rolled, 0.0)[:M]
-        return 0
-
-    lax.fori_loop(0, sz.pairs, body, 0)
-
-
-def grid_kernel(
-    sz, part, flip, recv, traj, synth, slope, scale, send, stage_in, stage, lhs, values, slopes, force
-):
+            mixed[u, pl.ds(p, EACH, stride=2), :] = state[p * EACH : (p + 1) * EACH]
+        out[2 * i] = jnp.where(r < length, mixed[u, :M, :], 0.0)
+        out[2 * i + 1] = jnp.where(r < M - wave_b, mixed[u, pl.ds(length, M), :], 0.0)
+
+    each_pair(sz, body)
+
+
+def grid_kernel(sz, part, members, place, recv, synth, slope, scale, *rest):
+    pieces, rest = rest[:members], rest[members:]
+    send, stage_in, stage, lhs, values, slopes, force, traj, sems = rest
+    south, member = place[0], place[1]
+    copies = [
+        pltpu.make_async_copy(piece, traj.at[i], sems.at[i]) for i, piece in enumerate(pieces)
+    ]
+    for copy in copies:
+        copy.start()
     lanes = recv.shape[2]
     rows = lanes // 2
     lats = sz.part_lats[part]
@@ -363,6 +382,18 @@
 
     lax.fori_loop(0, sz.space, load, 0)
     blank = jnp.zeros((DEPTH - M, lanes), jnp.float32)
+    for copy in copies:
+        copy.wait()
+
+    def levels(t, field):
+        mine = []
+        for block in range(members):
+            shift = lax.rem(block + members - member, members)
+            value = traj[0, t, field].astype(jnp.float32)
+            for i in range(1, members):
+                value = jnp.where(shift == i, traj[i, t, field].astype(jnp.float32), value)
+            mine.append(value)
+        return jnp.concatenate(mine, axis=0)
 
     def body(g, _):
         for q in range(sz.group):
@@ -376,11 +407,11 @@
         slopes[...] = jnp.dot(left, slope[...], preferred_element_type=jnp.float32)
         for q in range(sz.group):
             t = jnp.minimum(g * sz.group + q, lats - 1)
-            here = jnp.where(flip[0] == 1, lats - 1 - t, t)
-            wind = traj[here, 0].astype(jnp.float32)
+            here = jnp.where(south == 1, lats - 1 - t, t)
+            wind = levels(here, 0)
             for v in range(VARS):
                 lo = q * rows + v * LEV
-                other = traj[here, 1 + (v + 1) % VARS].astype(jnp.float32)
+                other = levels(here, 1 + (v + 1) % VARS)
                 force[lo : lo + LEV, :] = (
                     wind * slopes[lo : lo + LEV, :] + other * values[lo : lo + LEV, :]
                 ).astype(jnp.bfloat16)
@@ -424,14 +455,15 @@
     lax.fori_loop(0, sz.space, out, 0)
 
 
-def grid_stage(sz, part, flip, recv, traj, synth, slope, scale):
+def grid_stage(sz, part, place, recv, pieces, synth, slope, scale):
+    members = len(pieces)
     lanes = recv.shape[2]
     wide = sz.group * lanes // 2
     count = M * sz.part_lats[part]
     return pl.pallas_call(
-        lambda *refs: grid_kernel(sz, part, *refs),
+        lambda *refs: grid_kernel(sz, part, members, *refs),
         out_shape=jax.ShapeDtypeStruct(recv.shape, jnp.bfloat16),
-        in_specs=smem(1) + vmem(5),
+        in_specs=smem(1) + vmem(4) + [pl.BlockSpec(memory_space=pl.ANY)] * members,
         out_specs=vmem(1)[0],
         scratch_shapes=[
             pltpu.VMEM((count, lanes), jnp.float32),
@@ -440,11 +472,13 @@
             pltpu.VMEM((wide, NLON), jnp.float32),
             pltpu.VMEM((wide, NLON), jnp.float32),
             pltpu.VMEM((wide, NLON), jnp.bfloat16),
+            pltpu.VMEM((members,) + pieces[0].shape, jnp.bfloat16),
+            pltpu.SemaphoreType.DMA((members,)),
         ],
         compiler_params=params(),
         cost_estimate=cost(9.0),
         name="grid_stage",
-    )(flip, recv, traj, synth, slope, scale)
+    )(place, recv, synth, slope, scale, *pieces)
 
 
 def zonal_tables(wave_list):
@@ -492,11 +526,14 @@
     rank = lax.axis_index("space")
     waves = lax.dynamic_slice_in_dim(wave_order, rank * sz.slots, sz.slots)
 
-    place = np.arange(sz.north)
-    part, within = place // sz.part_rows, place % sz.part_rows
-    block, inner = within // sz.part_pad, within % sz.part_pad
-    real = inner < np.asarray(sz.part_lats)[part]
-    index = block * sz.lats + np.asarray(sz.part_start)[part] + inner
+    index, real = [], []
+    for ranges in sz.ranges:
+        within = np.concatenate([np.arange(lo, lo + size) for lo, size in ranges])
+        pad = sz.part_pad - within.size
+        for b in range(sz.half):
+            index.append(np.pad(b * sz.lats + within, (0, pad)))
+            real.append(np.pad(np.ones(within.size, bool), (0, pad)))
+    index, real = np.concatenate(index), np.concatenate(real)
     colat = np.where(real, (index + 0.5) * (math.pi / NLAT), math.pi / 2)
     cosines = jnp.asarray(np.cos(colat), jnp.float32)[None, :]
     log_sine = jnp.asarray(np.log(np.sin(colat)), jnp.float32)
@@ -521,8 +558,8 @@
     turn, turn_t = split_matrix(jnp.asarray(turn)), split_matrix(jnp.asarray(turn.T))
 
     synth, slope, scale = zonal_tables(wave_order)
-    south = rank >= sz.half
-    flip = jnp.where(south, 1, 0).astype(jnp.int32).reshape(1)
+    member = lax.axis_index("pert")
+    place = jnp.stack([jnp.where(rank >= sz.half, 1, 0), member]).astype(jnp.int32)
 
     def stages(part):
         return pltpu.VMEM((sz.space, sz.block_pad(part), columns), jnp.float32)
@@ -546,30 +583,24 @@
             name=name,
         )(*args)
 
-    count = traj_wind.shape[1]
-    members = LEV // count
-    member = lax.axis_index("pert")
-
-    def gather(step, part):
-        local = jnp.concatenate([traj_wind[step][None], traj_state[step]], axis=0)
-        start, size = sz.part_start[part], sz.part_lats[part]
-        at = jnp.where(south, sz.lats - start - size, start)
-        local = lax.dynamic_slice_in_dim(local, at, size, axis=2)
-        local = jnp.transpose(local, (2, 0, 1, 3))
-        pieces = [local]
-        for shift in range(1, members):
-            pieces.append(
-                lax.ppermute(
-                    local, "pert", [(i, (i - shift) % members) for i in range(members)]
-                )
-            )
-        placed = []
-        for place in range(members):
-            chosen = pieces[0]
-            for shift in range(1, members):
-                chosen = jnp.where((member + shift) % members == place, pieces[shift], chosen)
-            placed.append(chosen)
-        return jnp.concatenate(placed, axis=2)
+    members = LEV // traj_wind.shape[1]
+
+    def shared(value):
+        return [value] + [
+            lax.ppermute(value, "pert", [(i, (i - shift) % members) for i in range(members)])
+            for shift in range(1, members)
+        ]
+
+    def cut(step, part):
+        fields = [traj_wind[step][None], traj_state[step]]
+        local = jnp.concatenate(
+            [
+                jnp.concatenate([f[:, :, lo : lo + size] for f in fields], axis=0)
+                for lo, size in sz.ranges[part]
+            ],
+            axis=2,
+        )
+        return shared(jnp.transpose(local, (2, 0, 1, 3)))
 
     def transpose(value):
         return lax.all_to_all(value, "space", 0, 0, tiled=True)
@@ -580,31 +611,19 @@
             sends(1), (waves, state, table_t), [stages(1)], 6.0, "inverse_rest",
         )
 
+    traj = {(step, part): cut(step, part) for step in range(STEPS) for part in range(2)}
+
     state, send_0 = call(
         lambda *refs: first_kernel(sz, *refs),
         (state_shape, sends(0)), (waves, spectra, turn, table_t),
-        [stages(0), pltpu.VMEM((ROWS, columns), jnp.float32)], 8.0, "first_inverse",
+        [stages(0), pltpu.VMEM((UNROLL, SHIFTED, columns), jnp.float32)], 8.0, "first_inverse",
     )
-    traj = {(0, 0): gather(0, 0)}
+
     for step in range(STEPS):
         recv_0 = transpose(send_0)
-        send_1 = inverse_rest(state)
-        if step == 0:
-            traj[0, 1] = gather(0, 1)
-            send_1, traj[0, 0] = lax.optimization_barrier((send_1, traj[0, 0]))
-        recv_1 = transpose(send_1)
-        grid_0 = grid_stage(sz, 0, flip, recv_0, traj[step, 0], synth, slope, scale)
-        if step == 0:
-            traj[1, 0] = gather(1, 0)
-            grid_0, traj[0, 1] = lax.optimization_barrier((grid_0, traj[0, 1]))
-        back_0 = transpose(grid_0)
-        grid_1 = grid_stage(sz, 1, flip, recv_1, traj[step, 1], synth, slope, scale)
-        if step == 0:
-            traj[1, 1] = gather(1, 1)
-            grid_1, traj[1, 0] = lax.optimization_barrier((grid_1, traj[1, 0]))
-        back_1 = transpose(grid_1)
-        if step == 0:
-            back_0, traj[1, 1] = lax.optimization_barrier((back_0, traj[1, 1]))
+        recv_1 = transpose(inverse_rest(state))
+        back_0 = transpose(grid_stage(sz, 0, place, recv_0, traj[step, 0], synth, slope, scale))
+        back_1 = transpose(grid_stage(sz, 1, place, recv_1, traj[step, 1], synth, slope, scale))
         partial = call(
             lambda *refs: forward_kernel(sz, 0, *refs),
             state_shape, (waves, state, back_0, table, weights), [stages(0)], 6.0, "forward_part",
@@ -621,7 +640,7 @@
                 lambda *refs: last_kernel(sz, *refs),
                 jax.ShapeDtypeStruct(spectra.shape, jnp.float32),
                 (waves, partial, back_1, table, weights, mixing, mixing_t, speeds, turn_t),
-                [stages(1), pltpu.VMEM((ROWS, columns), jnp.float32)], 10.0, "forward_last",
+                [stages(1), pltpu.VMEM((UNROLL, SHIFTED, columns), jnp.float32)], 10.0, "forward_last",
             )
     return out
 

time: 346 us -> 312 us (0.902)
  other arithmetic: 31.6 us -> 14.8 us
  local copies, waits for them, and re-layouts: 31.3 us -> 21.4 us
  waiting for transfers between devices: 151 us -> 145 us
  starting transfers between devices: 48.1 us -> 42.6 us
    ppermute x4, waiting for transfers between devices: 49.2 us -> 11 us  [shared(): lax.ppermute(value, 'pert', [(i, (i - shift) % members) for i in range(me...]
    all_to_all x8, waiting for transfers between devices: 101 us -> 135 us  [transpose(): return lax.all_to_all(value, 'space', 0, 0, tiled=True)]
    pallas_call x4, Pallas kernels: 33.9 us -> 45 us  [grid_stage(): pl.pallas_call(lambda *refs: grid_kernel(sz, part, members, *refs), out_s...]
    pallas_call x7, Pallas kernels: 42.3 us -> 33.9 us  [call(): pl.pallas_call(body, out_shape=out_shape, in_specs=smem(1) + vmem(len(arg...]
    concatenate x4 -> x0, other arithmetic: 8.35 us -> none  [gather(): return jnp.concatenate(placed, axis=2)]
    unnamed x67 -> x70, local copies, waits for them, and re-layouts: 24.4 us -> 16.1 us
    select_n x4 -> x0, other arithmetic: 8.04 us -> none  [gather(): jnp.where((member + shift) % members == place, pieces[shift], chosen)]
    all_to_all x8, starting transfers between devices: 46.2 us -> 39.7 us  [transpose(): return lax.all_to_all(value, 'space', 0, 0, tiled=True)]
  transfers between devices with their start and end apart: 12 -> 12, of which waited for: 10 -> 10; matrix products, arithmetic and copies ran while one was open for 11% -> 6% of each run, Pallas kernels for 14% -> 21%
where the time goes in v3:
time: 312 us; the launch traced here: 310 us
  waiting for transfers between devices  145 us (46%)
  Pallas kernels  85.5 us (27%)
  starting transfers between devices  42.6 us (14%)
  local copies, waits for them, and re-layouts  21.4 us (7%)
  other arithmetic  14.8 us (5%)
    all_to_all x8, waiting for transfers between devices, transpose(): return lax.all_to_all(value, 'space', 0, 0, tiled=True)  135 us
    pallas_call x4, Pallas kernels, grid_stage(): pl.pallas_call(lambda *refs: grid_kernel(sz, part, members, *refs), out_s...  45 us
    all_to_all x8, starting transfers between devices, transpose(): return lax.all_to_all(value, 'space', 0, 0, tiled=True)  39.7 us
    pallas_call x7, Pallas kernels, call(): pl.pallas_call(body, out_shape=out_shape, in_specs=smem(1) + vmem(len(arg...  33.9 us
    unnamed x70, local copies, waits for them, and re-layouts  16.1 us
    ppermute x4, waiting for transfers between devices, shared(): lax.ppermute(value, 'pert', [(i, (i - shift) % members) for i in range(me...  11 us
    another operation x1, other arithmetic  7.49 us
    pallas_call x1, Pallas kernels, make_tables(): pl.pallas_call(lambda *refs: table_kernel(sz, *refs), out_shape=(jax.Shap...  6.61 us
  transfers between devices with their start and end apart: 12, of which 10 were waited for; matrix products, arithmetic and copies ran while one was open for 6% of the time, Pallas kernels for 21%

profile of v3, /device:TPU:15, one launch (start us, length us, event | category | flops | bytes accessed | tf_op | source)
XLA Modules:
  0.0 310.3 jit_solution(12347849945194979146)
XLA Ops:
  2.6 6.6 %legendre_tables.1 = (bf16[10,2,168,256]{3,2,1,0:T(8,128)(2,1)S(1)}, bf16[10,2,256,256]{3,2,1,0:T(8,128)(2,1)S(1)}) custom-call(f32[16,128]{1,0:T(8,128)S(1)} %broadcast_in_dim.21.refs_0_, f32[16,128]{1,0:T(8,128)S(1)} %broadcast_in_dim.23.refs_1_, f32[16,256]{1,0:T(8,128)S(1)} %get-tuple-element.56.refs_2_, f32[16,256]{1,0:T(8,128)S(1)} %get-tuple-element.55.refs_3_, ...), custom_call_target="tpu_custom_call" | custom-call | tf_op jit(solution)/shard_map/legendre_tables/pallas_call | solution.py:133
  10.4 6.4 %first_inverse.1 = (f32[10,336,128]{2,1,0:T(8,128)S(1)}, bf16[16,320,128]{2,1,0:T(8,128)(2,1)}) custom-call(s32[20]{0:T(128)S(1)} %dynamic_slice.3.refs_0_, f32[20,320,128]{2,1,0:T(8,128)} %refs_1_.1, bf16[256,256]{1,0:T(8,128)(2,1)S(1)} %copy-done.19, bf16[10,2,256,256]{3,2,1,0:T(8,128)(2,1)S(1)} %get-tuple-element.23.refs_3_.refs_2_.refs_4_), custom_call_target="tpu_custom_call" | custom-call | flops 240000008192 | bytes 1048576 | tf_op jit(solution)/shard_map/first_inverse/pallas_call | solution.py:575
  17.9 6.6 %all-to-all-start = ((bf16[16,320,128]{2,1,0:T(8,128)(2,1)}), bf16[16,320,128]{2,1,0:T(8,128)(2,1)}, u32[]{:S(2)}, u32[]{:S(2)}) async-start(bf16[16,320,128]{2,1,0:T(8,128)(2,1)} %get-tuple-element.25), calls=%async_computation | async-start | bytes 2621440 | tf_op jit(solution)/shard_map/all_to_all | solution.py:606
  41.8 7.5 %multiply_convert_fusion.1 = (bf16[384,960]{1,0:T(8,128)(2,1)S(1)}, bf16[384,960]{1,0:T(8,128)(2,1)S(1)}, bf16[384,960]{1,0:T(8,128)(2,1)S(1)}, bf16[384,960]{1,0:T(8,128)(2,1)S(1)}) fusion(f32[384]{0:T(512)S(1)} %get-tuple-element.53, s32[384]{0:T(512)S(1)} %get-tuple-element.54, f32[384]{0:T(512)S(1)} %get-tuple-element.52), kind=kLoop, calls=%fused_computation.10 | loop fusion | flops 6635520 | bytes 2953728 | tf_op jit(solution)/shard_map/convert
  49.8 5.6 %all-to-all-done.refs_1_ = bf16[16,320,128]{2,1,0:T(8,128)(2,1)} async-done(((bf16[16,320,128]{2,1,0:T(8,128)(2,1)}), bf16[16,320,128]{2,1,0:T(8,128)(2,1)}, u32[]{:S(2)}, u32[]{:S(2)}) %all-to-all-start) | async-done | bytes 1310752 | tf_op jit(solution)/shard_map/all_to_all | solution.py:606
  60.0 6.7 %collective-permute-done.refs_6_ = bf16[16,3,16,960]{3,2,1,0:T(8,128)(2,1)} collective-permute-done((bf16[16,3,16,960]{3,2,1,0:T(8,128)(2,1)}, bf16[16,3,16,960]{3,2,1,0:T(8,128)(2,1)}, u32[]{:S(2)}, u32[]{:S(2)}) %collective-permute-start) | collective-permute-done | bytes 1474592 | tf_op jit(solution)/shard_map/ppermute | solution.py:590
  66.9 10.8 %grid_stage.4 = bf16[16,320,128]{2,1,0:T(8,128)(2,1)S(1)} custom-call(s32[2]{0:T(128)S(1)} %pad_add_fusion.refs_0_, bf16[16,320,128]{2,1,0:T(8,128)(2,1)} %all-to-all-done.refs_1_, bf16[768,960]{1,0:T(8,128)(2,1)S(1)} %get-tuple-element.61.refs_2_, bf16[768,960]{1,0:T(8,128)(2,1)S(1)} %get-tuple-element.62.refs_3_, f32[320,128]{1,0:T(8,128)S(1)} %broadcast_in_dim.48.refs_4_, ...), custom_call_target="tpu_custom_call" | custom-call | flops 269999996928 | bytes 1048576 | tf_op jit(solution)/shard_map/grid_stage/pallas_call | solution.py:463
  78.8 8.6 %all-to-all-done.2.refs_1_ = bf16[16,280,128]{2,1,0:T(8,128)(2,1)} async-done(((bf16[16,280,128]{2,1,0:T(8,128)(2,1)}), bf16[16,280,128]{2,1,0:T(8,128)(2,1)}, u32[]{:S(2)}, u32[]{:S(2)}) %all-to-all-start.2) | async-done | bytes 1146912 | tf_op jit(solution)/shard_map/all_to_all | solution.py:606
  87.5 4.6 %all-to-all-start.1 = ((bf16[16,320,128]{2,1,0:T(8,128)(2,1)}), bf16[16,320,128]{2,1,0:T(8,128)(2,1)}, u32[]{:S(2)}, u32[]{:S(2)}) async-start(bf16[16,320,128]{2,1,0:T(8,128)(2,1)} %copy-done.4), calls=%async_computation.1 | async-start | bytes 2621440 | tf_op jit(solution)/shard_map/all_to_all | solution.py:606
  96.2 11.2 %grid_stage.5 = bf16[16,280,128]{2,1,0:T(8,128)(2,1)} custom-call(s32[2]{0:T(128)S(1)} %pad_add_fusion.refs_0_, bf16[16,280,128]{2,1,0:T(8,128)(2,1)} %all-to-all-done.2.refs_1_, bf16[768,960]{1,0:T(8,128)(2,1)} %copy-done, bf16[768,960]{1,0:T(8,128)(2,1)} %copy-done.2, f32[320,128]{1,0:T(8,128)S(1)} %broadcast_in_dim.48.refs_4_, ...), custom_call_target="tpu_custom_call" | custom-call | flops 269999996928 | bytes 1048576 | tf_op jit(solution)/shard_map/grid_stage/pallas_call | solution.py:463
  107.4 15.6 %all-to-all-done.1.refs_2_ = bf16[16,320,128]{2,1,0:T(8,128)(2,1)} async-done(((bf16[16,320,128]{2,1,0:T(8,128)(2,1)}), bf16[16,320,128]{2,1,0:T(8,128)(2,1)}, u32[]{:S(2)}, u32[]{:S(2)}) %all-to-all-start.1) | async-done | bytes 1310752 | tf_op jit(solution)/shard_map/all_to_all | solution.py:606
  131.8 23.2 %all-to-all-done.3.refs_2_ = bf16[16,280,128]{2,1,0:T(8,128)(2,1)} async-done(((bf16[16,280,128]{2,1,0:T(8,128)(2,1)}), bf16[16,280,128]{2,1,0:T(8,128)(2,1)}, u32[]{:S(2)}, u32[]{:S(2)}) %all-to-all-start.3) | async-done | bytes 1146912 | tf_op jit(solution)/shard_map/all_to_all | solution.py:606
  155.0 9.7 %forward_inverse.1 = (f32[10,336,128]{2,1,0:T(8,128)S(1)}, bf16[16,320,128]{2,1,0:T(8,128)(2,1)}) custom-call(s32[20]{0:T(128)S(1)} %copy-done.10, f32[10,336,128]{2,1,0:T(8,128)} %copy-done.28, bf16[16,280,128]{2,1,0:T(8,128)(2,1)} %all-to-all-done.3.refs_2_, bf16[10,2,168,256]{3,2,1,0:T(8,128)(2,1)} %copy-done.14, bf16[10,2,256,256]{3,2,1,0:T(8,128)(2,1)} %copy-done.12, ...), custom_call_target="tpu_custom_call" | custom-call | flops 359999995904 | bytes 1048576 | tf_op jit(solution)/shard_map/forward_inverse/pallas_call | solution.py:575
  165.9 4.8 %all-to-all-start.4 = ((bf16[16,320,128]{2,1,0:T(8,128)(2,1)}), bf16[16,320,128]{2,1,0:T(8,128)(2,1)}, u32[]{:S(2)}, u32[]{:S(2)}) async-start(bf16[16,320,128]{2,1,0:T(8,128)(2,1)} %get-tuple-element.28), calls=%async_computation.4 | async-start | bytes 2621440 | tf_op jit(solution)/shard_map/all_to_all | solution.py:606
  174.7 26.7 %all-to-all-done.4.refs_1_ = bf16[16,320,128]{2,1,0:T(8,128)(2,1)} async-done(((bf16[16,320,128]{2,1,0:T(8,128)(2,1)}), bf16[16,320,128]{2,1,0:T(8,128)(2,1)}, u32[]{:S(2)}, u32[]{:S(2)}) %all-to-all-start.4) | async-done | bytes 1310752 | tf_op jit(solution)/shard_map/all_to_all | solution.py:606
  201.4 4.9 %all-to-all-start.6 = ((bf16[16,280,128]{2,1,0:T(8,128)(2,1)}), bf16[16,280,128]{2,1,0:T(8,128)(2,1)}, u32[]{:S(2)}, u32[]{:S(2)}) async-start(bf16[16,280,128]{2,1,0:T(8,128)(2,1)} %inverse_rest.3), calls=%async_computation.6 | async-start | bytes 2293760 | tf_op jit(solution)/shard_map/all_to_all | solution.py:606
  207.7 11.8 %grid_stage.6 = bf16[16,320,128]{2,1,0:T(8,128)(2,1)} custom-call(s32[2]{0:T(128)S(1)} %pad_add_fusion.refs_0_, bf16[16,320,128]{2,1,0:T(8,128)(2,1)} %all-to-all-done.4.refs_1_, bf16[768,960]{1,0:T(8,128)(2,1)S(1)} %copy-done.1, bf16[768,960]{1,0:T(8,128)(2,1)S(1)} %copy-done.3, f32[320,128]{1,0:T(8,128)S(1)} %broadcast_in_dim.48.refs_4_, ...), custom_call_target="tpu_custom_call" | custom-call | flops 269999996928 | bytes 1048576 | tf_op jit(solution)/shard_map/grid_stage/pallas_call | solution.py:463
  219.5 13.9 %all-to-all-done.6.refs_1_ = bf16[16,280,128]{2,1,0:T(8,128)(2,1)} async-done(((bf16[16,280,128]{2,1,0:T(8,128)(2,1)}), bf16[16,280,128]{2,1,0:T(8,128)(2,1)}, u32[]{:S(2)}, u32[]{:S(2)}) %all-to-all-start.6) | async-done | bytes 1146912 | tf_op jit(solution)/shard_map/all_to_all | solution.py:606
  233.4 4.9 %all-to-all-start.5 = ((bf16[16,320,128]{2,1,0:T(8,128)(2,1)}), bf16[16,320,128]{2,1,0:T(8,128)(2,1)}, u32[]{:S(2)}, u32[]{:S(2)}) async-start(bf16[16,320,128]{2,1,0:T(8,128)(2,1)} %grid_stage.6), calls=%async_computation.5 | async-start | bytes 2621440 | tf_op jit(solution)/shard_map/all_to_all | solution.py:606
  238.3 11.2 %grid_stage.7 = bf16[16,280,128]{2,1,0:T(8,128)(2,1)} custom-call(s32[2]{0:T(128)S(1)} %pad_add_fusion.refs_0_, bf16[16,280,128]{2,1,0:T(8,128)(2,1)} %all-to-all-done.6.refs_1_, bf16[768,960]{1,0:T(8,128)(2,1)} %copy-done, bf16[768,960]{1,0:T(8,128)(2,1)} %copy-done.2, f32[320,128]{1,0:T(8,128)S(1)} %broadcast_in_dim.48.refs_4_, ...), custom_call_target="tpu_custom_call" | custom-call | flops 269999996928 | bytes 1048576 | tf_op jit(solution)/shard_map/grid_stage/pallas_call | solution.py:463
  249.5 19.5 %all-to-all-done.5.refs_2_ = bf16[16,320,128]{2,1,0:T(8,128)(2,1)} async-done(((bf16[16,320,128]{2,1,0:T(8,128)(2,1)}), bf16[16,320,128]{2,1,0:T(8,128)(2,1)}, u32[]{:S(2)}, u32[]{:S(2)}) %all-to-all-start.5) | async-done | bytes 1310752 | tf_op jit(solution)/shard_map/all_to_all | solution.py:606
  269.0 4.9 %all-to-all-start.7 = ((bf16[16,280,128]{2,1,0:T(8,128)(2,1)}), bf16[16,280,128]{2,1,0:T(8,128)(2,1)}, u32[]{:S(2)}, u32[]{:S(2)}) async-start(bf16[16,280,128]{2,1,0:T(8,128)(2,1)} %grid_stage.7), calls=%async_computation.7 | async-start | bytes 2293760 | tf_op jit(solution)/shard_map/all_to_all | solution.py:606
  279.6 21.4 %all-to-all-done.7.refs_2_ = bf16[16,280,128]{2,1,0:T(8,128)(2,1)} async-done(((bf16[16,280,128]{2,1,0:T(8,128)(2,1)}), bf16[16,280,128]{2,1,0:T(8,128)(2,1)}, u32[]{:S(2)}, u32[]{:S(2)}) %all-to-all-start.7) | async-done | bytes 1146912 | tf_op jit(solution)/shard_map/all_to_all | solution.py:606
  302.5 7.9 %forward_last.1 = f32[20,320,128]{2,1,0:T(8,128)} custom-call(s32[20]{0:T(128)S(1)} %copy-done.11, f32[10,336,128]{2,1,0:T(8,128)S(1)} %copy-done.27, bf16[16,280,128]{2,1,0:T(8,128)(2,1)} %all-to-all-done.7.refs_2_, bf16[10,2,168,256]{3,2,1,0:T(8,128)(2,1)S(1)} %copy-done.15, f32[256,128]{1,0:T(8,128)S(1)} %copy-done.17, ...), custom_call_target="tpu_custom_call" | custom-call | flops 299999985664 | bytes 1048576 | tf_op jit(solution)/shard_map/forward_last/pallas_call | solution.py:575
  (116 shorter events, 55.0 us)
Async XLA Ops:
  0.8 37.1 %copy-start.9 = (s32[20]{0:T(128)}, s32[20]{0:T(128)S(1)}, u32[]{:S(2)}) copy-start(s32[20]{0:T(128)S(1)} %dynamic_slice.3.refs_0_) | copy-start | bytes 244
  9.3 28.6 %copy-start.12 = (bf16[10,2,256,256]{3,2,1,0:T(8,128)(2,1)}, bf16[10,2,256,256]{3,2,1,0:T(8,128)(2,1)S(1)}, u32[]{:S(2)}) copy-start(bf16[10,2,256,256]{3,2,1,0:T(8,128)(2,1)S(1)} %get-tuple-element.23.refs_3_.refs_2_.refs_4_) | copy-start | bytes 7864324
  17.9 37.5 %all-to-all-start = ((bf16[16,320,128]{2,1,0:T(8,128)(2,1)}), bf16[16,320,128]{2,1,0:T(8,128)(2,1)}, u32[]{:S(2)}, u32[]{:S(2)}) async-start(bf16[16,320,128]{2,1,0:T(8,128)(2,1)} %get-tuple-element.25), calls=%async_computation | async-start | bytes 2621440 | tf_op jit(solution)/shard_map/all_to_all | solution.py:606
  30.8 35.9 %collective-permute-start = (bf16[16,3,16,960]{3,2,1,0:T(8,128)(2,1)}, bf16[16,3,16,960]{3,2,1,0:T(8,128)(2,1)}, u32[]{:S(2)}, u32[]{:S(2)}) collective-permute-start(bf16[16,3,16,960]{3,2,1,0:T(8,128)(2,1)} %maximum_bitcast_fusion.refs_5_), channel_id=1, source_target_pairs={{0,16},{16,0},{1,17},{17,1},{2,18},{18,2},{3,19},{19,3},{4,20},{20... | collective-permute-start | bytes 4423688 | tf_op jit(solution)/shard_map/ppermute | solution.py:590
  32.5 63.8 %collective-permute-start.1 = (bf16[14,3,16,960]{3,2,1,0:T(8,128)(2,1)}, bf16[14,3,16,960]{3,2,1,0:T(8,128)(2,1)}, u32[]{:S(2)}, u32[]{:S(2)}) collective-permute-start(bf16[14,3,16,960]{3,2,1,0:T(8,128)(2,1)} %maximum_bitcast_fusion.2.refs_5_), channel_id=1, source_target_pairs={{0,16},{16,0},{1,17},{17,1},{2,18},{18,2},{3,19},{19,3},{4,20},{20... | collective-permute-start | bytes 3870728 | tf_op jit(solution)/shard_map/ppermute | solution.py:590
  35.1 171.2 %collective-permute-start.2 = (bf16[16,3,16,960]{3,2,1,0:T(8,128)(2,1)}, bf16[16,3,16,960]{3,2,1,0:T(8,128)(2,1)}, u32[]{:S(2)}, u32[]{:S(2)}) collective-permute-start(bf16[16,3,16,960]{3,2,1,0:T(8,128)(2,1)} %maximum_bitcast_fusion.1.refs_5_), channel_id=1, source_target_pairs={{0,16},{16,0},{1,17},{17,1},{2,18},{18,2},{3,19},{19,3},{4,20},{20... | collective-permute-start | bytes 4423688 | tf_op jit(solution)/shard_map/ppermute | solution.py:590
  36.6 201.7 %collective-permute-start.3 = (bf16[14,3,16,960]{3,2,1,0:T(8,128)(2,1)}, bf16[14,3,16,960]{3,2,1,0:T(8,128)(2,1)}, u32[]{:S(2)}, u32[]{:S(2)}) collective-permute-start(bf16[14,3,16,960]{3,2,1,0:T(8,128)(2,1)} %maximum_bitcast_fusion.3.refs_5_), channel_id=1, source_target_pairs={{0,16},{16,0},{1,17},{17,1},{2,18},{18,2},{3,19},{19,3},{4,20},{20... | collective-permute-start | bytes 3870728 | tf_op jit(solution)/shard_map/ppermute | solution.py:590
  49.8 27.9 %copy-start = (bf16[768,960]{1,0:T(8,128)(2,1)}, bf16[768,960]{1,0:T(8,128)(2,1)S(1)}, u32[]{:S(2)}) copy-start(bf16[768,960]{1,0:T(8,128)(2,1)S(1)} %get-tuple-element.61.refs_2_) | copy-start | bytes 4423684
  49.8 27.9 %copy-start.2 = (bf16[768,960]{1,0:T(8,128)(2,1)}, bf16[768,960]{1,0:T(8,128)(2,1)S(1)}, u32[]{:S(2)}) copy-start(bf16[768,960]{1,0:T(8,128)(2,1)S(1)} %get-tuple-element.62.refs_3_) | copy-start | bytes 4423684
  55.4 32.0 %all-to-all-start.2 = ((bf16[16,280,128]{2,1,0:T(8,128)(2,1)}), bf16[16,280,128]{2,1,0:T(8,128)(2,1)}, u32[]{:S(2)}, u32[]{:S(2)}) async-start(bf16[16,280,128]{2,1,0:T(8,128)(2,1)} %copy-done.5), calls=%async_computation.2 | async-start | bytes 2293760 | tf_op jit(solution)/shard_map/all_to_all | solution.py:606
  87.5 35.5 %all-to-all-start.1 = ((bf16[16,320,128]{2,1,0:T(8,128)(2,1)}), bf16[16,320,128]{2,1,0:T(8,128)(2,1)}, u32[]{:S(2)}, u32[]{:S(2)}) async-start(bf16[16,320,128]{2,1,0:T(8,128)(2,1)} %copy-done.4), calls=%async_computation.1 | async-start | bytes 2621440 | tf_op jit(solution)/shard_map/all_to_all | solution.py:606
  107.4 20.2 %copy-start.10 = (s32[20]{0:T(128)S(1)}, s32[20]{0:T(128)}, u32[]{:S(2)}) copy-start(s32[20]{0:T(128)} %copy-done.9) | copy-start | bytes 244
  123.0 32.0 %all-to-all-start.3 = ((bf16[16,280,128]{2,1,0:T(8,128)(2,1)}), bf16[16,280,128]{2,1,0:T(8,128)(2,1)}, u32[]{:S(2)}, u32[]{:S(2)}) async-start(bf16[16,280,128]{2,1,0:T(8,128)(2,1)} %grid_stage.5), calls=%async_computation.3 | async-start | bytes 2293760 | tf_op jit(solution)/shard_map/all_to_all | solution.py:606
  127.6 27.4 %copy-start.6 = (bf16[256,256]{1,0:T(8,128)(2,1)S(1)}, bf16[256,256]{1,0:T(8,128)(2,1)}, u32[]{:S(2)}) copy-start(bf16[256,256]{1,0:T(8,128)(2,1)} %get-tuple-element.66.refs_7_.refs_6_) | copy-start | bytes 393220
  165.9 35.5 %all-to-all-start.4 = ((bf16[16,320,128]{2,1,0:T(8,128)(2,1)}), bf16[16,320,128]{2,1,0:T(8,128)(2,1)}, u32[]{:S(2)}, u32[]{:S(2)}) async-start(bf16[16,320,128]{2,1,0:T(8,128)(2,1)} %get-tuple-element.28), calls=%async_computation.4 | async-start | bytes 2621440 | tf_op jit(solution)/shard_map/all_to_all | solution.py:606
  174.7 31.6 %copy-start.1 = (bf16[768,960]{1,0:T(8,128)(2,1)S(1)}, bf16[768,960]{1,0:T(8,128)(2,1)}, u32[]{:S(2)}) copy-start(bf16[768,960]{1,0:T(8,128)(2,1)} %copy-done) | copy-start | bytes 4423684
  201.4 32.0 %all-to-all-start.6 = ((bf16[16,280,128]{2,1,0:T(8,128)(2,1)}), bf16[16,280,128]{2,1,0:T(8,128)(2,1)}, u32[]{:S(2)}, u32[]{:S(2)}) async-start(bf16[16,280,128]{2,1,0:T(8,128)(2,1)} %inverse_rest.3), calls=%async_computation.6 | async-start | bytes 2293760 | tf_op jit(solution)/shard_map/all_to_all | solution.py:606
  233.4 35.5 %all-to-all-start.5 = ((bf16[16,320,128]{2,1,0:T(8,128)(2,1)}), bf16[16,320,128]{2,1,0:T(8,128)(2,1)}, u32[]{:S(2)}, u32[]{:S(2)}) async-start(bf16[16,320,128]{2,1,0:T(8,128)(2,1)} %grid_stage.6), calls=%async_computation.5 | async-start | bytes 2621440 | tf_op jit(solution)/shard_map/all_to_all | solution.py:606
  249.5 24.4 %copy-start.11 = (s32[20]{0:T(128)S(1)}, s32[20]{0:T(128)}, u32[]{:S(2)}) copy-start(s32[20]{0:T(128)} %copy-done.9) | copy-start | bytes 244
  249.5 24.4 %copy-start.17 = (f32[256,128]{1,0:T(8,128)S(1)}, f32[256,128]{1,0:T(8,128)}, u32[]{:S(2)}) copy-start(f32[256,128]{1,0:T(8,128)} %constant.168.clone.refs_4_.refs_5_) | copy-start | bytes 393220
  269.0 32.0 %all-to-all-start.7 = ((bf16[16,280,128]{2,1,0:T(8,128)(2,1)}), bf16[16,280,128]{2,1,0:T(8,128)(2,1)}, u32[]{:S(2)}, u32[]{:S(2)}) async-start(bf16[16,280,128]{2,1,0:T(8,128)(2,1)} %grid_stage.7), calls=%async_computation.7 | async-start | bytes 2293760 | tf_op jit(solution)/shard_map/all_to_all | solution.py:606
  275.3 25.7 %copy-start.7 = (bf16[256,256]{1,0:T(8,128)(2,1)S(1)}, bf16[256,256]{1,0:T(8,128)(2,1)}, u32[]{:S(2)}) copy-start(bf16[256,256]{1,0:T(8,128)(2,1)} %get-tuple-element.66.refs_7_.refs_6_) | copy-start | bytes 393220
  275.3 25.7 %copy-start.15 = (bf16[10,2,168,256]{3,2,1,0:T(8,128)(2,1)S(1)}, bf16[10,2,168,256]{3,2,1,0:T(8,128)(2,1)}, u32[]{:S(2)}) copy-start(bf16[10,2,168,256]{3,2,1,0:T(8,128)(2,1)} %copy-done.14) | copy-start | bytes 5160964
  275.3 25.7 %copy-start.18 = (bf16[256,256]{1,0:T(8,128)(2,1)S(1)}, bf16[256,256]{1,0:T(8,128)(2,1)}, u32[]{:S(2)}) copy-start(bf16[256,256]{1,0:T(8,128)(2,1)} %constant.201.refs_8_) | copy-start | bytes 393220
  (22 other events, 82.3 us)

commit v4 on v3

v4 whole, which is shorter than its diff:
```python
import math

import jax
import jax.numpy as jnp
import numpy as np
from jax import lax
from jax.experimental import pallas as pl
from jax.experimental.pallas import tpu as pltpu
from jax.sharding import PartitionSpec as P

NLAT = 480
NLON = 960
M = 320
VARS = 2
LEV = 32
STEPS = 2
ROWS = 336
EACH = ROWS // 2
SHIFTED = 2 * ROWS
UNROLL = 5
DEPTH = 384
VMEM_BYTES = 48 * 1024 * 1024
VMEM_ALONE = 60 * 1024 * 1024
BIG = 2.0**32


def params(limit=VMEM_BYTES):
    return pltpu.CompilerParams(vmem_limit_bytes=limit)


def cost(microseconds):
    return pl.CostEstimate(flops=int(microseconds * 30.0e9), bytes_accessed=1 << 20, transcendentals=0)


def vmem(count):
    return [pl.BlockSpec(memory_space=pltpu.VMEM)] * count


def smem(count):
    return [pl.BlockSpec(memory_space=pltpu.SMEM)] * count


class Sizes:
    def __init__(self, space):
        self.space = space
        self.slots = M // space
        self.pairs = self.slots // 2
        self.lats = NLAT // space
        self.half = space // 2
        self.parts = 2
        middle = self.lats // 2
        middle += (self.lats - middle) % 2
        edge = (self.lats - middle) // 2
        self.ranges = [[(edge, middle)], [(0, edge), (self.lats - edge, edge)]]
        self.part_lats = [middle, 2 * edge]
        self.part_pad = -(-max(self.part_lats) // 8) * 8
        self.part_rows = self.half * self.part_pad
        self.north = self.parts * self.part_rows
        self.pair_pad = -(-self.pairs // 8) * 8
        self.group = 8
        self.step = max(d for d in range(1, UNROLL + 1) if self.pairs % d == 0)
        self.loops = self.pairs // self.step
        self.bundle = space // 4 if space % 4 == 0 else space
        self.bundles = space // self.bundle

    def block(self, part):
        return self.slots * self.part_lats[part]

    def block_pad(self, part):
        last = (self.slots - 1) * self.part_lats[part] + self.part_pad
        return -(-last // 8) * 8


def sectoral_logs():
    ratios = [0.5 * math.log2((2.0 * i + 1.0) / (2.0 * i)) for i in range(1, M)]
    return np.concatenate([[-0.5], -0.5 + np.cumsum(ratios)]).astype(np.float32)


def build_tables(sz, part, waves, logs, angles, table, table_t, rows_ref):
    cosines, log_sines = angles[2 * part : 2 * part + 1, :], angles[2 * part + 1 : 2 * part + 2, :]
    base = lax.axis_index("space") * sz.slots
    shape = (sz.pair_pad, 128)
    zero = jnp.zeros(shape, jnp.float32)
    size = sz.pair_pad
    rows_ref[: 4 * size, :] = jnp.zeros((4 * size, 128), jnp.float32)
    for i in range(sz.pairs):
        wave_a, wave_b = waves[base + 2 * i], waves[base + 2 * i + 1]
        facts = (wave_a.astype(jnp.float32), wave_b.astype(jnp.float32), logs[wave_a // 128, wave_a % 128], logs[wave_b // 128, wave_b % 128])
        for j, fact in enumerate(facts):
            rows_ref[j * size + i : j * size + i + 1, :] = jnp.full((1, 128), fact, jnp.float32)
    wa, wb, ca, cb = (rows_ref[j * size : (j + 1) * size, :] for j in range(4))
    length = M - wa
    start_a = ca + wa * log_sines
    start_b = cb + wb * log_sines
    base_b = jnp.exp2(0.5 * start_b)
    x = jnp.broadcast_to(cosines, shape)

    def body(block, carry):
        cur, prev, shift, inv_prev = carry
        second = (block * 8).astype(jnp.float32) > length
        big = jnp.maximum(jnp.abs(cur), jnp.abs(prev)) > BIG
        scale = jnp.where(big, 1.0 / BIG, 1.0)
        cur, prev = cur * scale, prev * scale
        shift = shift + jnp.where(big, 32.0, 0.0)
        factor = jnp.exp2(0.5 * (jnp.where(second, start_b, start_a) + shift))
        for j in range(8):
            r = (block * 8 + j).astype(jnp.float32)
            fresh = r == length
            begin = jnp.logical_or(fresh, r == 0.0)
            in_b = r >= length
            m = jnp.where(in_b, wb, wa)
            k = jnp.where(in_b, r - length, r)
            n = m + k
            den = k * (m + n)
            num = 4.0 * n * n - 1.0
            root = lax.rsqrt(jnp.maximum(num * den, 1.0))
            upper = num * root
            lower = upper * inv_prev
            inv_prev = den * root
            new = upper * x * cur - lower * prev
            prev = cur
            cur = jnp.where(begin, 1.0, new)
            shift = jnp.where(fresh, 0.0, shift)
            factor = jnp.where(fresh, base_b, factor)
            at = (j % 2) * EACH + block * 4 + j // 2
            rows_ref[pl.ds(at, sz.pair_pad, stride=ROWS), :] = (cur * factor) * factor
        return cur, prev, shift, inv_prev

    lax.fori_loop(0, ROWS // 8, body, (zero, zero, zero, zero))
    index = lax.broadcasted_iota(jnp.int32, (EACH, 128), 0)
    blank = jnp.zeros((256 - EACH, 128), jnp.float32)

    def emit(i, u):
        for p in range(2):
            full = rows_ref[pl.ds(i * ROWS + p * EACH, EACH), :]
            full = jnp.where(2 * index + p <= M, full, 0.0)
            table[i, p] = full.astype(jnp.bfloat16)
            turned = jnp.transpose(jnp.concatenate([full, blank], axis=0))
            table_t[i, p] = turned.astype(jnp.bfloat16)

    each_pair(sz, emit)


def table_shapes(sz):
    return [(sz.pairs, 2, EACH, 128), (sz.pairs, 2, 128, 256)]


def move(source, target, sem):
    copy = pltpu.make_async_copy(source, target, sem)
    copy.start()
    return copy


def each_pair(sz, body, done=None):
    def several(g, carry):
        for u in range(sz.step):
            body(g * sz.step + u, u)
        if done is not None:
            done(g)
        return carry

    lax.fori_loop(0, sz.pairs // sz.step, several, 0)


def group_copy(source, target, sems, g, size):
    rows = pl.ds(g * size, size)
    return pltpu.make_async_copy(source.at[rows], target.at[rows], sems.at[g])


def row_facts(sz, waves, i, columns):
    base = lax.axis_index("space") * sz.slots
    wave_a, wave_b = waves[base + 2 * i], waves[base + 2 * i + 1]
    length = M - wave_a
    q = lax.broadcasted_iota(jnp.int32, (ROWS, columns), 0)
    r = jnp.where(q < EACH, 2 * q, 2 * (q - EACH) + 1)
    in_a = r < length
    k = jnp.where(in_a, r, r - length)
    odd = jnp.bitwise_and(length, 1).astype(jnp.float32)
    sign_b = 1.0 - 2.0 * odd
    return wave_a, wave_b, length, r, in_a, k, sign_b


def send_rows(sz, part, i, state, facts, table_t, stage):
    in_a, sign_b = facts[4], facts[6]
    columns = state.shape[1]
    rhs = jnp.concatenate(
        [
            jnp.where(in_a, state, 0.0).astype(jnp.bfloat16),
            jnp.where(in_a, 0.0, state).astype(jnp.bfloat16),
        ],
        axis=1,
    )
    blank = jnp.zeros((256 - EACH, 2 * columns), jnp.bfloat16)
    sums = []
    for p in range(2):
        rows = table_t[i, p]
        side = jnp.concatenate([rhs[p * EACH : (p + 1) * EACH], blank], axis=0)
        sums.append(jnp.dot(rows, side, preferred_element_type=jnp.float32))
    size = sz.part_pad
    plus, minus = sums[0] + sums[1], sums[0] - sums[1]
    for s in range(2):
        north = plus[:, s * columns : (s + 1) * columns]
        south = minus[:, s * columns : (s + 1) * columns]
        south = south * sign_b if s == 1 else south
        at = (2 * i + s) * sz.part_lats[part]
        for b in range(sz.half):
            lo = b * size
            stage[b, pl.ds(at, size), :] = north[lo : lo + size]
            stage[sz.space - 1 - b, pl.ds(at, size), :] = south[lo : lo + size]


def flush(sz, part, stage, send, target=None, sems=None):
    def body(g, _):
        for o in range(sz.bundle):
            d = g * sz.bundle + o
            send[d] = stage[d, : sz.block(part), :].astype(jnp.bfloat16)
        if target is not None:
            group_copy(send, target, sems, g, sz.bundle).start()
        return 0

    lax.fori_loop(0, sz.bundles, body, 0)
    if target is not None:
        for g in range(sz.bundles):
            group_copy(send, target, sems, g, sz.bundle).wait()


def load_rows(sz, part, recv, stage, source=None, sems=None):
    rows = sz.block_pad(part)
    if source is not None:
        for g in range(sz.bundles):
            group_copy(source, recv, sems, g, sz.bundle).start()

    def body(g, _):
        if source is not None:
            group_copy(source, recv, sems, g, sz.bundle).wait()
        for o in range(sz.bundle):
            d = g * sz.bundle + o
            stage[d, rows - 16 : rows, :] = jnp.zeros((16, stage.shape[2]), jnp.float32)
            stage[d, : sz.block(part), :] = recv[d].astype(jnp.float32)
        return 0

    lax.fori_loop(0, sz.bundles, body, 0)


def change_rows(sz, part, i, facts, table, weights, stage):
    in_a, sign_b = facts[4], facts[6]
    w = weights[...]
    size = sz.part_pad
    plus, minus = [], []
    for s in range(2):
        at = (2 * i + s) * sz.part_lats[part]
        north = jnp.concatenate([stage[b, pl.ds(at, size), :] for b in range(sz.half)], axis=0)
        south = jnp.concatenate(
            [stage[sz.space - 1 - b, pl.ds(at, size), :] for b in range(sz.half)], axis=0
        )
        north, south = north * w, south * (w * sign_b if s == 1 else w)
        plus.append((north + south).astype(jnp.bfloat16))
        minus.append((north - south).astype(jnp.bfloat16))
    pieces = []
    for p, rows in enumerate((plus, minus)):
        out = jnp.dot(
            table[i, p],
            jnp.concatenate(rows, axis=1),
            preferred_element_type=jnp.float32,
        )
        c = out.shape[1] // 2
        mine = in_a[p * EACH : (p + 1) * EACH]
        pieces.append(jnp.where(mine, out[:, :c], out[:, c:]))
    return jnp.concatenate(pieces, axis=0)


def kept(state, facts):
    wave_a, wave_b, _, r, in_a = facts[:5]
    columns = state.shape[1]
    imaginary = lax.broadcasted_iota(jnp.int32, state.shape, 1) >= columns // 2
    wave = jnp.where(in_a, wave_a, wave_b)
    dropped = jnp.logical_or(jnp.logical_and(wave == 0, imaginary), r > M)
    return jnp.where(dropped, 0.0, state)


def turn_matrix(columns, back=False):
    shape = (2 * columns, 2 * columns)
    r = lax.broadcasted_iota(jnp.int32, shape, 0)
    c = lax.broadcasted_iota(jnp.int32, shape, 1)
    r = jnp.where(r < columns, r, r - columns)
    old, new = (c, r) if back else (r, c)
    target = jnp.bitwise_and(old, 1) * (columns // 2) + jnp.right_shift(old, 1)
    match = jnp.logical_and(target == new, c < columns)
    return jnp.where(match, 1.0, 0.0).astype(jnp.bfloat16)


def halves(x):
    high = x.astype(jnp.bfloat16)
    low = (x - high.astype(jnp.float32)).astype(jnp.bfloat16)
    return jnp.concatenate([high, low], axis=1)


def dot_split(x, both):
    out = jnp.dot(halves(x), both, preferred_element_type=jnp.float32)
    c = out.shape[1] // 2
    return out[:, :c] + out[:, c:]


def updated(state, change, facts, mixing, mixing_t, speeds):
    wave_a, wave_b, _, _, in_a, k = facts[:6]
    combined = state + change
    projected = dot_split(combined, mixing[...])
    n = (jnp.where(in_a, wave_a, wave_b) + k).astype(jnp.float32)
    stiffness = speeds[...] * (n * (n + 1.0))
    weighted = projected * (stiffness / (1.0 + stiffness))
    returned = dot_split(weighted, mixing_t[...])
    return kept(combined - returned, facts)


def first_kernel(
    sz, waves_hbm, angles_hbm, spectra_hbm,
    table_hbm, table_t_hbm, state_hbm, send_hbm,
    waves, logs, angles, spectra, table, table_t, state_ref, send, stage, shifted, rows_ref, one, state_sems, send_sems,
):
    columns = spectra.shape[2]
    blank = jnp.zeros((EACH - M // 2, columns), jnp.float32)
    facts = [
        move(waves_hbm, waves, one.at[3]),
        move(angles_hbm.at[8:16], logs, one.at[4]),
        move(angles_hbm.at[0:8], angles, one.at[5]),
    ]
    arriving = move(spectra_hbm, spectra, one.at[0])
    turn = turn_matrix(columns)
    shifted[...] = jnp.zeros_like(shifted)
    for copy in facts:
        copy.wait()
    build_tables(sz, 0, waves, logs, angles, table, table_t, rows_ref)
    leaving = [move(table, table_hbm, one.at[1]), move(table_t, table_t_hbm, one.at[2])]
    arriving.wait()

    def body(i, u):
        facts = row_facts(sz, waves, i, columns)
        length, in_a = facts[2], facts[4]
        shifted[u, pl.ds(ROWS, M), :] = spectra[2 * i + 1]
        rows = []
        for p in range(2):
            rows_a = jnp.concatenate(
                [spectra[2 * i, pl.ds(p, M // 2, stride=2), :], blank], axis=0
            )
            rows_b = shifted[u, pl.ds(ROWS - length + p, EACH, stride=2), :]
            rows.append(jnp.where(in_a[p * EACH : (p + 1) * EACH], rows_a, rows_b))
        state = dot_split(jnp.concatenate(rows, axis=0), turn)
        state = kept(state, facts)
        state_ref[i] = state
        send_rows(sz, 0, i, state, facts, table_t, stage)

    each_pair(
        sz, body, lambda g: group_copy(state_ref, state_hbm, state_sems, g, sz.step).start()
    )
    flush(sz, 0, stage, send, send_hbm, send_sems)
    for g in range(sz.loops):
        group_copy(state_ref, state_hbm, state_sems, g, sz.step).wait()
    for copy in leaving:
        copy.wait()


def rest_kernel(
    sz, waves, angles, angles_hbm, state_hbm, table_hbm, table_t_hbm, send_hbm,
    table, table_t, send, state, logs, stage, rows_ref, one, send_sems,
):
    arriving = move(state_hbm, state, one.at[0])
    scalars = move(angles_hbm.at[8:16], logs, one.at[1])
    scalars.wait()
    build_tables(sz, 1, waves, logs, angles, table, table_t, rows_ref)
    leaving = [move(table, table_hbm, one.at[2]), move(table_t, table_t_hbm, one.at[3])]
    arriving.wait()
    inverse_kernel(sz, 1, waves, state, table_t, send, stage, send_hbm, send_sems)
    for copy in leaving:
        copy.wait()


def inverse_kernel(sz, part, waves, state, table_t, send, stage, target=None, sems=None):
    def body(i, u):
        facts = row_facts(sz, waves, i, state.shape[2])
        send_rows(sz, part, i, state[i], facts, table_t, stage)

    each_pair(sz, body)
    flush(sz, part, stage, send, target, sems)


def forward_kernel(sz, part, waves, state, recv, table, weights, out, stage):
    load_rows(sz, part, recv, stage)

    def body(i, u):
        facts = row_facts(sz, waves, i, state.shape[2])
        out[i] = state[i] + change_rows(sz, part, i, facts, table, weights, stage)

    each_pair(sz, body)


def middle_kernel(
    sz, waves, weights, mixing, mixing_t, speeds, partial_hbm, recv_hbm, table_hbm, table_t_hbm,
    state_hbm, send_hbm,
    state_ref, recv, table, table_t, send, stage_in, stage, one, state_sems, recv_sems, send_sems,
):
    part = sz.parts - 1
    columns = state_ref.shape[2]
    arriving = [
        move(partial_hbm, state_ref, one.at[0]),
        move(table_hbm, table, one.at[1]),
        move(table_t_hbm, table_t, one.at[2]),
    ]
    load_rows(sz, part, recv, stage_in, recv_hbm, recv_sems)
    for copy in arriving:
        copy.wait()

    def body(i, u):
        facts = row_facts(sz, waves, i, columns)
        change = change_rows(sz, part, i, facts, table, weights, stage_in)
        state = updated(state_ref[i], change, facts, mixing, mixing_t, speeds)
        state_ref[i] = state
        send_rows(sz, 0, i, state, facts, table_t, stage)

    each_pair(
        sz, body, lambda g: group_copy(state_ref, state_hbm, state_sems, g, sz.step).start()
    )
    flush(sz, 0, stage, send, send_hbm, send_sems)
    for g in range(sz.loops):
        group_copy(state_ref, state_hbm, state_sems, g, sz.step).wait()


def last_kernel(
    sz, waves, weights, mixing, mixing_t, speeds, partial_hbm, recv_hbm, table_hbm,
    out_hbm,
    state_ref, recv, table, out, stage_in, mixed, one, out_sems, recv_sems,
):
    part = sz.parts - 1
    columns = state_ref.shape[2]
    arriving = [move(partial_hbm, state_ref, one.at[0]), move(table_hbm, table, one.at[1])]
    mixed[...] = jnp.zeros_like(mixed)
    turn_t = turn_matrix(columns, back=True)
    load_rows(sz, part, recv, stage_in, recv_hbm, recv_sems)
    for copy in arriving:
        copy.wait()

    def body(i, u):
        facts = row_facts(sz, waves, i, columns)
        wave_b, length = facts[1:3]
        r = lax.broadcasted_iota(jnp.int32, (M, columns), 0)
        change = change_rows(sz, part, i, facts, table, weights, stage_in)
        state = updated(state_ref[i], change, facts, mixing, mixing_t, speeds)
        state = dot_split(state, turn_t)
        for p in range(2):
            mixed[u, pl.ds(p, EACH, stride=2), :] = state[p * EACH : (p + 1) * EACH]
        out[2 * i] = jnp.where(r < length, mixed[u, :M, :], 0.0)
        out[2 * i + 1] = jnp.where(r < M - wave_b, mixed[u, pl.ds(length, M), :], 0.0)

    each_pair(
        sz, body, lambda g: group_copy(out, out_hbm, out_sems, g, 2 * sz.step).start()
    )
    for g in range(sz.loops):
        group_copy(out, out_hbm, out_sems, g, 2 * sz.step).wait()


def grid_kernel(sz, part, members, recv, synth, slope, scale, *rest):
    pieces, rest = rest[:members], rest[members:]
    send, stage_in, stage, lhs, values, slopes, force, traj, sems = rest
    south = lax.axis_index("space") >= sz.half
    member = lax.axis_index("pert")
    copies = [
        pltpu.make_async_copy(piece, traj.at[i], sems.at[i]) for i, piece in enumerate(pieces)
    ]
    for copy in copies:
        copy.start()
    lanes = recv.shape[2]
    rows = lanes // 2
    lats = sz.part_lats[part]
    block = sz.block(part)
    groups = -(-lats // sz.group)

    def load(d, _):
        stage_in[pl.ds(d * block, block), :] = recv[d].astype(jnp.float32)
        return 0

    lax.fori_loop(0, sz.space, load, 0)
    blank = jnp.zeros((DEPTH - M, lanes), jnp.float32)
    for copy in copies:
        copy.wait()

    def levels(t, field):
        mine = []
        for block in range(members):
            shift = lax.rem(block + members - member, members)
            value = traj[0, t, field].astype(jnp.float32)
            for i in range(1, members):
                value = jnp.where(shift == i, traj[i, t, field].astype(jnp.float32), value)
            mine.append(value)
        return jnp.concatenate(mine, axis=0)

    def body(g, _):
        for q in range(sz.group):
            t = jnp.minimum(g * sz.group + q, lats - 1)
            rows_t = stage_in[pl.ds(t, M, stride=lats), :]
            turned = jnp.transpose(jnp.concatenate([rows_t, blank], axis=0)).astype(jnp.bfloat16)
            lhs[q * rows : (q + 1) * rows, :DEPTH] = turned[:rows]
            lhs[q * rows : (q + 1) * rows, DEPTH:] = turned[rows:]
        left = lhs[...]
        values[...] = jnp.dot(left, synth[...], preferred_element_type=jnp.float32)
        slopes[...] = jnp.dot(left, slope[...], preferred_element_type=jnp.float32)
        for q in range(sz.group):
            t = jnp.minimum(g * sz.group + q, lats - 1)
            here = jnp.where(south, lats - 1 - t, t)
            wind = levels(here, 0)
            for v in range(VARS):
                lo = q * rows + v * LEV
                other = levels(here, 1 + (v + 1) % VARS)
                force[lo : lo + LEV, :] = (
                    wind * slopes[lo : lo + LEV, :] + other * values[lo : lo + LEV, :]
                ).astype(jnp.bfloat16)
        forcing = force[...]
        spectrum = [
            lax.dot_general(
                synth[c * DEPTH : c * DEPTH + M, :],
                forcing,
                (((1,), (1,)), ((), ())),
                preferred_element_type=jnp.float32,
            )
            * scale[...][:, :1]
            for c in range(2)
        ]
        left_side = lax.broadcasted_iota(jnp.int32, (M, lanes), 1) < rows
        for q in range(0, sz.group, 2):
            re = spectrum[0][:, q * rows : (q + 2) * rows]
            im = spectrum[1][:, q * rows : (q + 2) * rows]
            pair = (
                jnp.where(left_side, re, pltpu.roll(im, rows, 1)),
                jnp.where(left_side, pltpu.roll(re, rows, 1), im),
            )
            for o in range(2):
                t = g * sz.group + q + o

                def store(t=t, value=pair[o]):
                    stage[pl.ds(t, M, stride=lats), :] = value

                if (groups - 1) * sz.group + q + o < lats:
                    store()
                else:
                    pl.when(t < lats)(store)
        return 0

    lax.fori_loop(0, groups, body, 0)

    def out(d, _):
        send[d] = stage[pl.ds(d * block, block), :].astype(jnp.bfloat16)
        return 0

    lax.fori_loop(0, sz.space, out, 0)


def grid_stage(sz, part, recv, pieces, synth, slope, scale):
    members = len(pieces)
    lanes = recv.shape[2]
    wide = sz.group * lanes // 2
    count = M * sz.part_lats[part]
    return pl.pallas_call(
        lambda *refs: grid_kernel(sz, part, members, *refs),
        out_shape=jax.ShapeDtypeStruct(recv.shape, jnp.bfloat16),
        in_specs=vmem(4) + [pl.BlockSpec(memory_space=pl.ANY)] * members,
        out_specs=vmem(1)[0],
        scratch_shapes=[
            pltpu.VMEM((count, lanes), jnp.float32),
            pltpu.VMEM((count, lanes), jnp.float32),
            pltpu.VMEM((wide, 2 * DEPTH), jnp.bfloat16),
            pltpu.VMEM((wide, NLON), jnp.float32),
            pltpu.VMEM((wide, NLON), jnp.float32),
            pltpu.VMEM((wide, NLON), jnp.bfloat16),
            pltpu.VMEM((members,) + pieces[0].shape, jnp.bfloat16),
            pltpu.SemaphoreType.DMA((members,)),
        ],
        compiler_params=params(),
        cost_estimate=cost(9.0),
        name="grid_stage",
    )(recv, synth, slope, scale, *pieces)


def zonal_tables(wave_list):
    cell_index = jnp.arange(NLON, dtype=jnp.int32)
    wave_pad = jnp.concatenate([wave_list, jnp.zeros((DEPTH - M,), jnp.int32)])
    phase_index = wave_pad[:, None] * cell_index[None, :] % NLON
    angles = phase_index.astype(jnp.float32) * (2.0 * math.pi / NLON)
    factor = jnp.where(wave_pad == 0, 1.0, 2.0).astype(jnp.float32)
    inside = (jnp.arange(DEPTH) < M).astype(jnp.float32)
    gain = (factor * inside)[:, None]
    cosine, sine = gain * jnp.cos(angles), gain * jnp.sin(angles)
    wave = wave_pad.astype(jnp.float32)[:, None]
    synth = jnp.concatenate([-cosine, sine], axis=0).astype(jnp.bfloat16)
    slope = jnp.concatenate([wave * sine, wave * cosine], axis=0).astype(jnp.bfloat16)
    scale = jnp.broadcast_to((-1.0 / (NLON * factor[:M]))[:, None], (M, 128))
    return synth, slope, scale


def split_matrix(matrix):
    high = matrix.astype(jnp.bfloat16)
    low = (matrix - high.astype(jnp.float32)).astype(jnp.bfloat16)
    top = jnp.concatenate([high, low], axis=1)
    bottom = jnp.concatenate([high, jnp.zeros_like(low)], axis=1)
    return jnp.concatenate([top, bottom], axis=0)


def shards(sz, spectra, wave_order, traj_wind, traj_state, vertical_modes, mode_speeds):
    columns = spectra.shape[2]
    index, real = [], []
    for ranges in sz.ranges:
        within = np.concatenate([np.arange(lo, lo + size) for lo, size in ranges])
        pad = sz.part_pad - within.size
        for b in range(sz.half):
            index.append(np.pad(b * sz.lats + within, (0, pad)))
            real.append(np.pad(np.ones(within.size, bool), (0, pad)))
    index, real = np.concatenate(index), np.concatenate(real)
    colat = np.where(real, (index + 0.5) * (math.pi / NLAT), math.pi / 2)
    angles = np.zeros((16, 128), np.float32)
    angles[8:11] = np.pad(sectoral_logs(), (0, 3 * 128 - M)).reshape(3, 128)
    for part in range(sz.parts):
        mine = colat[part * sz.part_rows : (part + 1) * sz.part_rows]
        angles[2 * part] = np.cos(mine)
        angles[2 * part + 1] = np.log2(np.sin(mine))
    angles = jnp.asarray(angles)
    weights = (np.sin(colat) * (math.pi / NLAT) * real).astype(np.float32)
    weights = np.broadcast_to(weights[:, None], (sz.north, columns))
    weights = [jnp.asarray(w) for w in np.split(weights, sz.parts)]

    same = np.kron(np.eye(columns // LEV, dtype=np.float32), np.ones((LEV, LEV), np.float32))
    mixing = split_matrix(jnp.tile(vertical_modes.T, (columns // LEV, columns // LEV)) * same)
    mixing_t = split_matrix(jnp.tile(vertical_modes, (columns // LEV, columns // LEV)) * same)
    speeds = jnp.tile(mode_speeds, columns // LEV)[None, :]

    def stages(part):
        return pltpu.VMEM((sz.space, sz.block_pad(part), columns), jnp.float32)

    def sends(part):
        return jax.ShapeDtypeStruct((sz.space, sz.block(part), columns), jnp.bfloat16)

    state_shape = jax.ShapeDtypeStruct((sz.pairs, ROWS, columns), jnp.float32)

    table_specs = [jax.ShapeDtypeStruct(shape, jnp.bfloat16) for shape in table_shapes(sz)]
    table_vmem = [pltpu.VMEM(shape, jnp.bfloat16) for shape in table_shapes(sz)]
    rows_vmem = pltpu.VMEM((sz.pair_pad * ROWS, 128), jnp.float32)
    shift_vmem = pltpu.VMEM((UNROLL, SHIFTED, columns), jnp.float32)
    state_vmem = pltpu.VMEM(state_shape.shape, jnp.float32)

    def block_vmem(part):
        return pltpu.VMEM(sends(part).shape, jnp.bfloat16)

    def dma(count):
        return pltpu.SemaphoreType.DMA((count,))

    def call(body, outs, scalars, near, far, scratch, microseconds, name, away=True):
        anywhere = pl.BlockSpec(memory_space=pltpu.HBM)
        return pl.pallas_call(
            lambda *refs: body(sz, *refs),
            out_shape=tuple(outs),
            in_specs=smem(len(scalars)) + vmem(len(near)) + [anywhere] * len(far),
            out_specs=(anywhere,) * len(outs) if away else tuple(vmem(len(outs))),
            scratch_shapes=scratch,
            compiler_params=params(VMEM_ALONE if away else VMEM_BYTES),
            cost_estimate=cost(microseconds),
            name=name,
        )(*scalars, *near, *far)

    members = LEV // traj_wind.shape[1]

    def shared(value):
        return [value] + [
            lax.ppermute(value, "pert", [(i, (i - shift) % members) for i in range(members)])
            for shift in range(1, members)
        ]

    def cut(step, part):
        fields = [traj_wind[step][None], traj_state[step]]
        local = jnp.concatenate(
            [
                jnp.concatenate([f[:, :, lo : lo + size] for f in fields], axis=0)
                for lo, size in sz.ranges[part]
            ],
            axis=2,
        )
        return shared(jnp.transpose(local, (2, 0, 1, 3)))

    def transpose(value):
        return lax.all_to_all(value, "space", 0, 0, tiled=True)

    traj = {(step, part): cut(step, part) for step in range(STEPS) for part in range(2)}

    table_0, table_t_0, state, send_0 = call(
        first_kernel,
        table_specs + [state_shape, sends(0)],
        [], [], [wave_order, angles, spectra],
        [
            pltpu.SMEM((M,), jnp.int32), pltpu.SMEM((8, 128), jnp.float32),
            pltpu.VMEM((8, 128), jnp.float32),
            pltpu.VMEM(spectra.shape, jnp.float32), *table_vmem, state_vmem, block_vmem(0),
            stages(0), shift_vmem, rows_vmem, dma(7), dma(sz.loops), dma(sz.bundles),
        ],
        12.0, "tables_inverse",
    )
    table_1 = table_t_1 = None
    for step in range(STEPS):
        recv_0 = transpose(send_0)
        if step == 0:
            table_1, table_t_1, send_1 = call(
                rest_kernel,
                table_specs + [sends(1)],
                [wave_order], [angles], [angles, state],
                [
                    *table_vmem, block_vmem(1), state_vmem, pltpu.SMEM((8, 128), jnp.float32),
                    stages(1), rows_vmem, dma(4), dma(sz.bundles),
                ],
                8.0, "tables_inverse_rest",
            )
        else:
            (send_1,) = call(
                lambda s, *refs: inverse_kernel(s, 1, *refs),
                [sends(1)], [wave_order], [state, table_t_1], [], [stages(1)],
                4.0, "inverse_rest", away=False,
            )
        recv_1 = transpose(send_1)
        if step == 0:
            recv_0, later = lax.optimization_barrier((recv_0, wave_order))
            synth, slope, scale = zonal_tables(later)
        back_0 = transpose(grid_stage(sz, 0, recv_0, traj[step, 0], synth, slope, scale))
        back_1 = transpose(grid_stage(sz, 1, recv_1, traj[step, 1], synth, slope, scale))
        (partial,) = call(
            lambda s, *refs: forward_kernel(s, 0, *refs),
            [state_shape], [wave_order], [state, back_0, table_0, weights[0]], [], [stages(0)],
            5.0, "forward_part", away=False,
        )
        near = [weights[1], mixing, mixing_t, speeds]
        if step < STEPS - 1:
            state, send_0 = call(
                middle_kernel,
                [state_shape, sends(0)],
                [wave_order], near, [partial, back_1, table_1, table_t_0],
                [
                    state_vmem, block_vmem(1), *table_vmem, block_vmem(0), stages(1), stages(0),
                    dma(3), dma(sz.loops), dma(sz.bundles), dma(sz.bundles),
                ],
                12.0, "forward_inverse",
            )
        else:
            (out,) = call(
                last_kernel,
                [jax.ShapeDtypeStruct(spectra.shape, jnp.float32)],
                [wave_order], near, [partial, back_1, table_1],
                [
                    state_vmem, block_vmem(1), table_vmem[0],
                    pltpu.VMEM(spectra.shape, jnp.float32), stages(1), shift_vmem,
                    dma(2), dma(sz.loops), dma(sz.bundles),
                ],
                10.0, "forward_last",
            )
    return out


def solution(mesh):
    sz = Sizes(mesh.shape["space"])
    placed = (
        P("space", None, "pert"),
        P(),
        P(None, "pert", "space", None),
        P(None, None, "pert", "space", None),
        P(),
        P(),
    )
    return jax.shard_map(
        lambda *args: shards(sz, *args),
        mesh=mesh,
        in_specs=placed,
        out_specs=P("space", None, "pert"),
        check_vma=False,
    )
```

time: 312 us -> 301 us (0.965)
  waiting for transfers between devices: 145 us -> 140 us
  local copies, waits for them, and re-layouts: 21.4 us -> 17.4 us
    ppermute x4, waiting for transfers between devices: 11 us -> 4.27 us  [shared(): lax.ppermute(value, 'pert', [(i, (i - shift) % members) for i in range(me...]
    unnamed x70 -> x56, local copies, waits for them, and re-layouts: 16.1 us -> 11.9 us
    pallas_call x8 -> x7, Pallas kernels: 40.5 us -> 40.8 us  [call(): pl.pallas_call(lambda *refs: body(sz, *refs), out_shape=tuple(outs), in_s...]
    another operation x2 -> x1, other arithmetic: 7.56 us -> 7.51 us
  transfers between devices with their start and end apart: 12 -> 12, of which waited for: 10 -> 9; matrix products, arithmetic and copies ran while one was open for 6% -> 7% of each run, Pallas kernels for 21% -> 23%
where the time goes in v4:
time: 301 us; the launch traced here: 300 us
  waiting for transfers between devices  140 us (47%)
  Pallas kernels  85.4 us (28%)
  starting transfers between devices  42.5 us (14%)
  local copies, waits for them, and re-layouts  17.4 us (6%)
  other arithmetic  14 us (5%)
    all_to_all x8, waiting for transfers between devices, transpose(): return lax.all_to_all(value, 'space', 0, 0, tiled=True)  136 us
    pallas_call x4, Pallas kernels, grid_stage(): pl.pallas_call(lambda *refs: grid_kernel(sz, part, members, *refs), out_s...  44.6 us
    pallas_call x7, Pallas kernels, call(): pl.pallas_call(lambda *refs: body(sz, *refs), out_shape=tuple(outs), in_s...  40.8 us
    all_to_all x8, starting transfers between devices, transpose(): return lax.all_to_all(value, 'space', 0, 0, tiled=True)  39.6 us
    unnamed x56, local copies, waits for them, and re-layouts  11.9 us
    another operation x1, other arithmetic  7.51 us
  transfers between devices with their start and end apart: 12, of which 9 were waited for; matrix products, arithmetic and copies ran while one was open for 7% of the time, Pallas kernels for 23%

profile of v4, /device:TPU:15, one launch (start us, length us, event | category | flops | bytes accessed | tf_op | source)
XLA Modules:
  0.0 300.2 jit_solution(1737222973122396853)
XLA Ops:
  0.0 8.7 %tables_inverse.1 = (bf16[10,2,168,128]{3,2,1,0:T(8,128)(2,1)}, bf16[10,2,128,256]{3,2,1,0:T(8,128)(2,1)}, f32[10,336,128]{2,1,0:T(8,128)}, bf16[16,320,128]{2,1,0:T(8,128)(2,1)}) custom-call(s32[320]{0:T(512)} %refs_0_.13, f32[16,128]{1,0:T(8,128)} %constant.38.clone.refs_1_.refs_2_, f32[20,320,128]{2,1,0:T(8,128)} %refs_2_.2), custom_call_target="tpu_custom_call" | custom-call | flops 359999995904 | bytes 1048576 | tf_op jit(solution)/shard_map/tables_inverse/pallas_call | solution.py:654
  8.7 6.6 %all-to-all-start = ((bf16[16,320,128]{2,1,0:T(8,128)(2,1)}), bf16[16,320,128]{2,1,0:T(8,128)(2,1)}, u32[]{:S(2)}, u32[]{:S(2)}) async-start(bf16[16,320,128]{2,1,0:T(8,128)(2,1)} %get-tuple-element.17), calls=%async_computation | async-start | bytes 2621440 | tf_op jit(solution)/shard_map/all_to_all | solution.py:685
  28.8 7.5 %tables_inverse_rest.1 = (bf16[10,2,168,128]{3,2,1,0:T(8,128)(2,1)}, bf16[10,2,128,256]{3,2,1,0:T(8,128)(2,1)}, bf16[16,280,128]{2,1,0:T(8,128)(2,1)}) custom-call(s32[320]{0:T(512)} %refs_0_.13, f32[16,128]{1,0:T(8,128)} %constant.38.clone.refs_1_.refs_2_, f32[16,128]{1,0:T(8,128)} %constant.38.clone.refs_1_.refs_2_, ...), custom_call_target="tpu_custom_call" | custom-call | flops 240000008192 | bytes 1048576 | tf_op jit(solution)/shard_map/tables_inverse_rest/pallas_call | solution.py:654
  38.1 8.1 %all-to-all-done.refs_0_ = bf16[16,320,128]{2,1,0:T(8,128)(2,1)} async-done(((bf16[16,320,128]{2,1,0:T(8,128)(2,1)}), bf16[16,320,128]{2,1,0:T(8,128)(2,1)}, u32[]{:S(2)}, u32[]{:S(2)}) %all-to-all-start) | async-done | bytes 1310752 | tf_op jit(solution)/shard_map/all_to_all | solution.py:685
  46.2 4.6 %all-to-all-start.2 = ((bf16[16,280,128]{2,1,0:T(8,128)(2,1)}), bf16[16,280,128]{2,1,0:T(8,128)(2,1)}, u32[]{:S(2)}, u32[]{:S(2)}) async-start(bf16[16,280,128]{2,1,0:T(8,128)(2,1)} %get-tuple-element.21), calls=%async_computation.2 | async-start | bytes 2293760 | tf_op jit(solution)/shard_map/all_to_all | solution.py:685
  50.8 7.5 %multiply_convert_fusion.1 = (bf16[384,960]{1,0:T(8,128)(2,1)S(1)}, bf16[384,960]{1,0:T(8,128)(2,1)S(1)}, bf16[384,960]{1,0:T(8,128)(2,1)S(1)}, bf16[384,960]{1,0:T(8,128)(2,1)S(1)}) fusion(f32[384]{0:T(512)S(1)} %get-tuple-element.51, s32[384]{0:T(512)S(1)} %get-tuple-element.52, f32[384]{0:T(512)S(1)} %get-tuple-element.50), kind=kLoop, calls=%fused_computation.10 | loop fusion | flops 6635520 | bytes 2953728 | tf_op jit(solution)/shard_map/convert
  58.9 11.7 %grid_stage.4 = bf16[16,320,128]{2,1,0:T(8,128)(2,1)S(1)} custom-call(bf16[16,320,128]{2,1,0:T(8,128)(2,1)} %all-to-all-done.refs_0_, bf16[768,960]{1,0:T(8,128)(2,1)S(1)} %get-tuple-element.53.refs_1_, bf16[768,960]{1,0:T(8,128)(2,1)S(1)} %get-tuple-element.54.refs_2_, f32[320,128]{1,0:T(8,128)S(1)} %broadcast_in_dim.12.refs_3_, ...), custom_call_target="tpu_custom_call" | custom-call | flops 269999996928 | bytes 1048576 | tf_op jit(solution)/shard_map/grid_stage/pallas_call | solution.py:560
  71.7 6.5 %all-to-all-done.2.refs_0_ = bf16[16,280,128]{2,1,0:T(8,128)(2,1)} async-done(((bf16[16,280,128]{2,1,0:T(8,128)(2,1)}), bf16[16,280,128]{2,1,0:T(8,128)(2,1)}, u32[]{:S(2)}, u32[]{:S(2)}) %all-to-all-start.2) | async-done | bytes 1146912 | tf_op jit(solution)/shard_map/all_to_all | solution.py:685
  78.2 4.6 %all-to-all-start.1 = ((bf16[16,320,128]{2,1,0:T(8,128)(2,1)}), bf16[16,320,128]{2,1,0:T(8,128)(2,1)}, u32[]{:S(2)}, u32[]{:S(2)}) async-start(bf16[16,320,128]{2,1,0:T(8,128)(2,1)} %copy-done.5), calls=%async_computation.1 | async-start | bytes 2621440 | tf_op jit(solution)/shard_map/all_to_all | solution.py:685
  87.1 11.1 %grid_stage.5 = bf16[16,280,128]{2,1,0:T(8,128)(2,1)} custom-call(bf16[16,280,128]{2,1,0:T(8,128)(2,1)} %all-to-all-done.2.refs_0_, bf16[768,960]{1,0:T(8,128)(2,1)} %copy-done, bf16[768,960]{1,0:T(8,128)(2,1)} %copy-done.2, f32[320,128]{1,0:T(8,128)S(1)} %broadcast_in_dim.12.refs_3_, bf16[14,3,16,960]{3,2,1,0:T(8,128)(2,1)} %maximum_bitcast_fusion.2.refs_4_, ...), custom_call_target="tpu_custom_call" | custom-call | flops 269999996928 | bytes 1048576 | tf_op jit(solution)/shard_map/grid_stage/pallas_call | solution.py:560
  98.3 15.5 %all-to-all-done.1.refs_2_ = bf16[16,320,128]{2,1,0:T(8,128)(2,1)} async-done(((bf16[16,320,128]{2,1,0:T(8,128)(2,1)}), bf16[16,320,128]{2,1,0:T(8,128)(2,1)}, u32[]{:S(2)}, u32[]{:S(2)}) %all-to-all-start.1) | async-done | bytes 1310752 | tf_op jit(solution)/shard_map/all_to_all | solution.py:685
  124.1 21.7 %all-to-all-done.3.refs_6_ = bf16[16,280,128]{2,1,0:T(8,128)(2,1)} async-done(((bf16[16,280,128]{2,1,0:T(8,128)(2,1)}), bf16[16,280,128]{2,1,0:T(8,128)(2,1)}, u32[]{:S(2)}, u32[]{:S(2)}) %all-to-all-start.3) | async-done | bytes 1146912 | tf_op jit(solution)/shard_map/all_to_all | solution.py:685
  146.5 9.8 %forward_inverse.1 = (f32[10,336,128]{2,1,0:T(8,128)}, bf16[16,320,128]{2,1,0:T(8,128)(2,1)}) custom-call(s32[320]{0:T(512)} %refs_0_.13, f32[128,128]{1,0:T(8,128)} %jit_solution_.7.refs_1_, bf16[256,256]{1,0:T(8,128)(2,1)} %get-tuple-element.57.refs_2_, bf16[256,256]{1,0:T(8,128)(2,1)} %get-tuple-element.58.refs_3_, ...), custom_call_target="tpu_custom_call" | custom-call | flops 359999995904 | bytes 1048576 | tf_op jit(solution)/shard_map/forward_inverse/pallas_call | solution.py:654
  156.3 4.7 %all-to-all-start.4 = ((bf16[16,320,128]{2,1,0:T(8,128)(2,1)}), bf16[16,320,128]{2,1,0:T(8,128)(2,1)}, u32[]{:S(2)}, u32[]{:S(2)}) async-start(bf16[16,320,128]{2,1,0:T(8,128)(2,1)} %get-tuple-element.25), calls=%async_computation.4 | async-start | bytes 2621440 | tf_op jit(solution)/shard_map/all_to_all | solution.py:685
  165.0 26.8 %all-to-all-done.4.refs_0_ = bf16[16,320,128]{2,1,0:T(8,128)(2,1)} async-done(((bf16[16,320,128]{2,1,0:T(8,128)(2,1)}), bf16[16,320,128]{2,1,0:T(8,128)(2,1)}, u32[]{:S(2)}, u32[]{:S(2)}) %all-to-all-start.4) | async-done | bytes 1310752 | tf_op jit(solution)/shard_map/all_to_all | solution.py:685
  191.7 4.9 %all-to-all-start.6 = ((bf16[16,280,128]{2,1,0:T(8,128)(2,1)}), bf16[16,280,128]{2,1,0:T(8,128)(2,1)}, u32[]{:S(2)}, u32[]{:S(2)}) async-start(bf16[16,280,128]{2,1,0:T(8,128)(2,1)} %copy-done.6), calls=%async_computation.6 | async-start | bytes 2293760 | tf_op jit(solution)/shard_map/all_to_all | solution.py:685
  196.6 10.7 %grid_stage.6 = bf16[16,320,128]{2,1,0:T(8,128)(2,1)S(1)} custom-call(bf16[16,320,128]{2,1,0:T(8,128)(2,1)} %all-to-all-done.4.refs_0_, bf16[768,960]{1,0:T(8,128)(2,1)S(1)} %copy-done.1, bf16[768,960]{1,0:T(8,128)(2,1)S(1)} %copy-done.3, f32[320,128]{1,0:T(8,128)S(1)} %broadcast_in_dim.12.refs_3_, bf16[16,3,16,960]{3,2,1,0:T(8,128)(2,1)} %maximum_bitcast_fusion.1.refs_4_, ...), custom_call_target="tpu_custom_call" | custom-call | flops 269999996928 | bytes 1048576 | tf_op jit(solution)/shard_map/grid_stage/pallas_call | solution.py:560
  208.4 15.4 %all-to-all-done.6.refs_0_ = bf16[16,280,128]{2,1,0:T(8,128)(2,1)} async-done(((bf16[16,280,128]{2,1,0:T(8,128)(2,1)}), bf16[16,280,128]{2,1,0:T(8,128)(2,1)}, u32[]{:S(2)}, u32[]{:S(2)}) %all-to-all-start.6) | async-done | bytes 1146912 | tf_op jit(solution)/shard_map/all_to_all | solution.py:685
  223.8 4.9 %all-to-all-start.5 = ((bf16[16,320,128]{2,1,0:T(8,128)(2,1)}), bf16[16,320,128]{2,1,0:T(8,128)(2,1)}, u32[]{:S(2)}, u32[]{:S(2)}) async-start(bf16[16,320,128]{2,1,0:T(8,128)(2,1)} %copy-done.4), calls=%async_computation.5 | async-start | bytes 2621440 | tf_op jit(solution)/shard_map/all_to_all | solution.py:685
  228.6 11.1 %grid_stage.7 = bf16[16,280,128]{2,1,0:T(8,128)(2,1)} custom-call(bf16[16,280,128]{2,1,0:T(8,128)(2,1)} %all-to-all-done.6.refs_0_, bf16[768,960]{1,0:T(8,128)(2,1)} %copy-done, bf16[768,960]{1,0:T(8,128)(2,1)} %copy-done.2, f32[320,128]{1,0:T(8,128)S(1)} %broadcast_in_dim.12.refs_3_, bf16[14,3,16,960]{3,2,1,0:T(8,128)(2,1)} %maximum_bitcast_fusion.3.refs_4_, ...), custom_call_target="tpu_custom_call" | custom-call | flops 269999996928 | bytes 1048576 | tf_op jit(solution)/shard_map/grid_stage/pallas_call | solution.py:560
  239.8 19.5 %all-to-all-done.5.refs_2_ = bf16[16,320,128]{2,1,0:T(8,128)(2,1)} async-done(((bf16[16,320,128]{2,1,0:T(8,128)(2,1)}), bf16[16,320,128]{2,1,0:T(8,128)(2,1)}, u32[]{:S(2)}, u32[]{:S(2)}) %all-to-all-start.5) | async-done | bytes 1310752 | tf_op jit(solution)/shard_map/all_to_all | solution.py:685
  259.3 4.9 %all-to-all-start.7 = ((bf16[16,280,128]{2,1,0:T(8,128)(2,1)}), bf16[16,280,128]{2,1,0:T(8,128)(2,1)}, u32[]{:S(2)}, u32[]{:S(2)}) async-start(bf16[16,280,128]{2,1,0:T(8,128)(2,1)} %grid_stage.7), calls=%async_computation.7 | async-start | bytes 2293760 | tf_op jit(solution)/shard_map/all_to_all | solution.py:685
  268.9 22.4 %all-to-all-done.7.refs_6_ = bf16[16,280,128]{2,1,0:T(8,128)(2,1)} async-done(((bf16[16,280,128]{2,1,0:T(8,128)(2,1)}), bf16[16,280,128]{2,1,0:T(8,128)(2,1)}, u32[]{:S(2)}, u32[]{:S(2)}) %all-to-all-start.7) | async-done | bytes 1146912 | tf_op jit(solution)/shard_map/all_to_all | solution.py:685
  291.3 8.7 %forward_last.1 = f32[20,320,128]{2,1,0:T(8,128)} custom-call(s32[320]{0:T(512)} %refs_0_.13, f32[128,128]{1,0:T(8,128)} %jit_solution_.7.refs_1_, bf16[256,256]{1,0:T(8,128)(2,1)} %get-tuple-element.57.refs_2_, bf16[256,256]{1,0:T(8,128)(2,1)} %get-tuple-element.58.refs_3_, f32[1,128]{1,0:T(1,128)} %broadcast_in_dim_tile.3.refs_4_, ...), custom_call_target="tpu_custom_call" | custom-call | flops 299999985664 | bytes 1048576 | tf_op jit(solution)/shard_map/forward_last/pallas_call | solution.py:654
  (94 shorter events, 41.9 us)
Async XLA Ops:
  8.7 37.5 %all-to-all-start = ((bf16[16,320,128]{2,1,0:T(8,128)(2,1)}), bf16[16,320,128]{2,1,0:T(8,128)(2,1)}, u32[]{:S(2)}, u32[]{:S(2)}) async-start(bf16[16,320,128]{2,1,0:T(8,128)(2,1)} %get-tuple-element.17), calls=%async_computation | async-start | bytes 2621440 | tf_op jit(solution)/shard_map/all_to_all | solution.py:685
  21.6 37.2 %collective-permute-start = (bf16[16,3,16,960]{3,2,1,0:T(8,128)(2,1)}, bf16[16,3,16,960]{3,2,1,0:T(8,128)(2,1)}, u32[]{:S(2)}, u32[]{:S(2)}) collective-permute-start(bf16[16,3,16,960]{3,2,1,0:T(8,128)(2,1)} %maximum_bitcast_fusion.refs_4_), channel_id=1, source_target_pairs={{0,16},{16,0},{1,17},{17,1},{2,18},{18,2},{3,19},{19,3},{4,20},{20... | collective-permute-start | bytes 4423688 | tf_op jit(solution)/shard_map/ppermute | solution.py:669
  23.3 63.8 %collective-permute-start.1 = (bf16[14,3,16,960]{3,2,1,0:T(8,128)(2,1)}, bf16[14,3,16,960]{3,2,1,0:T(8,128)(2,1)}, u32[]{:S(2)}, u32[]{:S(2)}) collective-permute-start(bf16[14,3,16,960]{3,2,1,0:T(8,128)(2,1)} %maximum_bitcast_fusion.2.refs_4_), channel_id=1, source_target_pairs={{0,16},{16,0},{1,17},{17,1},{2,18},{18,2},{3,19},{19,3},{4,20},{20... | collective-permute-start | bytes 3870728 | tf_op jit(solution)/shard_map/ppermute | solution.py:669
  26.0 170.6 %collective-permute-start.2 = (bf16[16,3,16,960]{3,2,1,0:T(8,128)(2,1)}, bf16[16,3,16,960]{3,2,1,0:T(8,128)(2,1)}, u32[]{:S(2)}, u32[]{:S(2)}) collective-permute-start(bf16[16,3,16,960]{3,2,1,0:T(8,128)(2,1)} %maximum_bitcast_fusion.1.refs_4_), channel_id=1, source_target_pairs={{0,16},{16,0},{1,17},{17,1},{2,18},{18,2},{3,19},{19,3},{4,20},{20... | collective-permute-start | bytes 4423688 | tf_op jit(solution)/shard_map/ppermute | solution.py:669
  27.5 201.1 %collective-permute-start.3 = (bf16[14,3,16,960]{3,2,1,0:T(8,128)(2,1)}, bf16[14,3,16,960]{3,2,1,0:T(8,128)(2,1)}, u32[]{:S(2)}, u32[]{:S(2)}) collective-permute-start(bf16[14,3,16,960]{3,2,1,0:T(8,128)(2,1)} %maximum_bitcast_fusion.3.refs_4_), channel_id=1, source_target_pairs={{0,16},{16,0},{1,17},{17,1},{2,18},{18,2},{3,19},{19,3},{4,20},{20... | collective-permute-start | bytes 3870728 | tf_op jit(solution)/shard_map/ppermute | solution.py:669
  36.6 14.2 %copy-start.9 = (s32[320]{0:T(512)S(1)}, s32[320]{0:T(512)}, u32[]{:S(2)}) copy-start(s32[320]{0:T(512)} %refs_0_.13) | copy-start | bytes 3844
  46.2 32.0 %all-to-all-start.2 = ((bf16[16,280,128]{2,1,0:T(8,128)(2,1)}), bf16[16,280,128]{2,1,0:T(8,128)(2,1)}, u32[]{:S(2)}, u32[]{:S(2)}) async-start(bf16[16,280,128]{2,1,0:T(8,128)(2,1)} %get-tuple-element.21), calls=%async_computation.2 | async-start | bytes 2293760 | tf_op jit(solution)/shard_map/all_to_all | solution.py:685
  58.8 11.8 %copy-start = (bf16[768,960]{1,0:T(8,128)(2,1)}, bf16[768,960]{1,0:T(8,128)(2,1)S(1)}, u32[]{:S(2)}) copy-start(bf16[768,960]{1,0:T(8,128)(2,1)S(1)} %get-tuple-element.53.refs_1_) | copy-start | bytes 4423684
  58.8 11.8 %copy-start.2 = (bf16[768,960]{1,0:T(8,128)(2,1)}, bf16[768,960]{1,0:T(8,128)(2,1)S(1)}, u32[]{:S(2)}) copy-start(bf16[768,960]{1,0:T(8,128)(2,1)S(1)} %get-tuple-element.54.refs_2_) | copy-start | bytes 4423684
  78.2 35.5 %all-to-all-start.1 = ((bf16[16,320,128]{2,1,0:T(8,128)(2,1)}), bf16[16,320,128]{2,1,0:T(8,128)(2,1)}, u32[]{:S(2)}, u32[]{:S(2)}) async-start(bf16[16,320,128]{2,1,0:T(8,128)(2,1)} %copy-done.5), calls=%async_computation.1 | async-start | bytes 2621440 | tf_op jit(solution)/shard_map/all_to_all | solution.py:685
  98.2 20.1 %copy-start.25 = (f32[128]{0:T(128)S(1)}, f32[128]{0:T(128)}, u32[]{:S(2)}) copy-start(f32[128]{0:T(128)} %constant.39.clone) | copy-start | bytes 1540
  98.2 20.2 %copy-start.10 = (s32[320]{0:T(512)S(1)}, s32[320]{0:T(512)}, u32[]{:S(2)}) copy-start(s32[320]{0:T(512)} %refs_0_.13) | copy-start | bytes 3844
  98.2 20.2 %copy-start.19 = (bf16[10,2,168,128]{3,2,1,0:T(8,128)(2,1)S(1)}, bf16[10,2,168,128]{3,2,1,0:T(8,128)(2,1)}, u32[]{:S(2)}) copy-start(bf16[10,2,168,128]{3,2,1,0:T(8,128)(2,1)} %get-tuple-element.20.refs_3_) | copy-start | bytes 2580484
  113.8 32.0 %all-to-all-start.3 = ((bf16[16,280,128]{2,1,0:T(8,128)(2,1)}), bf16[16,280,128]{2,1,0:T(8,128)(2,1)}, u32[]{:S(2)}, u32[]{:S(2)}) async-start(bf16[16,280,128]{2,1,0:T(8,128)(2,1)} %grid_stage.5), calls=%async_computation.3 | async-start | bytes 2293760 | tf_op jit(solution)/shard_map/all_to_all | solution.py:685
  119.9 25.9 %copy-start.24 = (f32[128]{0:T(128)S(1)}, f32[128]{0:T(128)}, u32[]{:S(2)}) copy-start(f32[128]{0:T(128)} %constant.40.clone) | copy-start | bytes 1540
  156.3 35.4 %all-to-all-start.4 = ((bf16[16,320,128]{2,1,0:T(8,128)(2,1)}), bf16[16,320,128]{2,1,0:T(8,128)(2,1)}, u32[]{:S(2)}, u32[]{:S(2)}) async-start(bf16[16,320,128]{2,1,0:T(8,128)(2,1)} %get-tuple-element.25), calls=%async_computation.4 | async-start | bytes 2621440 | tf_op jit(solution)/shard_map/all_to_all | solution.py:685
  162.5 34.1 %copy-start.3 = (bf16[768,960]{1,0:T(8,128)(2,1)S(1)}, bf16[768,960]{1,0:T(8,128)(2,1)}, u32[]{:S(2)}) copy-start(bf16[768,960]{1,0:T(8,128)(2,1)} %copy-done.2) | copy-start | bytes 4423684
  165.0 31.7 %copy-start.1 = (bf16[768,960]{1,0:T(8,128)(2,1)S(1)}, bf16[768,960]{1,0:T(8,128)(2,1)}, u32[]{:S(2)}) copy-start(bf16[768,960]{1,0:T(8,128)(2,1)} %copy-done) | copy-start | bytes 4423684
  191.7 32.0 %all-to-all-start.6 = ((bf16[16,280,128]{2,1,0:T(8,128)(2,1)}), bf16[16,280,128]{2,1,0:T(8,128)(2,1)}, u32[]{:S(2)}, u32[]{:S(2)}) async-start(bf16[16,280,128]{2,1,0:T(8,128)(2,1)} %copy-done.6), calls=%async_computation.6 | async-start | bytes 2293760 | tf_op jit(solution)/shard_map/all_to_all | solution.py:685
  223.8 35.5 %all-to-all-start.5 = ((bf16[16,320,128]{2,1,0:T(8,128)(2,1)}), bf16[16,320,128]{2,1,0:T(8,128)(2,1)}, u32[]{:S(2)}, u32[]{:S(2)}) async-start(bf16[16,320,128]{2,1,0:T(8,128)(2,1)} %copy-done.4), calls=%async_computation.5 | async-start | bytes 2621440 | tf_op jit(solution)/shard_map/all_to_all | solution.py:685
  239.7 24.4 %copy-start.8 = (f32[128,128]{1,0:T(8,128)S(1)}, f32[128,128]{1,0:T(8,128)}, u32[]{:S(2)}) copy-start(f32[128,128]{1,0:T(8,128)} %copy-done.7) | copy-start | bytes 196612
  239.8 24.4 %copy-start.12 = (s32[320]{0:T(512)S(1)}, s32[320]{0:T(512)}, u32[]{:S(2)}) copy-start(s32[320]{0:T(512)} %refs_0_.13) | copy-start | bytes 3844
  239.8 24.4 %copy-start.14 = (f32[10,336,128]{2,1,0:T(8,128)S(1)}, f32[10,336,128]{2,1,0:T(8,128)}, u32[]{:S(2)}) copy-start(f32[10,336,128]{2,1,0:T(8,128)} %get-tuple-element.24.refs_1_) | copy-start | bytes 5160964
  259.3 32.0 %all-to-all-start.7 = ((bf16[16,280,128]{2,1,0:T(8,128)(2,1)}), bf16[16,280,128]{2,1,0:T(8,128)(2,1)}, u32[]{:S(2)}, u32[]{:S(2)}) async-start(bf16[16,280,128]{2,1,0:T(8,128)(2,1)} %grid_stage.7), calls=%async_computation.7 | async-start | bytes 2293760 | tf_op jit(solution)/shard_map/all_to_all | solution.py:685
  (15 other events, 44.3 us)

commit v5 on v4

--- a/solution.py
+++ b/solution.py
@@ -63,6 +63,9 @@
         self.bundle = space // 4 if space % 4 == 0 else space
         self.bundles = space // self.bundle
 
+    def direct(self, part):
+        return self.part_lats[part] % 16 == 0
+
     def block(self, part):
         return self.slots * self.part_lats[part]
 
@@ -78,6 +81,7 @@
 
 def build_tables(sz, part, waves, logs, angles, table, table_t, rows_ref):
     cosines, log_sines = angles[2 * part : 2 * part + 1, :], angles[2 * part + 1 : 2 * part + 2, :]
+    quadrature = angles[4 + part : 5 + part, :]
     base = lax.axis_index("space") * sz.slots
     shape = (sz.pair_pad, 128)
     zero = jnp.zeros(shape, jnp.float32)
@@ -134,7 +138,7 @@
         for p in range(2):
             full = rows_ref[pl.ds(i * ROWS + p * EACH, EACH), :]
             full = jnp.where(2 * index + p <= M, full, 0.0)
-            table[i, p] = full.astype(jnp.bfloat16)
+            table[i, p] = (full * quadrature).astype(jnp.bfloat16)
             turned = jnp.transpose(jnp.concatenate([full, blank], axis=0))
             table_t[i, p] = turned.astype(jnp.bfloat16)
 
@@ -151,15 +155,19 @@
     return copy
 
 
-def each_pair(sz, body, done=None):
-    def several(g, carry):
+def each_pair(sz, body, done=None, static=False):
+    def several(g, carry=0):
         for u in range(sz.step):
             body(g * sz.step + u, u)
         if done is not None:
             done(g)
         return carry
 
-    lax.fori_loop(0, sz.pairs // sz.step, several, 0)
+    if sz.loops == 1 or static:
+        for g in range(sz.loops):
+            several(g)
+    else:
+        lax.fori_loop(0, sz.loops, several, 0)
 
 
 def group_copy(source, target, sems, g, size):
@@ -178,6 +186,14 @@
     odd = jnp.bitwise_and(length, 1).astype(jnp.float32)
     sign_b = 1.0 - 2.0 * odd
     return wave_a, wave_b, length, r, in_a, k, sign_b
+
+
+def slot_offset(sz, part, slot):
+    lats = sz.part_lats[part]
+    at = slot * lats
+    if isinstance(at, int):
+        return at
+    return pl.multiple_of(at, 16 if sz.direct(part) else 8) if lats % 8 == 0 else at
 
 
 def send_rows(sz, part, i, state, facts, table_t, stage):
@@ -202,11 +218,12 @@
         north = plus[:, s * columns : (s + 1) * columns]
         south = minus[:, s * columns : (s + 1) * columns]
         south = south * sign_b if s == 1 else south
-        at = (2 * i + s) * sz.part_lats[part]
+        at = slot_offset(sz, part, 2 * i + s)
         for b in range(sz.half):
             lo = b * size
-            stage[b, pl.ds(at, size), :] = north[lo : lo + size]
-            stage[sz.space - 1 - b, pl.ds(at, size), :] = south[lo : lo + size]
+            kind = stage.dtype
+            stage[b, pl.ds(at, size), :] = north[lo : lo + size].astype(kind)
+            stage[sz.space - 1 - b, pl.ds(at, size), :] = south[lo : lo + size].astype(kind)
 
 
 def flush(sz, part, stage, send, target=None, sems=None):
@@ -224,11 +241,33 @@
             group_copy(send, target, sems, g, sz.bundle).wait()
 
 
+def rows_copy(sz, part, send, target, sems, g):
+    size = 2 * sz.step * sz.part_lats[part]
+    rows = pl.ds(g * size, size)
+    return pltpu.make_async_copy(send.at[:, rows, :], target.at[:, rows, :], sems.at[g])
+
+
+def send_pairs(sz, part, body, send, stage, target, sems, done):
+    if sz.direct(part):
+        def finish(g):
+            done(g)
+            rows_copy(sz, part, send, target, sems, g).start()
+
+        each_pair(sz, lambda i, u: body(i, u, send), finish, static=True)
+        for g in range(sz.loops):
+            rows_copy(sz, part, send, target, sems, g).wait()
+    else:
+        each_pair(sz, lambda i, u: body(i, u, stage), done)
+        flush(sz, part, stage, send, target, sems)
+
+
+def fetch_rows(sz, source, recv, sems):
+    for g in range(sz.bundles):
+        group_copy(source, recv, sems, g, sz.bundle).start()
+
+
 def load_rows(sz, part, recv, stage, source=None, sems=None):
     rows = sz.block_pad(part)
-    if source is not None:
-        for g in range(sz.bundles):
-            group_copy(source, recv, sems, g, sz.bundle).start()
 
     def body(g, _):
         if source is not None:
@@ -242,18 +281,17 @@
     lax.fori_loop(0, sz.bundles, body, 0)
 
 
-def change_rows(sz, part, i, facts, table, weights, stage):
+def change_rows(sz, part, i, facts, table, stage):
     in_a, sign_b = facts[4], facts[6]
-    w = weights[...]
     size = sz.part_pad
     plus, minus = [], []
     for s in range(2):
-        at = (2 * i + s) * sz.part_lats[part]
+        at = slot_offset(sz, part, 2 * i + s)
         north = jnp.concatenate([stage[b, pl.ds(at, size), :] for b in range(sz.half)], axis=0)
         south = jnp.concatenate(
             [stage[sz.space - 1 - b, pl.ds(at, size), :] for b in range(sz.half)], axis=0
         )
-        north, south = north * w, south * (w * sign_b if s == 1 else w)
+        south = south * sign_b if s == 1 else south
         plus.append((north + south).astype(jnp.bfloat16))
         minus.append((north - south).astype(jnp.bfloat16))
     pieces = []
@@ -301,13 +339,18 @@
     return out[:, :c] + out[:, c:]
 
 
+def inverse_of(x):
+    guess = pl.reciprocal(x, approx=True)
+    return guess * (2.0 - x * guess)
+
+
 def updated(state, change, facts, mixing, mixing_t, speeds):
     wave_a, wave_b, _, _, in_a, k = facts[:6]
     combined = state + change
     projected = dot_split(combined, mixing[...])
     n = (jnp.where(in_a, wave_a, wave_b) + k).astype(jnp.float32)
     stiffness = speeds[...] * (n * (n + 1.0))
-    weighted = projected * (stiffness / (1.0 + stiffness))
+    weighted = projected * (stiffness * inverse_of(1.0 + stiffness))
     returned = dot_split(weighted, mixing_t[...])
     return kept(combined - returned, facts)
 
@@ -333,7 +376,7 @@
     leaving = [move(table, table_hbm, one.at[1]), move(table_t, table_t_hbm, one.at[2])]
     arriving.wait()
 
-    def body(i, u):
+    def body(i, u, rows_out):
         facts = row_facts(sz, waves, i, columns)
         length, in_a = facts[2], facts[4]
         shifted[u, pl.ds(ROWS, M), :] = spectra[2 * i + 1]
@@ -347,12 +390,12 @@
         state = dot_split(jnp.concatenate(rows, axis=0), turn)
         state = kept(state, facts)
         state_ref[i] = state
-        send_rows(sz, 0, i, state, facts, table_t, stage)
-
-    each_pair(
-        sz, body, lambda g: group_copy(state_ref, state_hbm, state_sems, g, sz.step).start()
-    )
-    flush(sz, 0, stage, send, send_hbm, send_sems)
+        send_rows(sz, 0, i, state, facts, table_t, rows_out)
+
+    def state_out(g):
+        group_copy(state_ref, state_hbm, state_sems, g, sz.step).start()
+
+    send_pairs(sz, 0, body, send, stage, send_hbm, send_sems, state_out)
     for g in range(sz.loops):
         group_copy(state_ref, state_hbm, state_sems, g, sz.step).wait()
     for copy in leaving:
@@ -383,55 +426,60 @@
     flush(sz, part, stage, send, target, sems)
 
 
-def forward_kernel(sz, part, waves, state, recv, table, weights, out, stage):
+def forward_kernel(sz, part, waves, state, recv, table, out, stage):
     load_rows(sz, part, recv, stage)
 
     def body(i, u):
         facts = row_facts(sz, waves, i, state.shape[2])
-        out[i] = state[i] + change_rows(sz, part, i, facts, table, weights, stage)
+        out[i] = state[i] + change_rows(sz, part, i, facts, table, stage)
 
     each_pair(sz, body)
 
 
 def middle_kernel(
-    sz, waves, weights, mixing, mixing_t, speeds, partial_hbm, recv_hbm, table_hbm, table_t_hbm,
+    sz, waves, mixing, mixing_t, speeds, partial_hbm, recv_hbm, table_hbm, table_t_hbm,
     state_hbm, send_hbm,
     state_ref, recv, table, table_t, send, stage_in, stage, one, state_sems, recv_sems, send_sems,
 ):
     part = sz.parts - 1
     columns = state_ref.shape[2]
+    fetch_rows(sz, recv_hbm, recv, recv_sems)
     arriving = [
+        move(table_hbm, table, one.at[1]),
         move(partial_hbm, state_ref, one.at[0]),
-        move(table_hbm, table, one.at[1]),
         move(table_t_hbm, table_t, one.at[2]),
     ]
     load_rows(sz, part, recv, stage_in, recv_hbm, recv_sems)
     for copy in arriving:
         copy.wait()
 
-    def body(i, u):
+    def body(i, u, rows_out):
         facts = row_facts(sz, waves, i, columns)
-        change = change_rows(sz, part, i, facts, table, weights, stage_in)
+        change = change_rows(sz, part, i, facts, table, stage_in)
         state = updated(state_ref[i], change, facts, mixing, mixing_t, speeds)
         state_ref[i] = state
-        send_rows(sz, 0, i, state, facts, table_t, stage)
-
-    each_pair(
-        sz, body, lambda g: group_copy(state_ref, state_hbm, state_sems, g, sz.step).start()
-    )
-    flush(sz, 0, stage, send, send_hbm, send_sems)
+        send_rows(sz, 0, i, state, facts, table_t, rows_out)
+
+    def state_out(g):
+        group_copy(state_ref, state_hbm, state_sems, g, sz.step).start()
+
+    send_pairs(sz, 0, body, send, stage, send_hbm, send_sems, state_out)
     for g in range(sz.loops):
         group_copy(state_ref, state_hbm, state_sems, g, sz.step).wait()
 
 
 def last_kernel(
-    sz, waves, weights, mixing, mixing_t, speeds, partial_hbm, recv_hbm, table_hbm,
+    sz, waves, mixing, mixing_t, speeds, partial_hbm, recv_hbm, table_hbm,
     out_hbm,
     state_ref, recv, table, out, stage_in, mixed, one, out_sems, recv_sems,
 ):
     part = sz.parts - 1
     columns = state_ref.shape[2]
-    arriving = [move(partial_hbm, state_ref, one.at[0]), move(table_hbm, table, one.at[1])]
+    fetch_rows(sz, recv_hbm, recv, recv_sems)
+    arriving = [
+        move(table_hbm, table, one.at[1]),
+        move(partial_hbm, state_ref, one.at[0]),
+    ]
     mixed[...] = jnp.zeros_like(mixed)
     turn_t = turn_matrix(columns, back=True)
     load_rows(sz, part, recv, stage_in, recv_hbm, recv_sems)
@@ -442,7 +490,7 @@
         facts = row_facts(sz, waves, i, columns)
         wave_b, length = facts[1:3]
         r = lax.broadcasted_iota(jnp.int32, (M, columns), 0)
-        change = change_rows(sz, part, i, facts, table, weights, stage_in)
+        change = change_rows(sz, part, i, facts, table, stage_in)
         state = updated(state_ref[i], change, facts, mixing, mixing_t, speeds)
         state = dot_split(state, turn_t)
         for p in range(2):
@@ -616,14 +664,12 @@
     angles = np.zeros((16, 128), np.float32)
     angles[8:11] = np.pad(sectoral_logs(), (0, 3 * 128 - M)).reshape(3, 128)
     for part in range(sz.parts):
-        mine = colat[part * sz.part_rows : (part + 1) * sz.part_rows]
+        lanes = slice(part * sz.part_rows, (part + 1) * sz.part_rows)
+        mine = colat[lanes]
         angles[2 * part] = np.cos(mine)
         angles[2 * part + 1] = np.log2(np.sin(mine))
+        angles[4 + part] = np.sin(mine) * (math.pi / NLAT) * real[lanes]
     angles = jnp.asarray(angles)
-    weights = (np.sin(colat) * (math.pi / NLAT) * real).astype(np.float32)
-    weights = np.broadcast_to(weights[:, None], (sz.north, columns))
-    weights = [jnp.asarray(w) for w in np.split(weights, sz.parts)]
-
     same = np.kron(np.eye(columns // LEV, dtype=np.float32), np.ones((LEV, LEV), np.float32))
     mixing = split_matrix(jnp.tile(vertical_modes.T, (columns // LEV, columns // LEV)) * same)
     mixing_t = split_matrix(jnp.tile(vertical_modes, (columns // LEV, columns // LEV)) * same)
@@ -726,10 +772,10 @@
         back_1 = transpose(grid_stage(sz, 1, recv_1, traj[step, 1], synth, slope, scale))
         (partial,) = call(
             lambda s, *refs: forward_kernel(s, 0, *refs),
-            [state_shape], [wave_order], [state, back_0, table_0, weights[0]], [], [stages(0)],
+            [state_shape], [wave_order], [state, back_0, table_0], [], [stages(0)],
             5.0, "forward_part", away=False,
         )
-        near = [weights[1], mixing, mixing_t, speeds]
+        near = [mixing, mixing_t, speeds]
         if step < STEPS - 1:
             state, send_0 = call(
                 middle_kernel,
@@ -749,7 +795,7 @@
                 [
                     state_vmem, block_vmem(1), table_vmem[0],
                     pltpu.VMEM(spectra.shape, jnp.float32), stages(1), shift_vmem,
-                    dma(2), dma(sz.loops), dma(sz.bundles),
+                    dma(3), dma(sz.loops), dma(sz.bundles),
                 ],
                 10.0, "forward_last",
             )

time: 301 us -> 300 us (level)
    unnamed x56 -> x48, local copies, waits for them, and re-layouts: 11.9 us -> 11.3 us
  transfers between devices with their start and end apart: 12 -> 12, of which waited for: 9 -> 9; matrix products, arithmetic and copies ran while one was open for 7% -> 6% of each run, Pallas kernels for 23% -> 23%
where the time goes in v5:
time: 300 us; the launch traced here: 299 us
  waiting for transfers between devices  141 us (47%)
  Pallas kernels  84.7 us (28%)
  starting transfers between devices  42.5 us (14%)
  local copies, waits for them, and re-layouts  16 us (5%)
  other arithmetic  14 us (5%)
    all_to_all x8, waiting for transfers between devices, transpose(): return lax.all_to_all(value, 'space', 0, 0, tiled=True)  137 us
    pallas_call x4, Pallas kernels, grid_stage(): pl.pallas_call(lambda *refs: grid_kernel(sz, part, members, *refs), out_s...  44.5 us
    pallas_call x7, Pallas kernels, call(): pl.pallas_call(lambda *refs: body(sz, *refs), out_shape=tuple(outs), in_s...  40.2 us
    all_to_all x8, starting transfers between devices, transpose(): return lax.all_to_all(value, 'space', 0, 0, tiled=True)  39.6 us
    unnamed x48, local copies, waits for them, and re-layouts  11.3 us
    another operation x1, other arithmetic  7.51 us
  transfers between devices with their start and end apart: 12, of which 9 were waited for; matrix products, arithmetic and copies ran while one was open for 6% of the time, Pallas kernels for 23%

profile of v5, /device:TPU:15, one launch (start us, length us, event | category | flops | bytes accessed | tf_op | source)
XLA Modules:
  0.0 299.0 jit_solution(2355697028688676565)
XLA Ops:
  0.0 8.5 %tables_inverse.1 = (bf16[10,2,168,128]{3,2,1,0:T(8,128)(2,1)}, bf16[10,2,128,256]{3,2,1,0:T(8,128)(2,1)}, f32[10,336,128]{2,1,0:T(8,128)}, bf16[16,320,128]{2,1,0:T(8,128)(2,1)}) custom-call(s32[320]{0:T(512)} %refs_0_.13, f32[16,128]{1,0:T(8,128)} %constant.34.clone.refs_1_.refs_2_, f32[20,320,128]{2,1,0:T(8,128)} %refs_2_.2), custom_call_target="tpu_custom_call" | custom-call | flops 359999995904 | bytes 1048576 | tf_op jit(solution)/shard_map/tables_inverse/pallas_call | solution.py:700
  8.5 6.6 %all-to-all-start = ((bf16[16,320,128]{2,1,0:T(8,128)(2,1)}), bf16[16,320,128]{2,1,0:T(8,128)(2,1)}, u32[]{:S(2)}, u32[]{:S(2)}) async-start(bf16[16,320,128]{2,1,0:T(8,128)(2,1)} %get-tuple-element.17), calls=%async_computation | async-start | bytes 2621440 | tf_op jit(solution)/shard_map/all_to_all | solution.py:731
  28.6 7.4 %tables_inverse_rest.1 = (bf16[10,2,168,128]{3,2,1,0:T(8,128)(2,1)}, bf16[10,2,128,256]{3,2,1,0:T(8,128)(2,1)}, bf16[16,280,128]{2,1,0:T(8,128)(2,1)}) custom-call(s32[320]{0:T(512)} %refs_0_.13, f32[16,128]{1,0:T(8,128)} %constant.34.clone.refs_1_.refs_2_, f32[16,128]{1,0:T(8,128)} %constant.34.clone.refs_1_.refs_2_, ...), custom_call_target="tpu_custom_call" | custom-call | flops 240000008192 | bytes 1048576 | tf_op jit(solution)/shard_map/tables_inverse_rest/pallas_call | solution.py:700
  37.9 8.2 %all-to-all-done.refs_0_ = bf16[16,320,128]{2,1,0:T(8,128)(2,1)} async-done(((bf16[16,320,128]{2,1,0:T(8,128)(2,1)}), bf16[16,320,128]{2,1,0:T(8,128)(2,1)}, u32[]{:S(2)}, u32[]{:S(2)}) %all-to-all-start) | async-done | bytes 1310752 | tf_op jit(solution)/shard_map/all_to_all | solution.py:731
  46.0 4.6 %all-to-all-start.2 = ((bf16[16,280,128]{2,1,0:T(8,128)(2,1)}), bf16[16,280,128]{2,1,0:T(8,128)(2,1)}, u32[]{:S(2)}, u32[]{:S(2)}) async-start(bf16[16,280,128]{2,1,0:T(8,128)(2,1)} %get-tuple-element.21), calls=%async_computation.2 | async-start | bytes 2293760 | tf_op jit(solution)/shard_map/all_to_all | solution.py:731
  50.6 7.5 %multiply_convert_fusion.1 = (bf16[384,960]{1,0:T(8,128)(2,1)S(1)}, bf16[384,960]{1,0:T(8,128)(2,1)S(1)}, bf16[384,960]{1,0:T(8,128)(2,1)S(1)}, bf16[384,960]{1,0:T(8,128)(2,1)S(1)}) fusion(f32[384]{0:T(512)S(1)} %get-tuple-element.51, s32[384]{0:T(512)S(1)} %get-tuple-element.52, f32[384]{0:T(512)S(1)} %get-tuple-element.50), kind=kLoop, calls=%fused_computation.10 | loop fusion | flops 6635520 | bytes 2953728 | tf_op jit(solution)/shard_map/convert
  58.8 11.7 %grid_stage.4 = bf16[16,320,128]{2,1,0:T(8,128)(2,1)S(1)} custom-call(bf16[16,320,128]{2,1,0:T(8,128)(2,1)} %all-to-all-done.refs_0_, bf16[768,960]{1,0:T(8,128)(2,1)S(1)} %get-tuple-element.53.refs_1_, bf16[768,960]{1,0:T(8,128)(2,1)S(1)} %get-tuple-element.54.refs_2_, f32[320,128]{1,0:T(8,128)S(1)} %broadcast_in_dim.12.refs_3_, ...), custom_call_target="tpu_custom_call" | custom-call | flops 269999996928 | bytes 1048576 | tf_op jit(solution)/shard_map/grid_stage/pallas_call | solution.py:608
  71.5 6.5 %all-to-all-done.2.refs_0_ = bf16[16,280,128]{2,1,0:T(8,128)(2,1)} async-done(((bf16[16,280,128]{2,1,0:T(8,128)(2,1)}), bf16[16,280,128]{2,1,0:T(8,128)(2,1)}, u32[]{:S(2)}, u32[]{:S(2)}) %all-to-all-start.2) | async-done | bytes 1146912 | tf_op jit(solution)/shard_map/all_to_all | solution.py:731
  78.1 4.6 %all-to-all-start.1 = ((bf16[16,320,128]{2,1,0:T(8,128)(2,1)}), bf16[16,320,128]{2,1,0:T(8,128)(2,1)}, u32[]{:S(2)}, u32[]{:S(2)}) async-start(bf16[16,320,128]{2,1,0:T(8,128)(2,1)} %copy-done.5), calls=%async_computation.1 | async-start | bytes 2621440 | tf_op jit(solution)/shard_map/all_to_all | solution.py:731
  86.9 11.1 %grid_stage.5 = bf16[16,280,128]{2,1,0:T(8,128)(2,1)} custom-call(bf16[16,280,128]{2,1,0:T(8,128)(2,1)} %all-to-all-done.2.refs_0_, bf16[768,960]{1,0:T(8,128)(2,1)} %copy-done, bf16[768,960]{1,0:T(8,128)(2,1)} %copy-done.2, f32[320,128]{1,0:T(8,128)S(1)} %broadcast_in_dim.12.refs_3_, bf16[14,3,16,960]{3,2,1,0:T(8,128)(2,1)} %maximum_bitcast_fusion.2.refs_4_, ...), custom_call_target="tpu_custom_call" | custom-call | flops 269999996928 | bytes 1048576 | tf_op jit(solution)/shard_map/grid_stage/pallas_call | solution.py:608
  98.0 15.5 %all-to-all-done.1.refs_2_ = bf16[16,320,128]{2,1,0:T(8,128)(2,1)} async-done(((bf16[16,320,128]{2,1,0:T(8,128)(2,1)}), bf16[16,320,128]{2,1,0:T(8,128)(2,1)}, u32[]{:S(2)}, u32[]{:S(2)}) %all-to-all-start.1) | async-done | bytes 1310752 | tf_op jit(solution)/shard_map/all_to_all | solution.py:731
  123.2 22.4 %all-to-all-done.3.refs_5_ = bf16[16,280,128]{2,1,0:T(8,128)(2,1)} async-done(((bf16[16,280,128]{2,1,0:T(8,128)(2,1)}), bf16[16,280,128]{2,1,0:T(8,128)(2,1)}, u32[]{:S(2)}, u32[]{:S(2)}) %all-to-all-start.3) | async-done | bytes 1146912 | tf_op jit(solution)/shard_map/all_to_all | solution.py:731
  145.6 9.3 %forward_inverse.1 = (f32[10,336,128]{2,1,0:T(8,128)}, bf16[16,320,128]{2,1,0:T(8,128)(2,1)}) custom-call(s32[320]{0:T(512)} %refs_0_.13, bf16[256,256]{1,0:T(8,128)(2,1)} %get-tuple-element.57.refs_1_, bf16[256,256]{1,0:T(8,128)(2,1)} %get-tuple-element.58.refs_2_, f32[1,128]{1,0:T(1,128)} %broadcast_in_dim_tile.3.refs_3_, f32[10,336,128]{2,1,0:T(8,128)} %copy-done.15, ...), custom_call_target="tpu_custom_call" | custom-call | flops 359999995904 | bytes 1048576 | tf_op jit(solution)/shard_map/forward_inverse/pallas_call | solution.py:700
  155.0 4.7 %all-to-all-start.4 = ((bf16[16,320,128]{2,1,0:T(8,128)(2,1)}), bf16[16,320,128]{2,1,0:T(8,128)(2,1)}, u32[]{:S(2)}, u32[]{:S(2)}) async-start(bf16[16,320,128]{2,1,0:T(8,128)(2,1)} %get-tuple-element.25), calls=%async_computation.4 | async-start | bytes 2621440 | tf_op jit(solution)/shard_map/all_to_all | solution.py:731
  163.6 26.8 %all-to-all-done.4.refs_0_ = bf16[16,320,128]{2,1,0:T(8,128)(2,1)} async-done(((bf16[16,320,128]{2,1,0:T(8,128)(2,1)}), bf16[16,320,128]{2,1,0:T(8,128)(2,1)}, u32[]{:S(2)}, u32[]{:S(2)}) %all-to-all-start.4) | async-done | bytes 1310752 | tf_op jit(solution)/shard_map/all_to_all | solution.py:731
  190.4 4.9 %all-to-all-start.6 = ((bf16[16,280,128]{2,1,0:T(8,128)(2,1)}), bf16[16,280,128]{2,1,0:T(8,128)(2,1)}, u32[]{:S(2)}, u32[]{:S(2)}) async-start(bf16[16,280,128]{2,1,0:T(8,128)(2,1)} %copy-done.6), calls=%async_computation.6 | async-start | bytes 2293760 | tf_op jit(solution)/shard_map/all_to_all | solution.py:731
  195.2 10.7 %grid_stage.6 = bf16[16,320,128]{2,1,0:T(8,128)(2,1)S(1)} custom-call(bf16[16,320,128]{2,1,0:T(8,128)(2,1)} %all-to-all-done.4.refs_0_, bf16[768,960]{1,0:T(8,128)(2,1)S(1)} %copy-done.1, bf16[768,960]{1,0:T(8,128)(2,1)S(1)} %copy-done.3, f32[320,128]{1,0:T(8,128)S(1)} %broadcast_in_dim.12.refs_3_, bf16[16,3,16,960]{3,2,1,0:T(8,128)(2,1)} %maximum_bitcast_fusion.1.refs_4_, ...), custom_call_target="tpu_custom_call" | custom-call | flops 269999996928 | bytes 1048576 | tf_op jit(solution)/shard_map/grid_stage/pallas_call | solution.py:608
  207.0 15.4 %all-to-all-done.6.refs_0_ = bf16[16,280,128]{2,1,0:T(8,128)(2,1)} async-done(((bf16[16,280,128]{2,1,0:T(8,128)(2,1)}), bf16[16,280,128]{2,1,0:T(8,128)(2,1)}, u32[]{:S(2)}, u32[]{:S(2)}) %all-to-all-start.6) | async-done | bytes 1146912 | tf_op jit(solution)/shard_map/all_to_all | solution.py:731
  222.4 4.9 %all-to-all-start.5 = ((bf16[16,320,128]{2,1,0:T(8,128)(2,1)}), bf16[16,320,128]{2,1,0:T(8,128)(2,1)}, u32[]{:S(2)}, u32[]{:S(2)}) async-start(bf16[16,320,128]{2,1,0:T(8,128)(2,1)} %copy-done.4), calls=%async_computation.5 | async-start | bytes 2621440 | tf_op jit(solution)/shard_map/all_to_all | solution.py:731
  227.3 11.1 %grid_stage.7 = bf16[16,280,128]{2,1,0:T(8,128)(2,1)} custom-call(bf16[16,280,128]{2,1,0:T(8,128)(2,1)} %all-to-all-done.6.refs_0_, bf16[768,960]{1,0:T(8,128)(2,1)} %copy-done, bf16[768,960]{1,0:T(8,128)(2,1)} %copy-done.2, f32[320,128]{1,0:T(8,128)S(1)} %broadcast_in_dim.12.refs_3_, bf16[14,3,16,960]{3,2,1,0:T(8,128)(2,1)} %maximum_bitcast_fusion.3.refs_4_, ...), custom_call_target="tpu_custom_call" | custom-call | flops 269999996928 | bytes 1048576 | tf_op jit(solution)/shard_map/grid_stage/pallas_call | solution.py:608
  238.4 19.6 %all-to-all-done.5.refs_2_ = bf16[16,320,128]{2,1,0:T(8,128)(2,1)} async-done(((bf16[16,320,128]{2,1,0:T(8,128)(2,1)}), bf16[16,320,128]{2,1,0:T(8,128)(2,1)}, u32[]{:S(2)}, u32[]{:S(2)}) %all-to-all-start.5) | async-done | bytes 1310752 | tf_op jit(solution)/shard_map/all_to_all | solution.py:731
  257.9 4.9 %all-to-all-start.7 = ((bf16[16,280,128]{2,1,0:T(8,128)(2,1)}), bf16[16,280,128]{2,1,0:T(8,128)(2,1)}, u32[]{:S(2)}, u32[]{:S(2)}) async-start(bf16[16,280,128]{2,1,0:T(8,128)(2,1)} %grid_stage.7), calls=%async_computation.7 | async-start | bytes 2293760 | tf_op jit(solution)/shard_map/all_to_all | solution.py:731
  267.5 22.4 %all-to-all-done.7.refs_5_ = bf16[16,280,128]{2,1,0:T(8,128)(2,1)} async-done(((bf16[16,280,128]{2,1,0:T(8,128)(2,1)}), bf16[16,280,128]{2,1,0:T(8,128)(2,1)}, u32[]{:S(2)}, u32[]{:S(2)}) %all-to-all-start.7) | async-done | bytes 1146912 | tf_op jit(solution)/shard_map/all_to_all | solution.py:731
  289.9 8.8 %forward_last.1 = f32[20,320,128]{2,1,0:T(8,128)} custom-call(s32[320]{0:T(512)} %refs_0_.13, bf16[256,256]{1,0:T(8,128)(2,1)} %get-tuple-element.57.refs_1_, bf16[256,256]{1,0:T(8,128)(2,1)} %get-tuple-element.58.refs_2_, f32[1,128]{1,0:T(1,128)} %broadcast_in_dim_tile.3.refs_3_, f32[10,336,128]{2,1,0:T(8,128)} %copy-done.16, ...), custom_call_target="tpu_custom_call" | custom-call | flops 299999985664 | bytes 1048576 | tf_op jit(solution)/shard_map/forward_last/pallas_call | solution.py:700
  (84 shorter events, 40.4 us)
Async XLA Ops:
  8.5 37.5 %all-to-all-start = ((bf16[16,320,128]{2,1,0:T(8,128)(2,1)}), bf16[16,320,128]{2,1,0:T(8,128)(2,1)}, u32[]{:S(2)}, u32[]{:S(2)}) async-start(bf16[16,320,128]{2,1,0:T(8,128)(2,1)} %get-tuple-element.17), calls=%async_computation | async-start | bytes 2621440 | tf_op jit(solution)/shard_map/all_to_all | solution.py:731
  21.5 37.2 %collective-permute-start = (bf16[16,3,16,960]{3,2,1,0:T(8,128)(2,1)}, bf16[16,3,16,960]{3,2,1,0:T(8,128)(2,1)}, u32[]{:S(2)}, u32[]{:S(2)}) collective-permute-start(bf16[16,3,16,960]{3,2,1,0:T(8,128)(2,1)} %maximum_bitcast_fusion.refs_4_), channel_id=1, source_target_pairs={{0,16},{16,0},{1,17},{17,1},{2,18},{18,2},{3,19},{19,3},{4,20},{20... | collective-permute-start | bytes 4423688 | tf_op jit(solution)/shard_map/ppermute | solution.py:715
  23.1 63.8 %collective-permute-start.1 = (bf16[14,3,16,960]{3,2,1,0:T(8,128)(2,1)}, bf16[14,3,16,960]{3,2,1,0:T(8,128)(2,1)}, u32[]{:S(2)}, u32[]{:S(2)}) collective-permute-start(bf16[14,3,16,960]{3,2,1,0:T(8,128)(2,1)} %maximum_bitcast_fusion.2.refs_4_), channel_id=1, source_target_pairs={{0,16},{16,0},{1,17},{17,1},{2,18},{18,2},{3,19},{19,3},{4,20},{20... | collective-permute-start | bytes 3870728 | tf_op jit(solution)/shard_map/ppermute | solution.py:715
  25.8 169.5 %collective-permute-start.2 = (bf16[16,3,16,960]{3,2,1,0:T(8,128)(2,1)}, bf16[16,3,16,960]{3,2,1,0:T(8,128)(2,1)}, u32[]{:S(2)}, u32[]{:S(2)}) collective-permute-start(bf16[16,3,16,960]{3,2,1,0:T(8,128)(2,1)} %maximum_bitcast_fusion.1.refs_4_), channel_id=1, source_target_pairs={{0,16},{16,0},{1,17},{17,1},{2,18},{18,2},{3,19},{19,3},{4,20},{20... | collective-permute-start | bytes 4423688 | tf_op jit(solution)/shard_map/ppermute | solution.py:715
  27.3 199.9 %collective-permute-start.3 = (bf16[14,3,16,960]{3,2,1,0:T(8,128)(2,1)}, bf16[14,3,16,960]{3,2,1,0:T(8,128)(2,1)}, u32[]{:S(2)}, u32[]{:S(2)}) collective-permute-start(bf16[14,3,16,960]{3,2,1,0:T(8,128)(2,1)} %maximum_bitcast_fusion.3.refs_4_), channel_id=1, source_target_pairs={{0,16},{16,0},{1,17},{17,1},{2,18},{18,2},{3,19},{19,3},{4,20},{20... | collective-permute-start | bytes 3870728 | tf_op jit(solution)/shard_map/ppermute | solution.py:715
  28.6 7.5 %copy-start.21 = (f32[32,32]{1,0:T(8,128)S(1)}, f32[32,32]{1,0:T(8,128)}, u32[]{:S(2)}) copy-start(f32[32,32]{1,0:T(8,128)} %param.12) | copy-start | bytes 12292
  28.6 7.5 %copy-start.20 = (f32[4,32,4,32]{3,2,1,0:T(4,128)S(1)}, f32[4,32,4,32]{3,2,1,0:T(4,128)}, u32[]{:S(2)}) copy-start(f32[4,32,4,32]{3,2,1,0:T(4,128)} %constant.45) | copy-start | bytes 196612
  28.6 8.0 %copy-start.22 = (f32[32]{0:T(128)S(1)}, f32[32]{0:T(128)}, u32[]{:S(2)}) copy-start(f32[32]{0:T(128)} %param.13) | copy-start | bytes 388
  36.4 14.3 %copy-start.7 = (s32[320]{0:T(512)S(1)}, s32[320]{0:T(512)}, u32[]{:S(2)}) copy-start(s32[320]{0:T(512)} %refs_0_.13) | copy-start | bytes 3844
  46.0 32.0 %all-to-all-start.2 = ((bf16[16,280,128]{2,1,0:T(8,128)(2,1)}), bf16[16,280,128]{2,1,0:T(8,128)(2,1)}, u32[]{:S(2)}, u32[]{:S(2)}) async-start(bf16[16,280,128]{2,1,0:T(8,128)(2,1)} %get-tuple-element.21), calls=%async_computation.2 | async-start | bytes 2293760 | tf_op jit(solution)/shard_map/all_to_all | solution.py:731
  58.6 11.8 %copy-start = (bf16[768,960]{1,0:T(8,128)(2,1)}, bf16[768,960]{1,0:T(8,128)(2,1)S(1)}, u32[]{:S(2)}) copy-start(bf16[768,960]{1,0:T(8,128)(2,1)S(1)} %get-tuple-element.53.refs_1_) | copy-start | bytes 4423684
  58.6 11.8 %copy-start.2 = (bf16[768,960]{1,0:T(8,128)(2,1)}, bf16[768,960]{1,0:T(8,128)(2,1)S(1)}, u32[]{:S(2)}) copy-start(bf16[768,960]{1,0:T(8,128)(2,1)S(1)} %get-tuple-element.54.refs_2_) | copy-start | bytes 4423684
  78.1 35.5 %all-to-all-start.1 = ((bf16[16,320,128]{2,1,0:T(8,128)(2,1)}), bf16[16,320,128]{2,1,0:T(8,128)(2,1)}, u32[]{:S(2)}, u32[]{:S(2)}) async-start(bf16[16,320,128]{2,1,0:T(8,128)(2,1)} %copy-done.5), calls=%async_computation.1 | async-start | bytes 2621440 | tf_op jit(solution)/shard_map/all_to_all | solution.py:731
  98.0 20.1 %copy-start.8 = (s32[320]{0:T(512)S(1)}, s32[320]{0:T(512)}, u32[]{:S(2)}) copy-start(s32[320]{0:T(512)} %refs_0_.13) | copy-start | bytes 3844
  98.0 20.1 %copy-start.17 = (bf16[10,2,168,128]{3,2,1,0:T(8,128)(2,1)S(1)}, bf16[10,2,168,128]{3,2,1,0:T(8,128)(2,1)}, u32[]{:S(2)}) copy-start(bf16[10,2,168,128]{3,2,1,0:T(8,128)(2,1)} %get-tuple-element.20.refs_3_) | copy-start | bytes 2580484
  113.6 32.0 %all-to-all-start.3 = ((bf16[16,280,128]{2,1,0:T(8,128)(2,1)}), bf16[16,280,128]{2,1,0:T(8,128)(2,1)}, u32[]{:S(2)}, u32[]{:S(2)}) async-start(bf16[16,280,128]{2,1,0:T(8,128)(2,1)} %grid_stage.5), calls=%async_computation.3 | async-start | bytes 2293760 | tf_op jit(solution)/shard_map/all_to_all | solution.py:731
  155.0 35.4 %all-to-all-start.4 = ((bf16[16,320,128]{2,1,0:T(8,128)(2,1)}), bf16[16,320,128]{2,1,0:T(8,128)(2,1)}, u32[]{:S(2)}, u32[]{:S(2)}) async-start(bf16[16,320,128]{2,1,0:T(8,128)(2,1)} %get-tuple-element.25), calls=%async_computation.4 | async-start | bytes 2621440 | tf_op jit(solution)/shard_map/all_to_all | solution.py:731
  161.2 34.1 %copy-start.3 = (bf16[768,960]{1,0:T(8,128)(2,1)S(1)}, bf16[768,960]{1,0:T(8,128)(2,1)}, u32[]{:S(2)}) copy-start(bf16[768,960]{1,0:T(8,128)(2,1)} %copy-done.2) | copy-start | bytes 4423684
  163.6 31.7 %copy-start.1 = (bf16[768,960]{1,0:T(8,128)(2,1)S(1)}, bf16[768,960]{1,0:T(8,128)(2,1)}, u32[]{:S(2)}) copy-start(bf16[768,960]{1,0:T(8,128)(2,1)} %copy-done) | copy-start | bytes 4423684
  190.4 32.0 %all-to-all-start.6 = ((bf16[16,280,128]{2,1,0:T(8,128)(2,1)}), bf16[16,280,128]{2,1,0:T(8,128)(2,1)}, u32[]{:S(2)}, u32[]{:S(2)}) async-start(bf16[16,280,128]{2,1,0:T(8,128)(2,1)} %copy-done.6), calls=%async_computation.6 | async-start | bytes 2293760 | tf_op jit(solution)/shard_map/all_to_all | solution.py:731
  222.4 35.5 %all-to-all-start.5 = ((bf16[16,320,128]{2,1,0:T(8,128)(2,1)}), bf16[16,320,128]{2,1,0:T(8,128)(2,1)}, u32[]{:S(2)}, u32[]{:S(2)}) async-start(bf16[16,320,128]{2,1,0:T(8,128)(2,1)} %copy-done.4), calls=%async_computation.5 | async-start | bytes 2621440 | tf_op jit(solution)/shard_map/all_to_all | solution.py:731
  238.3 24.4 %copy-start.10 = (s32[320]{0:T(512)S(1)}, s32[320]{0:T(512)}, u32[]{:S(2)}) copy-start(s32[320]{0:T(512)} %refs_0_.13) | copy-start | bytes 3844
  238.4 24.4 %copy-start.12 = (f32[10,336,128]{2,1,0:T(8,128)S(1)}, f32[10,336,128]{2,1,0:T(8,128)}, u32[]{:S(2)}) copy-start(f32[10,336,128]{2,1,0:T(8,128)} %get-tuple-element.24.refs_1_) | copy-start | bytes 5160964
  257.9 32.0 %all-to-all-start.7 = ((bf16[16,280,128]{2,1,0:T(8,128)(2,1)}), bf16[16,280,128]{2,1,0:T(8,128)(2,1)}, u32[]{:S(2)}, u32[]{:S(2)}) async-start(bf16[16,280,128]{2,1,0:T(8,128)(2,1)} %grid_stage.7), calls=%async_computation.7 | async-start | bytes 2293760 | tf_op jit(solution)/shard_map/all_to_all | solution.py:731
  (11 other events, 20.7 us)

commit v6 on v5

--- a/solution.py
+++ b/solution.py
@@ -16,6 +16,7 @@
 STEPS = 2
 ROWS = 336
 EACH = ROWS // 2
+SPAN = 16
 SHIFTED = 2 * ROWS
 UNROLL = 5
 DEPTH = 384
@@ -101,14 +102,14 @@
 
     def body(block, carry):
         cur, prev, shift, inv_prev = carry
-        second = (block * 8).astype(jnp.float32) > length
+        second = (block * SPAN).astype(jnp.float32) > length
         big = jnp.maximum(jnp.abs(cur), jnp.abs(prev)) > BIG
         scale = jnp.where(big, 1.0 / BIG, 1.0)
         cur, prev = cur * scale, prev * scale
         shift = shift + jnp.where(big, 32.0, 0.0)
         factor = jnp.exp2(0.5 * (jnp.where(second, start_b, start_a) + shift))
-        for j in range(8):
-            r = (block * 8 + j).astype(jnp.float32)
+        for j in range(SPAN):
+            r = (block * SPAN + j).astype(jnp.float32)
             fresh = r == length
             begin = jnp.logical_or(fresh, r == 0.0)
             in_b = r >= length
@@ -126,11 +127,11 @@
             cur = jnp.where(begin, 1.0, new)
             shift = jnp.where(fresh, 0.0, shift)
             factor = jnp.where(fresh, base_b, factor)
-            at = (j % 2) * EACH + block * 4 + j // 2
+            at = (j % 2) * EACH + block * (SPAN // 2) + j // 2
             rows_ref[pl.ds(at, sz.pair_pad, stride=ROWS), :] = (cur * factor) * factor
         return cur, prev, shift, inv_prev
 
-    lax.fori_loop(0, ROWS // 8, body, (zero, zero, zero, zero))
+    lax.fori_loop(0, ROWS // SPAN, body, (zero, zero, zero, zero))
     index = lax.broadcasted_iota(jnp.int32, (EACH, 128), 0)
     blank = jnp.zeros((256 - EACH, 128), jnp.float32)
 
@@ -257,7 +258,7 @@
         for g in range(sz.loops):
             rows_copy(sz, part, send, target, sems, g).wait()
     else:
-        each_pair(sz, lambda i, u: body(i, u, stage), done)
+        each_pair(sz, lambda i, u: body(i, u, stage), done, static=True)
         flush(sz, part, stage, send, target, sems)
 
 
@@ -439,25 +440,29 @@
 def middle_kernel(
     sz, waves, mixing, mixing_t, speeds, partial_hbm, recv_hbm, table_hbm, table_t_hbm,
     state_hbm, send_hbm,
-    state_ref, recv, table, table_t, send, stage_in, stage, one, state_sems, recv_sems, send_sems,
+    state_ref, recv, table, table_t, send, stage_in, stage, one, part_sems, state_sems, recv_sems, send_sems,
 ):
     part = sz.parts - 1
     columns = state_ref.shape[2]
     fetch_rows(sz, recv_hbm, recv, recv_sems)
-    arriving = [
-        move(table_hbm, table, one.at[1]),
-        move(partial_hbm, state_ref, one.at[0]),
-        move(table_t_hbm, table_t, one.at[2]),
-    ]
+    early = move(table_hbm, table, one.at[1])
+    late = pltpu.make_async_copy(table_t_hbm, table_t, one.at[2])
+    group_copy(partial_hbm, state_ref, part_sems, 0, sz.step).start()
+    late.start()
+    for g in range(1, sz.loops):
+        group_copy(partial_hbm, state_ref, part_sems, g, sz.step).start()
     load_rows(sz, part, recv, stage_in, recv_hbm, recv_sems)
-    for copy in arriving:
-        copy.wait()
+    early.wait()
 
     def body(i, u, rows_out):
+        if u == 0:
+            group_copy(partial_hbm, state_ref, part_sems, i // sz.step, sz.step).wait()
         facts = row_facts(sz, waves, i, columns)
         change = change_rows(sz, part, i, facts, table, stage_in)
         state = updated(state_ref[i], change, facts, mixing, mixing_t, speeds)
         state_ref[i] = state
+        if isinstance(i, int) and i == 0:
+            late.wait()
         send_rows(sz, 0, i, state, facts, table_t, rows_out)
 
     def state_out(g):
@@ -471,22 +476,22 @@
 def last_kernel(
     sz, waves, mixing, mixing_t, speeds, partial_hbm, recv_hbm, table_hbm,
     out_hbm,
-    state_ref, recv, table, out, stage_in, mixed, one, out_sems, recv_sems,
+    state_ref, recv, table, out, stage_in, mixed, one, part_sems, out_sems, recv_sems,
 ):
     part = sz.parts - 1
     columns = state_ref.shape[2]
     fetch_rows(sz, recv_hbm, recv, recv_sems)
-    arriving = [
-        move(table_hbm, table, one.at[1]),
-        move(partial_hbm, state_ref, one.at[0]),
-    ]
+    early = move(table_hbm, table, one.at[1])
+    for g in range(sz.loops):
+        group_copy(partial_hbm, state_ref, part_sems, g, sz.step).start()
     mixed[...] = jnp.zeros_like(mixed)
     turn_t = turn_matrix(columns, back=True)
     load_rows(sz, part, recv, stage_in, recv_hbm, recv_sems)
-    for copy in arriving:
-        copy.wait()
+    early.wait()
 
     def body(i, u):
+        if u == 0:
+            group_copy(partial_hbm, state_ref, part_sems, i // sz.step, sz.step).wait()
         facts = row_facts(sz, waves, i, columns)
         wave_b, length = facts[1:3]
         r = lax.broadcasted_iota(jnp.int32, (M, columns), 0)
@@ -499,7 +504,10 @@
         out[2 * i + 1] = jnp.where(r < M - wave_b, mixed[u, pl.ds(length, M), :], 0.0)
 
     each_pair(
-        sz, body, lambda g: group_copy(out, out_hbm, out_sems, g, 2 * sz.step).start()
+        sz,
+        body,
+        lambda g: group_copy(out, out_hbm, out_sems, g, 2 * sz.step).start(),
+        static=True,
     )
     for g in range(sz.loops):
         group_copy(out, out_hbm, out_sems, g, 2 * sz.step).wait()
@@ -783,7 +791,8 @@
                 [wave_order], near, [partial, back_1, table_1, table_t_0],
                 [
                     state_vmem, block_vmem(1), *table_vmem, block_vmem(0), stages(1), stages(0),
-                    dma(3), dma(sz.loops), dma(sz.bundles), dma(sz.bundles),
+                    dma(3), dma(sz.loops), dma(sz.loops), dma(sz.bundles),
+                    dma(sz.bundles),
                 ],
                 12.0, "forward_inverse",
             )
@@ -795,7 +804,7 @@
                 [
                     state_vmem, block_vmem(1), table_vmem[0],
                     pltpu.VMEM(spectra.shape, jnp.float32), stages(1), shift_vmem,
-                    dma(3), dma(sz.loops), dma(sz.bundles),
+                    dma(2), dma(sz.loops), dma(sz.loops), dma(sz.bundles),
                 ],
                 10.0, "forward_last",
             )

time: 300 us -> 299 us (level)
  transfers between devices with their start and end apart: 12 -> 12, of which waited for: 9 -> 9; matrix products, arithmetic and copies ran while one was open for 6% -> 6% of each run, Pallas kernels for 23% -> 22%
where the time goes in v6:
time: 299 us; the launch traced here: 298 us
  waiting for transfers between devices  141 us (47%)
  Pallas kernels  83.4 us (28%)
  starting transfers between devices  42.7 us (14%)
  local copies, waits for them, and re-layouts  16 us (5%)
  other arithmetic  14 us (5%)
    all_to_all x8, waiting for transfers between devices, transpose(): return lax.all_to_all(value, 'space', 0, 0, tiled=True)  137 us
    pallas_call x4, Pallas kernels, grid_stage(): pl.pallas_call(lambda *refs: grid_kernel(sz, part, members, *refs), out_s...  44.5 us
    all_to_all x8, starting transfers between devices, transpose(): return lax.all_to_all(value, 'space', 0, 0, tiled=True)  39.8 us
    pallas_call x7, Pallas kernels, call(): pl.pallas_call(lambda *refs: body(sz, *refs), out_shape=tuple(outs), in_s...  38.8 us
    unnamed x48, local copies, waits for them, and re-layouts  11.3 us
    another operation x1, other arithmetic  7.51 us
  transfers between devices with their start and end apart: 12, of which 9 were waited for; matrix products, arithmetic and copies ran while one was open for 6% of the time, Pallas kernels for 22%

profile of v6, /device:TPU:15, one launch (start us, length us, event | category | flops | bytes accessed | tf_op | source)
XLA Modules:
  0.0 298.1 jit_solution(11409570061191920697)
XLA Ops:
  0.0 8.2 %tables_inverse.1 = (bf16[10,2,168,128]{3,2,1,0:T(8,128)(2,1)}, bf16[10,2,128,256]{3,2,1,0:T(8,128)(2,1)}, f32[10,336,128]{2,1,0:T(8,128)}, bf16[16,320,128]{2,1,0:T(8,128)(2,1)}) custom-call(s32[320]{0:T(512)} %refs_0_.13, f32[16,128]{1,0:T(8,128)} %constant.34.clone.refs_1_.refs_2_, f32[20,320,128]{2,1,0:T(8,128)} %refs_2_.2), custom_call_target="tpu_custom_call" | custom-call | flops 359999995904 | bytes 1048576 | tf_op jit(solution)/shard_map/tables_inverse/pallas_call | solution.py:708
  8.2 6.6 %all-to-all-start = ((bf16[16,320,128]{2,1,0:T(8,128)(2,1)}), bf16[16,320,128]{2,1,0:T(8,128)(2,1)}, u32[]{:S(2)}, u32[]{:S(2)}) async-start(bf16[16,320,128]{2,1,0:T(8,128)(2,1)} %get-tuple-element.17), calls=%async_computation | async-start | bytes 2621440 | tf_op jit(solution)/shard_map/all_to_all | solution.py:739
  28.2 7.2 %tables_inverse_rest.1 = (bf16[10,2,168,128]{3,2,1,0:T(8,128)(2,1)}, bf16[10,2,128,256]{3,2,1,0:T(8,128)(2,1)}, bf16[16,280,128]{2,1,0:T(8,128)(2,1)}) custom-call(s32[320]{0:T(512)} %refs_0_.13, f32[16,128]{1,0:T(8,128)} %constant.34.clone.refs_1_.refs_2_, f32[16,128]{1,0:T(8,128)} %constant.34.clone.refs_1_.refs_2_, ...), custom_call_target="tpu_custom_call" | custom-call | flops 240000008192 | bytes 1048576 | tf_op jit(solution)/shard_map/tables_inverse_rest/pallas_call | solution.py:708
  37.3 8.4 %all-to-all-done.refs_0_ = bf16[16,320,128]{2,1,0:T(8,128)(2,1)} async-done(((bf16[16,320,128]{2,1,0:T(8,128)(2,1)}), bf16[16,320,128]{2,1,0:T(8,128)(2,1)}, u32[]{:S(2)}, u32[]{:S(2)}) %all-to-all-start) | async-done | bytes 1310752 | tf_op jit(solution)/shard_map/all_to_all | solution.py:739
  45.7 4.6 %all-to-all-start.2 = ((bf16[16,280,128]{2,1,0:T(8,128)(2,1)}), bf16[16,280,128]{2,1,0:T(8,128)(2,1)}, u32[]{:S(2)}, u32[]{:S(2)}) async-start(bf16[16,280,128]{2,1,0:T(8,128)(2,1)} %get-tuple-element.21), calls=%async_computation.2 | async-start | bytes 2293760 | tf_op jit(solution)/shard_map/all_to_all | solution.py:739
  50.3 7.5 %multiply_convert_fusion.1 = (bf16[384,960]{1,0:T(8,128)(2,1)S(1)}, bf16[384,960]{1,0:T(8,128)(2,1)S(1)}, bf16[384,960]{1,0:T(8,128)(2,1)S(1)}, bf16[384,960]{1,0:T(8,128)(2,1)S(1)}) fusion(f32[384]{0:T(512)S(1)} %get-tuple-element.51, s32[384]{0:T(512)S(1)} %get-tuple-element.52, f32[384]{0:T(512)S(1)} %get-tuple-element.50), kind=kLoop, calls=%fused_computation.10 | loop fusion | flops 6635520 | bytes 2953728 | tf_op jit(solution)/shard_map/convert
  58.4 11.7 %grid_stage.4 = bf16[16,320,128]{2,1,0:T(8,128)(2,1)S(1)} custom-call(bf16[16,320,128]{2,1,0:T(8,128)(2,1)} %all-to-all-done.refs_0_, bf16[768,960]{1,0:T(8,128)(2,1)S(1)} %get-tuple-element.53.refs_1_, bf16[768,960]{1,0:T(8,128)(2,1)S(1)} %get-tuple-element.54.refs_2_, f32[320,128]{1,0:T(8,128)S(1)} %broadcast_in_dim.12.refs_3_, ...), custom_call_target="tpu_custom_call" | custom-call | flops 269999996928 | bytes 1048576 | tf_op jit(solution)/shard_map/grid_stage/pallas_call | solution.py:616
  71.2 6.5 %all-to-all-done.2.refs_0_ = bf16[16,280,128]{2,1,0:T(8,128)(2,1)} async-done(((bf16[16,280,128]{2,1,0:T(8,128)(2,1)}), bf16[16,280,128]{2,1,0:T(8,128)(2,1)}, u32[]{:S(2)}, u32[]{:S(2)}) %all-to-all-start.2) | async-done | bytes 1146912 | tf_op jit(solution)/shard_map/all_to_all | solution.py:739
  77.7 4.8 %all-to-all-start.1 = ((bf16[16,320,128]{2,1,0:T(8,128)(2,1)}), bf16[16,320,128]{2,1,0:T(8,128)(2,1)}, u32[]{:S(2)}, u32[]{:S(2)}) async-start(bf16[16,320,128]{2,1,0:T(8,128)(2,1)} %copy-done.5), calls=%async_computation.1 | async-start | bytes 2621440 | tf_op jit(solution)/shard_map/all_to_all | solution.py:739
  86.6 11.1 %grid_stage.5 = bf16[16,280,128]{2,1,0:T(8,128)(2,1)} custom-call(bf16[16,280,128]{2,1,0:T(8,128)(2,1)} %all-to-all-done.2.refs_0_, bf16[768,960]{1,0:T(8,128)(2,1)} %copy-done, bf16[768,960]{1,0:T(8,128)(2,1)} %copy-done.2, f32[320,128]{1,0:T(8,128)S(1)} %broadcast_in_dim.12.refs_3_, bf16[14,3,16,960]{3,2,1,0:T(8,128)(2,1)} %maximum_bitcast_fusion.2.refs_4_, ...), custom_call_target="tpu_custom_call" | custom-call | flops 269999996928 | bytes 1048576 | tf_op jit(solution)/shard_map/grid_stage/pallas_call | solution.py:616
  97.7 15.7 %all-to-all-done.1.refs_2_ = bf16[16,320,128]{2,1,0:T(8,128)(2,1)} async-done(((bf16[16,320,128]{2,1,0:T(8,128)(2,1)}), bf16[16,320,128]{2,1,0:T(8,128)(2,1)}, u32[]{:S(2)}, u32[]{:S(2)}) %all-to-all-start.1) | async-done | bytes 1310752 | tf_op jit(solution)/shard_map/all_to_all | solution.py:739
  123.0 22.4 %all-to-all-done.3.refs_5_ = bf16[16,280,128]{2,1,0:T(8,128)(2,1)} async-done(((bf16[16,280,128]{2,1,0:T(8,128)(2,1)}), bf16[16,280,128]{2,1,0:T(8,128)(2,1)}, u32[]{:S(2)}, u32[]{:S(2)}) %all-to-all-start.3) | async-done | bytes 1146912 | tf_op jit(solution)/shard_map/all_to_all | solution.py:739
  145.5 8.9 %forward_inverse.1 = (f32[10,336,128]{2,1,0:T(8,128)}, bf16[16,320,128]{2,1,0:T(8,128)(2,1)}) custom-call(s32[320]{0:T(512)} %refs_0_.13, bf16[256,256]{1,0:T(8,128)(2,1)} %get-tuple-element.57.refs_1_, bf16[256,256]{1,0:T(8,128)(2,1)} %get-tuple-element.58.refs_2_, f32[1,128]{1,0:T(1,128)} %broadcast_in_dim_tile.3.refs_3_, f32[10,336,128]{2,1,0:T(8,128)} %copy-done.15, ...), custom_call_target="tpu_custom_call" | custom-call | flops 359999995904 | bytes 1048576 | tf_op jit(solution)/shard_map/forward_inverse/pallas_call | solution.py:708
  154.5 4.7 %all-to-all-start.4 = ((bf16[16,320,128]{2,1,0:T(8,128)(2,1)}), bf16[16,320,128]{2,1,0:T(8,128)(2,1)}, u32[]{:S(2)}, u32[]{:S(2)}) async-start(bf16[16,320,128]{2,1,0:T(8,128)(2,1)} %get-tuple-element.25), calls=%async_computation.4 | async-start | bytes 2621440 | tf_op jit(solution)/shard_map/all_to_all | solution.py:739
  163.1 26.8 %all-to-all-done.4.refs_0_ = bf16[16,320,128]{2,1,0:T(8,128)(2,1)} async-done(((bf16[16,320,128]{2,1,0:T(8,128)(2,1)}), bf16[16,320,128]{2,1,0:T(8,128)(2,1)}, u32[]{:S(2)}, u32[]{:S(2)}) %all-to-all-start.4) | async-done | bytes 1310752 | tf_op jit(solution)/shard_map/all_to_all | solution.py:739
  189.8 4.9 %all-to-all-start.6 = ((bf16[16,280,128]{2,1,0:T(8,128)(2,1)}), bf16[16,280,128]{2,1,0:T(8,128)(2,1)}, u32[]{:S(2)}, u32[]{:S(2)}) async-start(bf16[16,280,128]{2,1,0:T(8,128)(2,1)} %copy-done.6), calls=%async_computation.6 | async-start | bytes 2293760 | tf_op jit(solution)/shard_map/all_to_all | solution.py:739
  194.7 10.7 %grid_stage.6 = bf16[16,320,128]{2,1,0:T(8,128)(2,1)S(1)} custom-call(bf16[16,320,128]{2,1,0:T(8,128)(2,1)} %all-to-all-done.4.refs_0_, bf16[768,960]{1,0:T(8,128)(2,1)S(1)} %copy-done.1, bf16[768,960]{1,0:T(8,128)(2,1)S(1)} %copy-done.3, f32[320,128]{1,0:T(8,128)S(1)} %broadcast_in_dim.12.refs_3_, bf16[16,3,16,960]{3,2,1,0:T(8,128)(2,1)} %maximum_bitcast_fusion.1.refs_4_, ...), custom_call_target="tpu_custom_call" | custom-call | flops 269999996928 | bytes 1048576 | tf_op jit(solution)/shard_map/grid_stage/pallas_call | solution.py:616
  206.5 15.4 %all-to-all-done.6.refs_0_ = bf16[16,280,128]{2,1,0:T(8,128)(2,1)} async-done(((bf16[16,280,128]{2,1,0:T(8,128)(2,1)}), bf16[16,280,128]{2,1,0:T(8,128)(2,1)}, u32[]{:S(2)}, u32[]{:S(2)}) %all-to-all-start.6) | async-done | bytes 1146912 | tf_op jit(solution)/shard_map/all_to_all | solution.py:739
  221.9 4.9 %all-to-all-start.5 = ((bf16[16,320,128]{2,1,0:T(8,128)(2,1)}), bf16[16,320,128]{2,1,0:T(8,128)(2,1)}, u32[]{:S(2)}, u32[]{:S(2)}) async-start(bf16[16,320,128]{2,1,0:T(8,128)(2,1)} %copy-done.4), calls=%async_computation.5 | async-start | bytes 2621440 | tf_op jit(solution)/shard_map/all_to_all | solution.py:739
  226.7 11.1 %grid_stage.7 = bf16[16,280,128]{2,1,0:T(8,128)(2,1)} custom-call(bf16[16,280,128]{2,1,0:T(8,128)(2,1)} %all-to-all-done.6.refs_0_, bf16[768,960]{1,0:T(8,128)(2,1)} %copy-done, bf16[768,960]{1,0:T(8,128)(2,1)} %copy-done.2, f32[320,128]{1,0:T(8,128)S(1)} %broadcast_in_dim.12.refs_3_, bf16[14,3,16,960]{3,2,1,0:T(8,128)(2,1)} %maximum_bitcast_fusion.3.refs_4_, ...), custom_call_target="tpu_custom_call" | custom-call | flops 269999996928 | bytes 1048576 | tf_op jit(solution)/shard_map/grid_stage/pallas_call | solution.py:616
  237.9 19.5 %all-to-all-done.5.refs_2_ = bf16[16,320,128]{2,1,0:T(8,128)(2,1)} async-done(((bf16[16,320,128]{2,1,0:T(8,128)(2,1)}), bf16[16,320,128]{2,1,0:T(8,128)(2,1)}, u32[]{:S(2)}, u32[]{:S(2)}) %all-to-all-start.5) | async-done | bytes 1310752 | tf_op jit(solution)/shard_map/all_to_all | solution.py:739
  257.4 4.9 %all-to-all-start.7 = ((bf16[16,280,128]{2,1,0:T(8,128)(2,1)}), bf16[16,280,128]{2,1,0:T(8,128)(2,1)}, u32[]{:S(2)}, u32[]{:S(2)}) async-start(bf16[16,280,128]{2,1,0:T(8,128)(2,1)} %grid_stage.7), calls=%async_computation.7 | async-start | bytes 2293760 | tf_op jit(solution)/shard_map/all_to_all | solution.py:739
  267.0 22.4 %all-to-all-done.7.refs_5_ = bf16[16,280,128]{2,1,0:T(8,128)(2,1)} async-done(((bf16[16,280,128]{2,1,0:T(8,128)(2,1)}), bf16[16,280,128]{2,1,0:T(8,128)(2,1)}, u32[]{:S(2)}, u32[]{:S(2)}) %all-to-all-start.7) | async-done | bytes 1146912 | tf_op jit(solution)/shard_map/all_to_all | solution.py:739
  289.4 8.5 %forward_last.1 = f32[20,320,128]{2,1,0:T(8,128)} custom-call(s32[320]{0:T(512)} %refs_0_.13, bf16[256,256]{1,0:T(8,128)(2,1)} %get-tuple-element.57.refs_1_, bf16[256,256]{1,0:T(8,128)(2,1)} %get-tuple-element.58.refs_2_, f32[1,128]{1,0:T(1,128)} %broadcast_in_dim_tile.3.refs_3_, f32[10,336,128]{2,1,0:T(8,128)} %copy-done.16, ...), custom_call_target="tpu_custom_call" | custom-call | flops 299999985664 | bytes 1048576 | tf_op jit(solution)/shard_map/forward_last/pallas_call | solution.py:708
  (84 shorter events, 40.2 us)
Async XLA Ops:
  8.2 37.5 %all-to-all-start = ((bf16[16,320,128]{2,1,0:T(8,128)(2,1)}), bf16[16,320,128]{2,1,0:T(8,128)(2,1)}, u32[]{:S(2)}, u32[]{:S(2)}) async-start(bf16[16,320,128]{2,1,0:T(8,128)(2,1)} %get-tuple-element.17), calls=%async_computation | async-start | bytes 2621440 | tf_op jit(solution)/shard_map/all_to_all | solution.py:739
  21.2 37.2 %collective-permute-start = (bf16[16,3,16,960]{3,2,1,0:T(8,128)(2,1)}, bf16[16,3,16,960]{3,2,1,0:T(8,128)(2,1)}, u32[]{:S(2)}, u32[]{:S(2)}) collective-permute-start(bf16[16,3,16,960]{3,2,1,0:T(8,128)(2,1)} %maximum_bitcast_fusion.refs_4_), channel_id=1, source_target_pairs={{0,16},{16,0},{1,17},{17,1},{2,18},{18,2},{3,19},{19,3},{4,20},{20... | collective-permute-start | bytes 4423688 | tf_op jit(solution)/shard_map/ppermute | solution.py:723
  22.8 63.8 %collective-permute-start.1 = (bf16[14,3,16,960]{3,2,1,0:T(8,128)(2,1)}, bf16[14,3,16,960]{3,2,1,0:T(8,128)(2,1)}, u32[]{:S(2)}, u32[]{:S(2)}) collective-permute-start(bf16[14,3,16,960]{3,2,1,0:T(8,128)(2,1)} %maximum_bitcast_fusion.2.refs_4_), channel_id=1, source_target_pairs={{0,16},{16,0},{1,17},{17,1},{2,18},{18,2},{3,19},{19,3},{4,20},{20... | collective-permute-start | bytes 3870728 | tf_op jit(solution)/shard_map/ppermute | solution.py:723
  25.5 169.3 %collective-permute-start.2 = (bf16[16,3,16,960]{3,2,1,0:T(8,128)(2,1)}, bf16[16,3,16,960]{3,2,1,0:T(8,128)(2,1)}, u32[]{:S(2)}, u32[]{:S(2)}) collective-permute-start(bf16[16,3,16,960]{3,2,1,0:T(8,128)(2,1)} %maximum_bitcast_fusion.1.refs_4_), channel_id=1, source_target_pairs={{0,16},{16,0},{1,17},{17,1},{2,18},{18,2},{3,19},{19,3},{4,20},{20... | collective-permute-start | bytes 4423688 | tf_op jit(solution)/shard_map/ppermute | solution.py:723
  27.0 199.7 %collective-permute-start.3 = (bf16[14,3,16,960]{3,2,1,0:T(8,128)(2,1)}, bf16[14,3,16,960]{3,2,1,0:T(8,128)(2,1)}, u32[]{:S(2)}, u32[]{:S(2)}) collective-permute-start(bf16[14,3,16,960]{3,2,1,0:T(8,128)(2,1)} %maximum_bitcast_fusion.3.refs_4_), channel_id=1, source_target_pairs={{0,16},{16,0},{1,17},{17,1},{2,18},{18,2},{3,19},{19,3},{4,20},{20... | collective-permute-start | bytes 3870728 | tf_op jit(solution)/shard_map/ppermute | solution.py:723
  28.2 7.2 %copy-start.21 = (f32[32,32]{1,0:T(8,128)S(1)}, f32[32,32]{1,0:T(8,128)}, u32[]{:S(2)}) copy-start(f32[32,32]{1,0:T(8,128)} %param.12) | copy-start | bytes 12292
  28.2 7.3 %copy-start.20 = (f32[4,32,4,32]{3,2,1,0:T(4,128)S(1)}, f32[4,32,4,32]{3,2,1,0:T(4,128)}, u32[]{:S(2)}) copy-start(f32[4,32,4,32]{3,2,1,0:T(4,128)} %constant.45) | copy-start | bytes 196612
  28.2 7.7 %copy-start.22 = (f32[32]{0:T(128)S(1)}, f32[32]{0:T(128)}, u32[]{:S(2)}) copy-start(f32[32]{0:T(128)} %param.13) | copy-start | bytes 388
  35.7 14.5 %copy-start.7 = (s32[320]{0:T(512)S(1)}, s32[320]{0:T(512)}, u32[]{:S(2)}) copy-start(s32[320]{0:T(512)} %refs_0_.13) | copy-start | bytes 3844
  45.7 32.0 %all-to-all-start.2 = ((bf16[16,280,128]{2,1,0:T(8,128)(2,1)}), bf16[16,280,128]{2,1,0:T(8,128)(2,1)}, u32[]{:S(2)}, u32[]{:S(2)}) async-start(bf16[16,280,128]{2,1,0:T(8,128)(2,1)} %get-tuple-element.21), calls=%async_computation.2 | async-start | bytes 2293760 | tf_op jit(solution)/shard_map/all_to_all | solution.py:739
  58.3 11.8 %copy-start = (bf16[768,960]{1,0:T(8,128)(2,1)}, bf16[768,960]{1,0:T(8,128)(2,1)S(1)}, u32[]{:S(2)}) copy-start(bf16[768,960]{1,0:T(8,128)(2,1)S(1)} %get-tuple-element.53.refs_1_) | copy-start | bytes 4423684
  58.3 11.8 %copy-start.2 = (bf16[768,960]{1,0:T(8,128)(2,1)}, bf16[768,960]{1,0:T(8,128)(2,1)S(1)}, u32[]{:S(2)}) copy-start(bf16[768,960]{1,0:T(8,128)(2,1)S(1)} %get-tuple-element.54.refs_2_) | copy-start | bytes 4423684
  77.7 35.7 %all-to-all-start.1 = ((bf16[16,320,128]{2,1,0:T(8,128)(2,1)}), bf16[16,320,128]{2,1,0:T(8,128)(2,1)}, u32[]{:S(2)}, u32[]{:S(2)}) async-start(bf16[16,320,128]{2,1,0:T(8,128)(2,1)} %copy-done.5), calls=%async_computation.1 | async-start | bytes 2621440 | tf_op jit(solution)/shard_map/all_to_all | solution.py:739
  97.7 20.3 %copy-start.8 = (s32[320]{0:T(512)S(1)}, s32[320]{0:T(512)}, u32[]{:S(2)}) copy-start(s32[320]{0:T(512)} %refs_0_.13) | copy-start | bytes 3844
  97.7 20.3 %copy-start.17 = (bf16[10,2,168,128]{3,2,1,0:T(8,128)(2,1)S(1)}, bf16[10,2,168,128]{3,2,1,0:T(8,128)(2,1)}, u32[]{:S(2)}) copy-start(bf16[10,2,168,128]{3,2,1,0:T(8,128)(2,1)} %get-tuple-element.20.refs_3_) | copy-start | bytes 2580484
  113.5 32.0 %all-to-all-start.3 = ((bf16[16,280,128]{2,1,0:T(8,128)(2,1)}), bf16[16,280,128]{2,1,0:T(8,128)(2,1)}, u32[]{:S(2)}, u32[]{:S(2)}) async-start(bf16[16,280,128]{2,1,0:T(8,128)(2,1)} %grid_stage.5), calls=%async_computation.3 | async-start | bytes 2293760 | tf_op jit(solution)/shard_map/all_to_all | solution.py:739
  154.5 35.4 %all-to-all-start.4 = ((bf16[16,320,128]{2,1,0:T(8,128)(2,1)}), bf16[16,320,128]{2,1,0:T(8,128)(2,1)}, u32[]{:S(2)}, u32[]{:S(2)}) async-start(bf16[16,320,128]{2,1,0:T(8,128)(2,1)} %get-tuple-element.25), calls=%async_computation.4 | async-start | bytes 2621440 | tf_op jit(solution)/shard_map/all_to_all | solution.py:739
  160.6 34.1 %copy-start.3 = (bf16[768,960]{1,0:T(8,128)(2,1)S(1)}, bf16[768,960]{1,0:T(8,128)(2,1)}, u32[]{:S(2)}) copy-start(bf16[768,960]{1,0:T(8,128)(2,1)} %copy-done.2) | copy-start | bytes 4423684
  163.1 31.7 %copy-start.1 = (bf16[768,960]{1,0:T(8,128)(2,1)S(1)}, bf16[768,960]{1,0:T(8,128)(2,1)}, u32[]{:S(2)}) copy-start(bf16[768,960]{1,0:T(8,128)(2,1)} %copy-done) | copy-start | bytes 4423684
  189.8 32.0 %all-to-all-start.6 = ((bf16[16,280,128]{2,1,0:T(8,128)(2,1)}), bf16[16,280,128]{2,1,0:T(8,128)(2,1)}, u32[]{:S(2)}, u32[]{:S(2)}) async-start(bf16[16,280,128]{2,1,0:T(8,128)(2,1)} %copy-done.6), calls=%async_computation.6 | async-start | bytes 2293760 | tf_op jit(solution)/shard_map/all_to_all | solution.py:739
  221.9 35.5 %all-to-all-start.5 = ((bf16[16,320,128]{2,1,0:T(8,128)(2,1)}), bf16[16,320,128]{2,1,0:T(8,128)(2,1)}, u32[]{:S(2)}, u32[]{:S(2)}) async-start(bf16[16,320,128]{2,1,0:T(8,128)(2,1)} %copy-done.4), calls=%async_computation.5 | async-start | bytes 2621440 | tf_op jit(solution)/shard_map/all_to_all | solution.py:739
  237.8 24.4 %copy-start.10 = (s32[320]{0:T(512)S(1)}, s32[320]{0:T(512)}, u32[]{:S(2)}) copy-start(s32[320]{0:T(512)} %refs_0_.13) | copy-start | bytes 3844
  237.8 24.4 %copy-start.12 = (f32[10,336,128]{2,1,0:T(8,128)S(1)}, f32[10,336,128]{2,1,0:T(8,128)}, u32[]{:S(2)}) copy-start(f32[10,336,128]{2,1,0:T(8,128)} %get-tuple-element.24.refs_1_) | copy-start | bytes 5160964
  257.4 32.0 %all-to-all-start.7 = ((bf16[16,280,128]{2,1,0:T(8,128)(2,1)}), bf16[16,280,128]{2,1,0:T(8,128)(2,1)}, u32[]{:S(2)}, u32[]{:S(2)}) async-start(bf16[16,280,128]{2,1,0:T(8,128)(2,1)} %grid_stage.7), calls=%async_computation.7 | async-start | bytes 2293760 | tf_op jit(solution)/shard_map/all_to_all | solution.py:739
  (11 other events, 20.7 us)

commit v7 on v6

--- a/solution.py
+++ b/solution.py
@@ -61,7 +61,7 @@
         self.group = 8
         self.step = max(d for d in range(1, UNROLL + 1) if self.pairs % d == 0)
         self.loops = self.pairs // self.step
-        self.bundle = space // 4 if space % 4 == 0 else space
+        self.bundle = space // 8 if space % 8 == 0 else space
         self.bundles = space // self.bundle
 
     def direct(self, part):
@@ -279,7 +279,11 @@
             stage[d, : sz.block(part), :] = recv[d].astype(jnp.float32)
         return 0
 
-    lax.fori_loop(0, sz.bundles, body, 0)
+    if source is None:
+        lax.fori_loop(0, sz.bundles, body, 0)
+    else:
+        for g in range(sz.bundles):
+            body(g, 0)
 
 
 def change_rows(sz, part, i, facts, table, stage):

time: 299 us -> 299 us (level)
  no operation moved by 1% of the time
where the time goes in v7:
time: 299 us; the launch traced here: 298 us
  waiting for transfers between devices  141 us (47%)
  Pallas kernels  83.8 us (28%)
  starting transfers between devices  42.5 us (14%)
  local copies, waits for them, and re-layouts  16 us (5%)
  other arithmetic  14 us (5%)
    all_to_all x8, waiting for transfers between devices, transpose(): return lax.all_to_all(value, 'space', 0, 0, tiled=True)  137 us
    pallas_call x4, Pallas kernels, grid_stage(): pl.pallas_call(lambda *refs: grid_kernel(sz, part, members, *refs), out_s...  44.5 us
    all_to_all x8, starting transfers between devices, transpose(): return lax.all_to_all(value, 'space', 0, 0, tiled=True)  39.6 us
    pallas_call x7, Pallas kernels, call(): pl.pallas_call(lambda *refs: body(sz, *refs), out_shape=tuple(outs), in_s...  39.2 us
    unnamed x48, local copies, waits for them, and re-layouts  11.3 us
    another operation x1, other arithmetic  7.51 us
  transfers between devices with their start and end apart: 12, of which 9 were waited for; matrix products, arithmetic and copies ran while one was open for 6% of the time, Pallas kernels for 22%

profile of v7, /device:TPU:15, one launch (start us, length us, event | category | flops | bytes accessed | tf_op | source)
XLA Modules:
  0.0 298.2 jit_solution(14717582771358641811)
XLA Ops:
  0.0 8.2 %tables_inverse.1 = (bf16[10,2,168,128]{3,2,1,0:T(8,128)(2,1)}, bf16[10,2,128,256]{3,2,1,0:T(8,128)(2,1)}, f32[10,336,128]{2,1,0:T(8,128)}, bf16[16,320,128]{2,1,0:T(8,128)(2,1)}) custom-call(s32[320]{0:T(512)} %refs_0_.13, f32[16,128]{1,0:T(8,128)} %constant.34.clone.refs_1_.refs_2_, f32[20,320,128]{2,1,0:T(8,128)} %refs_2_.2), custom_call_target="tpu_custom_call" | custom-call | flops 359999995904 | bytes 1048576 | tf_op jit(solution)/shard_map/tables_inverse/pallas_call | solution.py:712
  8.2 6.6 %all-to-all-start = ((bf16[16,320,128]{2,1,0:T(8,128)(2,1)}), bf16[16,320,128]{2,1,0:T(8,128)(2,1)}, u32[]{:S(2)}, u32[]{:S(2)}) async-start(bf16[16,320,128]{2,1,0:T(8,128)(2,1)} %get-tuple-element.17), calls=%async_computation | async-start | bytes 2621440 | tf_op jit(solution)/shard_map/all_to_all | solution.py:743
  28.3 7.2 %tables_inverse_rest.1 = (bf16[10,2,168,128]{3,2,1,0:T(8,128)(2,1)}, bf16[10,2,128,256]{3,2,1,0:T(8,128)(2,1)}, bf16[16,280,128]{2,1,0:T(8,128)(2,1)}) custom-call(s32[320]{0:T(512)} %refs_0_.13, f32[16,128]{1,0:T(8,128)} %constant.34.clone.refs_1_.refs_2_, f32[16,128]{1,0:T(8,128)} %constant.34.clone.refs_1_.refs_2_, ...), custom_call_target="tpu_custom_call" | custom-call | flops 240000008192 | bytes 1048576 | tf_op jit(solution)/shard_map/tables_inverse_rest/pallas_call | solution.py:712
  37.3 8.4 %all-to-all-done.refs_0_ = bf16[16,320,128]{2,1,0:T(8,128)(2,1)} async-done(((bf16[16,320,128]{2,1,0:T(8,128)(2,1)}), bf16[16,320,128]{2,1,0:T(8,128)(2,1)}, u32[]{:S(2)}, u32[]{:S(2)}) %all-to-all-start) | async-done | bytes 1310752 | tf_op jit(solution)/shard_map/all_to_all | solution.py:743
  45.8 4.6 %all-to-all-start.2 = ((bf16[16,280,128]{2,1,0:T(8,128)(2,1)}), bf16[16,280,128]{2,1,0:T(8,128)(2,1)}, u32[]{:S(2)}, u32[]{:S(2)}) async-start(bf16[16,280,128]{2,1,0:T(8,128)(2,1)} %get-tuple-element.21), calls=%async_computation.2 | async-start | bytes 2293760 | tf_op jit(solution)/shard_map/all_to_all | solution.py:743
  50.4 7.5 %multiply_convert_fusion.1 = (bf16[384,960]{1,0:T(8,128)(2,1)S(1)}, bf16[384,960]{1,0:T(8,128)(2,1)S(1)}, bf16[384,960]{1,0:T(8,128)(2,1)S(1)}, bf16[384,960]{1,0:T(8,128)(2,1)S(1)}) fusion(f32[384]{0:T(512)S(1)} %get-tuple-element.51, s32[384]{0:T(512)S(1)} %get-tuple-element.52, f32[384]{0:T(512)S(1)} %get-tuple-element.50), kind=kLoop, calls=%fused_computation.10 | loop fusion | flops 6635520 | bytes 2953728 | tf_op jit(solution)/shard_map/convert
  58.5 11.7 %grid_stage.4 = bf16[16,320,128]{2,1,0:T(8,128)(2,1)S(1)} custom-call(bf16[16,320,128]{2,1,0:T(8,128)(2,1)} %all-to-all-done.refs_0_, bf16[768,960]{1,0:T(8,128)(2,1)S(1)} %get-tuple-element.53.refs_1_, bf16[768,960]{1,0:T(8,128)(2,1)S(1)} %get-tuple-element.54.refs_2_, f32[320,128]{1,0:T(8,128)S(1)} %broadcast_in_dim.12.refs_3_, ...), custom_call_target="tpu_custom_call" | custom-call | flops 269999996928 | bytes 1048576 | tf_op jit(solution)/shard_map/grid_stage/pallas_call | solution.py:620
  71.3 6.5 %all-to-all-done.2.refs_0_ = bf16[16,280,128]{2,1,0:T(8,128)(2,1)} async-done(((bf16[16,280,128]{2,1,0:T(8,128)(2,1)}), bf16[16,280,128]{2,1,0:T(8,128)(2,1)}, u32[]{:S(2)}, u32[]{:S(2)}) %all-to-all-start.2) | async-done | bytes 1146912 | tf_op jit(solution)/shard_map/all_to_all | solution.py:743
  77.8 4.6 %all-to-all-start.1 = ((bf16[16,320,128]{2,1,0:T(8,128)(2,1)}), bf16[16,320,128]{2,1,0:T(8,128)(2,1)}, u32[]{:S(2)}, u32[]{:S(2)}) async-start(bf16[16,320,128]{2,1,0:T(8,128)(2,1)} %copy-done.5), calls=%async_computation.1 | async-start | bytes 2621440 | tf_op jit(solution)/shard_map/all_to_all | solution.py:743
  86.6 11.1 %grid_stage.5 = bf16[16,280,128]{2,1,0:T(8,128)(2,1)} custom-call(bf16[16,280,128]{2,1,0:T(8,128)(2,1)} %all-to-all-done.2.refs_0_, bf16[768,960]{1,0:T(8,128)(2,1)} %copy-done, bf16[768,960]{1,0:T(8,128)(2,1)} %copy-done.2, f32[320,128]{1,0:T(8,128)S(1)} %broadcast_in_dim.12.refs_3_, bf16[14,3,16,960]{3,2,1,0:T(8,128)(2,1)} %maximum_bitcast_fusion.2.refs_4_, ...), custom_call_target="tpu_custom_call" | custom-call | flops 269999996928 | bytes 1048576 | tf_op jit(solution)/shard_map/grid_stage/pallas_call | solution.py:620
  97.8 15.5 %all-to-all-done.1.refs_2_ = bf16[16,320,128]{2,1,0:T(8,128)(2,1)} async-done(((bf16[16,320,128]{2,1,0:T(8,128)(2,1)}), bf16[16,320,128]{2,1,0:T(8,128)(2,1)}, u32[]{:S(2)}, u32[]{:S(2)}) %all-to-all-start.1) | async-done | bytes 1310752 | tf_op jit(solution)/shard_map/all_to_all | solution.py:743
  122.9 22.4 %all-to-all-done.3.refs_5_ = bf16[16,280,128]{2,1,0:T(8,128)(2,1)} async-done(((bf16[16,280,128]{2,1,0:T(8,128)(2,1)}), bf16[16,280,128]{2,1,0:T(8,128)(2,1)}, u32[]{:S(2)}, u32[]{:S(2)}) %all-to-all-start.3) | async-done | bytes 1146912 | tf_op jit(solution)/shard_map/all_to_all | solution.py:743
  145.3 9.1 %forward_inverse.1 = (f32[10,336,128]{2,1,0:T(8,128)}, bf16[16,320,128]{2,1,0:T(8,128)(2,1)}) custom-call(s32[320]{0:T(512)} %refs_0_.13, bf16[256,256]{1,0:T(8,128)(2,1)} %get-tuple-element.57.refs_1_, bf16[256,256]{1,0:T(8,128)(2,1)} %get-tuple-element.58.refs_2_, f32[1,128]{1,0:T(1,128)} %broadcast_in_dim_tile.3.refs_3_, f32[10,336,128]{2,1,0:T(8,128)} %copy-done.15, ...), custom_call_target="tpu_custom_call" | custom-call | flops 359999995904 | bytes 1048576 | tf_op jit(solution)/shard_map/forward_inverse/pallas_call | solution.py:712
  154.5 4.7 %all-to-all-start.4 = ((bf16[16,320,128]{2,1,0:T(8,128)(2,1)}), bf16[16,320,128]{2,1,0:T(8,128)(2,1)}, u32[]{:S(2)}, u32[]{:S(2)}) async-start(bf16[16,320,128]{2,1,0:T(8,128)(2,1)} %get-tuple-element.25), calls=%async_computation.4 | async-start | bytes 2621440 | tf_op jit(solution)/shard_map/all_to_all | solution.py:743
  163.1 26.8 %all-to-all-done.4.refs_0_ = bf16[16,320,128]{2,1,0:T(8,128)(2,1)} async-done(((bf16[16,320,128]{2,1,0:T(8,128)(2,1)}), bf16[16,320,128]{2,1,0:T(8,128)(2,1)}, u32[]{:S(2)}, u32[]{:S(2)}) %all-to-all-start.4) | async-done | bytes 1310752 | tf_op jit(solution)/shard_map/all_to_all | solution.py:743
  189.9 4.9 %all-to-all-start.6 = ((bf16[16,280,128]{2,1,0:T(8,128)(2,1)}), bf16[16,280,128]{2,1,0:T(8,128)(2,1)}, u32[]{:S(2)}, u32[]{:S(2)}) async-start(bf16[16,280,128]{2,1,0:T(8,128)(2,1)} %copy-done.6), calls=%async_computation.6 | async-start | bytes 2293760 | tf_op jit(solution)/shard_map/all_to_all | solution.py:743
  194.8 10.7 %grid_stage.6 = bf16[16,320,128]{2,1,0:T(8,128)(2,1)S(1)} custom-call(bf16[16,320,128]{2,1,0:T(8,128)(2,1)} %all-to-all-done.4.refs_0_, bf16[768,960]{1,0:T(8,128)(2,1)S(1)} %copy-done.1, bf16[768,960]{1,0:T(8,128)(2,1)S(1)} %copy-done.3, f32[320,128]{1,0:T(8,128)S(1)} %broadcast_in_dim.12.refs_3_, bf16[16,3,16,960]{3,2,1,0:T(8,128)(2,1)} %maximum_bitcast_fusion.1.refs_4_, ...), custom_call_target="tpu_custom_call" | custom-call | flops 269999996928 | bytes 1048576 | tf_op jit(solution)/shard_map/grid_stage/pallas_call | solution.py:620
  206.5 15.4 %all-to-all-done.6.refs_0_ = bf16[16,280,128]{2,1,0:T(8,128)(2,1)} async-done(((bf16[16,280,128]{2,1,0:T(8,128)(2,1)}), bf16[16,280,128]{2,1,0:T(8,128)(2,1)}, u32[]{:S(2)}, u32[]{:S(2)}) %all-to-all-start.6) | async-done | bytes 1146912 | tf_op jit(solution)/shard_map/all_to_all | solution.py:743
  221.9 4.9 %all-to-all-start.5 = ((bf16[16,320,128]{2,1,0:T(8,128)(2,1)}), bf16[16,320,128]{2,1,0:T(8,128)(2,1)}, u32[]{:S(2)}, u32[]{:S(2)}) async-start(bf16[16,320,128]{2,1,0:T(8,128)(2,1)} %copy-done.4), calls=%async_computation.5 | async-start | bytes 2621440 | tf_op jit(solution)/shard_map/all_to_all | solution.py:743
  226.8 11.1 %grid_stage.7 = bf16[16,280,128]{2,1,0:T(8,128)(2,1)} custom-call(bf16[16,280,128]{2,1,0:T(8,128)(2,1)} %all-to-all-done.6.refs_0_, bf16[768,960]{1,0:T(8,128)(2,1)} %copy-done, bf16[768,960]{1,0:T(8,128)(2,1)} %copy-done.2, f32[320,128]{1,0:T(8,128)S(1)} %broadcast_in_dim.12.refs_3_, bf16[14,3,16,960]{3,2,1,0:T(8,128)(2,1)} %maximum_bitcast_fusion.3.refs_4_, ...), custom_call_target="tpu_custom_call" | custom-call | flops 269999996928 | bytes 1048576 | tf_op jit(solution)/shard_map/grid_stage/pallas_call | solution.py:620
  237.9 19.6 %all-to-all-done.5.refs_2_ = bf16[16,320,128]{2,1,0:T(8,128)(2,1)} async-done(((bf16[16,320,128]{2,1,0:T(8,128)(2,1)}), bf16[16,320,128]{2,1,0:T(8,128)(2,1)}, u32[]{:S(2)}, u32[]{:S(2)}) %all-to-all-start.5) | async-done | bytes 1310752 | tf_op jit(solution)/shard_map/all_to_all | solution.py:743
  257.4 4.9 %all-to-all-start.7 = ((bf16[16,280,128]{2,1,0:T(8,128)(2,1)}), bf16[16,280,128]{2,1,0:T(8,128)(2,1)}, u32[]{:S(2)}, u32[]{:S(2)}) async-start(bf16[16,280,128]{2,1,0:T(8,128)(2,1)} %grid_stage.7), calls=%async_computation.7 | async-start | bytes 2293760 | tf_op jit(solution)/shard_map/all_to_all | solution.py:743
  267.0 22.4 %all-to-all-done.7.refs_5_ = bf16[16,280,128]{2,1,0:T(8,128)(2,1)} async-done(((bf16[16,280,128]{2,1,0:T(8,128)(2,1)}), bf16[16,280,128]{2,1,0:T(8,128)(2,1)}, u32[]{:S(2)}, u32[]{:S(2)}) %all-to-all-start.7) | async-done | bytes 1146912 | tf_op jit(solution)/shard_map/all_to_all | solution.py:743
  289.5 8.6 %forward_last.1 = f32[20,320,128]{2,1,0:T(8,128)} custom-call(s32[320]{0:T(512)} %refs_0_.13, bf16[256,256]{1,0:T(8,128)(2,1)} %get-tuple-element.57.refs_1_, bf16[256,256]{1,0:T(8,128)(2,1)} %get-tuple-element.58.refs_2_, f32[1,128]{1,0:T(1,128)} %broadcast_in_dim_tile.3.refs_3_, f32[10,336,128]{2,1,0:T(8,128)} %copy-done.16, ...), custom_call_target="tpu_custom_call" | custom-call | flops 299999985664 | bytes 1048576 | tf_op jit(solution)/shard_map/forward_last/pallas_call | solution.py:712
  (84 shorter events, 40.4 us)
Async XLA Ops:
  8.2 37.5 %all-to-all-start = ((bf16[16,320,128]{2,1,0:T(8,128)(2,1)}), bf16[16,320,128]{2,1,0:T(8,128)(2,1)}, u32[]{:S(2)}, u32[]{:S(2)}) async-start(bf16[16,320,128]{2,1,0:T(8,128)(2,1)} %get-tuple-element.17), calls=%async_computation | async-start | bytes 2621440 | tf_op jit(solution)/shard_map/all_to_all | solution.py:743
  21.2 37.2 %collective-permute-start = (bf16[16,3,16,960]{3,2,1,0:T(8,128)(2,1)}, bf16[16,3,16,960]{3,2,1,0:T(8,128)(2,1)}, u32[]{:S(2)}, u32[]{:S(2)}) collective-permute-start(bf16[16,3,16,960]{3,2,1,0:T(8,128)(2,1)} %maximum_bitcast_fusion.refs_4_), channel_id=1, source_target_pairs={{0,16},{16,0},{1,17},{17,1},{2,18},{18,2},{3,19},{19,3},{4,20},{20... | collective-permute-start | bytes 4423688 | tf_op jit(solution)/shard_map/ppermute | solution.py:727
  22.8 63.8 %collective-permute-start.1 = (bf16[14,3,16,960]{3,2,1,0:T(8,128)(2,1)}, bf16[14,3,16,960]{3,2,1,0:T(8,128)(2,1)}, u32[]{:S(2)}, u32[]{:S(2)}) collective-permute-start(bf16[14,3,16,960]{3,2,1,0:T(8,128)(2,1)} %maximum_bitcast_fusion.2.refs_4_), channel_id=1, source_target_pairs={{0,16},{16,0},{1,17},{17,1},{2,18},{18,2},{3,19},{19,3},{4,20},{20... | collective-permute-start | bytes 3870728 | tf_op jit(solution)/shard_map/ppermute | solution.py:727
  25.5 169.2 %collective-permute-start.2 = (bf16[16,3,16,960]{3,2,1,0:T(8,128)(2,1)}, bf16[16,3,16,960]{3,2,1,0:T(8,128)(2,1)}, u32[]{:S(2)}, u32[]{:S(2)}) collective-permute-start(bf16[16,3,16,960]{3,2,1,0:T(8,128)(2,1)} %maximum_bitcast_fusion.1.refs_4_), channel_id=1, source_target_pairs={{0,16},{16,0},{1,17},{17,1},{2,18},{18,2},{3,19},{19,3},{4,20},{20... | collective-permute-start | bytes 4423688 | tf_op jit(solution)/shard_map/ppermute | solution.py:727
  27.0 199.7 %collective-permute-start.3 = (bf16[14,3,16,960]{3,2,1,0:T(8,128)(2,1)}, bf16[14,3,16,960]{3,2,1,0:T(8,128)(2,1)}, u32[]{:S(2)}, u32[]{:S(2)}) collective-permute-start(bf16[14,3,16,960]{3,2,1,0:T(8,128)(2,1)} %maximum_bitcast_fusion.3.refs_4_), channel_id=1, source_target_pairs={{0,16},{16,0},{1,17},{17,1},{2,18},{18,2},{3,19},{19,3},{4,20},{20... | collective-permute-start | bytes 3870728 | tf_op jit(solution)/shard_map/ppermute | solution.py:727
  28.3 7.2 %copy-start.21 = (f32[32,32]{1,0:T(8,128)S(1)}, f32[32,32]{1,0:T(8,128)}, u32[]{:S(2)}) copy-start(f32[32,32]{1,0:T(8,128)} %param.12) | copy-start | bytes 12292
  28.3 7.3 %copy-start.20 = (f32[4,32,4,32]{3,2,1,0:T(4,128)S(1)}, f32[4,32,4,32]{3,2,1,0:T(4,128)}, u32[]{:S(2)}) copy-start(f32[4,32,4,32]{3,2,1,0:T(4,128)} %constant.45) | copy-start | bytes 196612
  28.3 7.7 %copy-start.22 = (f32[32]{0:T(128)S(1)}, f32[32]{0:T(128)}, u32[]{:S(2)}) copy-start(f32[32]{0:T(128)} %param.13) | copy-start | bytes 388
  35.8 14.5 %copy-start.7 = (s32[320]{0:T(512)S(1)}, s32[320]{0:T(512)}, u32[]{:S(2)}) copy-start(s32[320]{0:T(512)} %refs_0_.13) | copy-start | bytes 3844
  45.8 32.0 %all-to-all-start.2 = ((bf16[16,280,128]{2,1,0:T(8,128)(2,1)}), bf16[16,280,128]{2,1,0:T(8,128)(2,1)}, u32[]{:S(2)}, u32[]{:S(2)}) async-start(bf16[16,280,128]{2,1,0:T(8,128)(2,1)} %get-tuple-element.21), calls=%async_computation.2 | async-start | bytes 2293760 | tf_op jit(solution)/shard_map/all_to_all | solution.py:743
  58.3 11.8 %copy-start = (bf16[768,960]{1,0:T(8,128)(2,1)}, bf16[768,960]{1,0:T(8,128)(2,1)S(1)}, u32[]{:S(2)}) copy-start(bf16[768,960]{1,0:T(8,128)(2,1)S(1)} %get-tuple-element.53.refs_1_) | copy-start | bytes 4423684
  58.3 11.8 %copy-start.2 = (bf16[768,960]{1,0:T(8,128)(2,1)}, bf16[768,960]{1,0:T(8,128)(2,1)S(1)}, u32[]{:S(2)}) copy-start(bf16[768,960]{1,0:T(8,128)(2,1)S(1)} %get-tuple-element.54.refs_2_) | copy-start | bytes 4423684
  77.8 35.5 %all-to-all-start.1 = ((bf16[16,320,128]{2,1,0:T(8,128)(2,1)}), bf16[16,320,128]{2,1,0:T(8,128)(2,1)}, u32[]{:S(2)}, u32[]{:S(2)}) async-start(bf16[16,320,128]{2,1,0:T(8,128)(2,1)} %copy-done.5), calls=%async_computation.1 | async-start | bytes 2621440 | tf_op jit(solution)/shard_map/all_to_all | solution.py:743
  97.8 20.1 %copy-start.8 = (s32[320]{0:T(512)S(1)}, s32[320]{0:T(512)}, u32[]{:S(2)}) copy-start(s32[320]{0:T(512)} %refs_0_.13) | copy-start | bytes 3844
  97.8 20.1 %copy-start.17 = (bf16[10,2,168,128]{3,2,1,0:T(8,128)(2,1)S(1)}, bf16[10,2,168,128]{3,2,1,0:T(8,128)(2,1)}, u32[]{:S(2)}) copy-start(bf16[10,2,168,128]{3,2,1,0:T(8,128)(2,1)} %get-tuple-element.20.refs_3_) | copy-start | bytes 2580484
  113.3 32.0 %all-to-all-start.3 = ((bf16[16,280,128]{2,1,0:T(8,128)(2,1)}), bf16[16,280,128]{2,1,0:T(8,128)(2,1)}, u32[]{:S(2)}, u32[]{:S(2)}) async-start(bf16[16,280,128]{2,1,0:T(8,128)(2,1)} %grid_stage.5), calls=%async_computation.3 | async-start | bytes 2293760 | tf_op jit(solution)/shard_map/all_to_all | solution.py:743
  154.5 35.4 %all-to-all-start.4 = ((bf16[16,320,128]{2,1,0:T(8,128)(2,1)}), bf16[16,320,128]{2,1,0:T(8,128)(2,1)}, u32[]{:S(2)}, u32[]{:S(2)}) async-start(bf16[16,320,128]{2,1,0:T(8,128)(2,1)} %get-tuple-element.25), calls=%async_computation.4 | async-start | bytes 2621440 | tf_op jit(solution)/shard_map/all_to_all | solution.py:743
  160.7 34.1 %copy-start.3 = (bf16[768,960]{1,0:T(8,128)(2,1)S(1)}, bf16[768,960]{1,0:T(8,128)(2,1)}, u32[]{:S(2)}) copy-start(bf16[768,960]{1,0:T(8,128)(2,1)} %copy-done.2) | copy-start | bytes 4423684
  163.1 31.6 %copy-start.1 = (bf16[768,960]{1,0:T(8,128)(2,1)S(1)}, bf16[768,960]{1,0:T(8,128)(2,1)}, u32[]{:S(2)}) copy-start(bf16[768,960]{1,0:T(8,128)(2,1)} %copy-done) | copy-start | bytes 4423684
  189.9 32.0 %all-to-all-start.6 = ((bf16[16,280,128]{2,1,0:T(8,128)(2,1)}), bf16[16,280,128]{2,1,0:T(8,128)(2,1)}, u32[]{:S(2)}, u32[]{:S(2)}) async-start(bf16[16,280,128]{2,1,0:T(8,128)(2,1)} %copy-done.6), calls=%async_computation.6 | async-start | bytes 2293760 | tf_op jit(solution)/shard_map/all_to_all | solution.py:743
  221.9 35.5 %all-to-all-start.5 = ((bf16[16,320,128]{2,1,0:T(8,128)(2,1)}), bf16[16,320,128]{2,1,0:T(8,128)(2,1)}, u32[]{:S(2)}, u32[]{:S(2)}) async-start(bf16[16,320,128]{2,1,0:T(8,128)(2,1)} %copy-done.4), calls=%async_computation.5 | async-start | bytes 2621440 | tf_op jit(solution)/shard_map/all_to_all | solution.py:743
  237.8 24.4 %copy-start.10 = (s32[320]{0:T(512)S(1)}, s32[320]{0:T(512)}, u32[]{:S(2)}) copy-start(s32[320]{0:T(512)} %refs_0_.13) | copy-start | bytes 3844
  237.9 24.4 %copy-start.12 = (f32[10,336,128]{2,1,0:T(8,128)S(1)}, f32[10,336,128]{2,1,0:T(8,128)}, u32[]{:S(2)}) copy-start(f32[10,336,128]{2,1,0:T(8,128)} %get-tuple-element.24.refs_1_) | copy-start | bytes 5160964
  257.4 32.0 %all-to-all-start.7 = ((bf16[16,280,128]{2,1,0:T(8,128)(2,1)}), bf16[16,280,128]{2,1,0:T(8,128)(2,1)}, u32[]{:S(2)}, u32[]{:S(2)}) async-start(bf16[16,280,128]{2,1,0:T(8,128)(2,1)} %grid_stage.7), calls=%async_computation.7 | async-start | bytes 2293760 | tf_op jit(solution)/shard_map/all_to_all | solution.py:743
  (11 other events, 20.7 us)
